TPU v7x, 256 devices: a whole 4x4x8 slice. The times are simulated.
256 devices in a mesh: segment: 8 (over x, core), adapter: 32 (over y, z).
Axes of the slice: x: 4, y: 4, z: 8, core: 2. Of those that a mesh axis runs over, the one named last changes fastest.
Arguments:
- tokens: bfloat16 [2, 64, 8192], P(None, 'adapter'), may hold values from -6 to 6
- adapter_ids: int32 [2, 64, 1], P(None, 'adapter'), may hold values from 0 to 63
- ranks: int32 [64], P('adapter'), may hold values from 16 to 64, as said below
- gain: float32 [8, 8192], P('segment'), may hold values from 0.1 to 1.9
- base_weight: bfloat16 [8, 8192, 8192], P('segment', None, 'adapter'), may hold values from -0.0625 to 0.0625
- shrink_weight: bfloat16 [8, 64, 8192, 64], P('segment', 'adapter'), may hold values from -0.0625 to 0.0625
- expand_weight: bfloat16 [8, 64, 64, 8192], P('segment', None, None, 'adapter'), may hold values from -0.75 to 0.75
Outputs:
- layer_states: bfloat16 [8, 2, 64, 8192], P('segment', None, None, 'adapter')
Inputs may be any that keep to these rules, and one draw needn't show every extreme that they name: `adapter_ids`: adapter a of a request is held on adapter index a // 2. `ranks`: each rank is a multiple of 16.
All inputs are finite; a program needn't handle non-finite values.
Results may differ from a plain program's by a relative error of at most 0.02.
Values may be sent and summed in bfloat16 or wider, within the bound.
No kernel may reach another device: no remote copies, remote signals or barrier semaphores. Data moves between devices by JAX's collectives and lax.ppermute only.
A program may use at most 64 MiB of HBM per device.

v0:
```python
import jax
import jax.numpy as jnp
from jax import lax
from jax.sharding import PartitionSpec as P


def passed_along(shard, axis, by):
    size = lax.axis_size(axis)
    pairs = [(i, i + by) for i in range(size) if 0 <= i + by < size]
    return lax.ppermute(shard, axis, pairs)


def rms_normed(hidden, gain_row):
    as_float = hidden.astype(jnp.float32)
    mean_square = jnp.mean(as_float * as_float, axis=-1, keepdims=True)
    return (as_float * lax.rsqrt(mean_square + 1e-05) * gain_row).astype(jnp.bfloat16)


def on_device(tokens, adapter_ids, ranks, gain, base_weight, shrink_weight, expand_weight):
    micro_count = tokens.shape[0]
    model_width = tokens.shape[2]
    own_cols = base_weight.shape[2]
    ad_count = ranks.shape[0]
    rank_most = shrink_weight.shape[3]
    total_adapters = expand_weight.shape[1]
    segment_count = lax.axis_size("segment")
    segment_index = lax.axis_index("segment")
    owner_index = lax.axis_index("adapter")
    all_rows = tokens.shape[1] * lax.axis_size("adapter")
    tick_count = segment_count + micro_count - 1
    all_ids = lax.all_gather(adapter_ids, "adapter", axis=1, tiled=True)[:, :, 0]
    wide_weight = jnp.concatenate(
        [
            base_weight[0],
            jnp.transpose(shrink_weight[0], (1, 0, 2)).reshape(model_width, ad_count * rank_most),
        ],
        axis=1,
    )
    my_adapters = owner_index * ad_count + jnp.arange(ad_count, dtype=jnp.int32)
    column_keep = (jnp.arange(rank_most)[None, :] < ranks[:, None]).astype(jnp.float32)
    factor_table = column_keep * (32.0 / ranks.astype(jnp.float32))[:, None]
    expand_flattened = expand_weight[0].reshape(total_adapters * rank_most, own_cols)
    gain_row = gain[0]
    adapter_range = jnp.arange(total_adapters, dtype=jnp.int32)

    def finish(joined_out, ids_now):
        base_contribution = joined_out[:, :own_cols]
        shrink_part = joined_out[:, own_cols:].reshape(all_rows, ad_count, rank_most)
        picked = (ids_now[:, None] == my_adapters[None, :]).astype(jnp.float32)
        local_terms = jnp.sum(shrink_part * (picked[:, :, None] * factor_table[None, :, :]), axis=1)
        low_rank = lax.psum(local_terms, "adapter").astype(jnp.bfloat16)
        onehot = (ids_now[:, None] == adapter_range[None, :]).astype(jnp.bfloat16)
        broadcast_rows = (onehot[:, :, None] * low_rank[:, None, :]).reshape(
            all_rows, total_adapters * rank_most
        )
        adapter_contribution = jnp.dot(
            broadcast_rows, expand_flattened, preferred_element_type=jnp.float32
        )
        return (base_contribution + adapter_contribution).astype(jnp.bfloat16)

    held_start = jnp.zeros((tokens.shape[1], model_width), jnp.bfloat16)

    def one_tick(tick_index, carry):
        held_rows, out_buffer = carry
        micro_now = tick_index - segment_index
        is_valid = jnp.logical_and(micro_now >= 0, micro_now < micro_count)
        micro_clip = jnp.clip(micro_now, 0, micro_count - 1)
        entering = lax.dynamic_index_in_dim(tokens, micro_clip, 0, keepdims=False)
        current = jnp.where(segment_index == 0, entering, held_rows)
        ids_now = lax.dynamic_index_in_dim(all_ids, micro_clip, 0, keepdims=False)
        normalized_hidden = rms_normed(current, gain_row)
        joined_out = jnp.dot(
            lax.all_gather(normalized_hidden, "adapter", axis=0, tiled=True),
            wide_weight,
            preferred_element_type=jnp.float32,
        )
        hidden_update = finish(joined_out, ids_now)
        returned = lax.all_to_all(hidden_update, "adapter", split_axis=0, concat_axis=1, tiled=True)
        new_hidden = (current.astype(jnp.float32) + returned.astype(jnp.float32)).astype(
            jnp.bfloat16
        )
        stored = lax.all_to_all(new_hidden, "adapter", split_axis=1, concat_axis=0, tiled=True)
        written = lax.dynamic_update_index_in_dim(out_buffer, stored, micro_clip, 0)
        out_buffer = jnp.where(is_valid, written, out_buffer)
        passed = passed_along(new_hidden, "segment", 1)
        return (passed, out_buffer)

    out_start = jnp.zeros((micro_count, all_rows, own_cols), jnp.bfloat16)
    final_carry = lax.fori_loop(0, tick_count, one_tick, (held_start, out_start))
    return final_carry[1][None]


def solution(mesh):
    in_specs = (
        P(None, "adapter", None),
        P(None, "adapter", None),
        P("adapter"),
        P("segment", None),
        P("segment", None, "adapter"),
        P("segment", "adapter", None, None),
        P("segment", None, None, "adapter"),
    )
    out_specs = P("segment", None, None, "adapter")
    return jax.shard_map(
        on_device, mesh=mesh, in_specs=in_specs, out_specs=out_specs, check_vma=False
    )
```

profile of v0, /device:TPU:7, one launch (start us, length us, event | category | flops | bytes accessed | tf_op | source)
XLA Modules:
  0.0 2343.8 jit_solution(12480859660475187758)
XLA Ops:
  17.0 36.1 %all_gather.11 = s32[2,64,1]{0,2,1:T(1,128)S(1)} all-gather(s32[2,2,1]{0,2,1:T(1,128)S(1)} %copy.23), channel_id=1, replica_groups=mesh['segment'=8,'adapter'=32] {'adapter'}, dimensions={1}, use_global_device_ids=true | all-gather | bytes 528 | tf_op jit(solution)/shard_map/all_gather | solution.py:31
  53.3 2283.4 %while.17 = (s32[]{:T(128)}, bf16[2,8192]{1,0:T(2,128)(2,1)S(1)}, bf16[2,64,256]{2,1,0:T(8,128)(2,1)S(1)}, pred[]{:T(512)}, s32[]{:T(128)}, /*index=5*/bf16[2,2,...) while((s32[]{:T(128)}, bf16[2,8192]{1,0:T(2,128)(2,1)S(1)}, ...), condition=%wide.region_4.5_spmd.clone, body=%wide.region_0.4_spmd.clone.sunk | while | flops 537412096 | bytes 18256268 | solution.py:89
  54.7 81.5 %all-gather.6.cloned.1.call-done = bf16[32,2,8192]{2,1,0:T(2,128)(2,1)} async-done(((bf16[1,2,8192]{2,1,0:T(2,128)(2,1)}), bf16[32,2,8192]{2,1,0:T(2,128)(2,1)}) %all-gather.6.cloned.1.call-update) | async-done | bytes 1048592 | tf_op jit(solution)/shard_map/while/body/eval_jaxpr/all_gather | solution.py:73
  141.8 112.5 %psum.14 = bf16[64,64]{1,0:T(8,128)(2,1)S(1)} all-reduce(f32[64,64]{1,0:T(8,128)S(1)} %multiply_reduce_fusion.2), channel_id=1, replica_groups=mesh['segment'=8,'adapter'=32] {'adapter'}, use_global_device_ids=true, to_apply=%region_3.3 | all-reduce | flops 4096 | bytes 24576 | tf_op jit(solution)/shard_map/while/body/eval_jaxpr/psum | solution.py:51
  283.0 28.1 %collective-permute-done = bf16[2,8192]{1,0:T(2,128)(2,1)S(1)} collective-permute-done((bf16[2,8192]{1,0:T(2,128)(2,1)}, bf16[2,8192]{1,0:T(2,128)(2,1)S(1)}, u32[]{:S(2)}, u32[]{:S(2)}) %collective-permute-start) | collective-permute-done | bytes 32800 | tf_op jit(solution)/shard_map/while/body/eval_jaxpr/ppermute | solution.py:10
  312.4 77.1 %all-gather.6.cloned.1.call-done = bf16[32,2,8192]{2,1,0:T(2,128)(2,1)} async-done(((bf16[1,2,8192]{2,1,0:T(2,128)(2,1)}), bf16[32,2,8192]{2,1,0:T(2,128)(2,1)}) %all-gather.6.cloned.1.call-update) | async-done | bytes 1048592 | tf_op jit(solution)/shard_map/while/body/eval_jaxpr/all_gather | solution.py:73
  395.1 112.5 %psum.14 = bf16[64,64]{1,0:T(8,128)(2,1)S(1)} all-reduce(f32[64,64]{1,0:T(8,128)S(1)} %multiply_reduce_fusion.2), channel_id=1, replica_groups=mesh['segment'=8,'adapter'=32] {'adapter'}, use_global_device_ids=true, to_apply=%region_3.3 | all-reduce | flops 4096 | bytes 24576 | tf_op jit(solution)/shard_map/while/body/eval_jaxpr/psum | solution.py:51
  536.3 28.1 %collective-permute-done = bf16[2,8192]{1,0:T(2,128)(2,1)S(1)} collective-permute-done((bf16[2,8192]{1,0:T(2,128)(2,1)}, bf16[2,8192]{1,0:T(2,128)(2,1)S(1)}, u32[]{:S(2)}, u32[]{:S(2)}) %collective-permute-start) | collective-permute-done | bytes 32800 | tf_op jit(solution)/shard_map/while/body/eval_jaxpr/ppermute | solution.py:10
  565.7 77.1 %all-gather.6.cloned.1.call-done = bf16[32,2,8192]{2,1,0:T(2,128)(2,1)} async-done(((bf16[1,2,8192]{2,1,0:T(2,128)(2,1)}), bf16[32,2,8192]{2,1,0:T(2,128)(2,1)}) %all-gather.6.cloned.1.call-update) | async-done | bytes 1048592 | tf_op jit(solution)/shard_map/while/body/eval_jaxpr/all_gather | solution.py:73
  648.4 112.5 %psum.14 = bf16[64,64]{1,0:T(8,128)(2,1)S(1)} all-reduce(f32[64,64]{1,0:T(8,128)S(1)} %multiply_reduce_fusion.2), channel_id=1, replica_groups=mesh['segment'=8,'adapter'=32] {'adapter'}, use_global_device_ids=true, to_apply=%region_3.3 | all-reduce | flops 4096 | bytes 24576 | tf_op jit(solution)/shard_map/while/body/eval_jaxpr/psum | solution.py:51
  789.6 28.1 %collective-permute-done = bf16[2,8192]{1,0:T(2,128)(2,1)S(1)} collective-permute-done((bf16[2,8192]{1,0:T(2,128)(2,1)}, bf16[2,8192]{1,0:T(2,128)(2,1)S(1)}, u32[]{:S(2)}, u32[]{:S(2)}) %collective-permute-start) | collective-permute-done | bytes 32800 | tf_op jit(solution)/shard_map/while/body/eval_jaxpr/ppermute | solution.py:10
  819.0 76.8 %all-gather.6.cloned.1.call-done = bf16[32,2,8192]{2,1,0:T(2,128)(2,1)} async-done(((bf16[1,2,8192]{2,1,0:T(2,128)(2,1)}), bf16[32,2,8192]{2,1,0:T(2,128)(2,1)}) %all-gather.6.cloned.1.call-update) | async-done | bytes 1048592 | tf_op jit(solution)/shard_map/while/body/eval_jaxpr/all_gather | solution.py:73
  901.4 112.5 %psum.14 = bf16[64,64]{1,0:T(8,128)(2,1)S(1)} all-reduce(f32[64,64]{1,0:T(8,128)S(1)} %multiply_reduce_fusion.2), channel_id=1, replica_groups=mesh['segment'=8,'adapter'=32] {'adapter'}, use_global_device_ids=true, to_apply=%region_3.3 | all-reduce | flops 4096 | bytes 24576 | tf_op jit(solution)/shard_map/while/body/eval_jaxpr/psum | solution.py:51
  1072.0 76.8 %all-gather.6.cloned.1.call-done = bf16[32,2,8192]{2,1,0:T(2,128)(2,1)} async-done(((bf16[1,2,8192]{2,1,0:T(2,128)(2,1)}), bf16[32,2,8192]{2,1,0:T(2,128)(2,1)}) %all-gather.6.cloned.1.call-update) | async-done | bytes 1048592 | tf_op jit(solution)/shard_map/while/body/eval_jaxpr/all_gather | solution.py:73
  1154.4 112.5 %psum.14 = bf16[64,64]{1,0:T(8,128)(2,1)S(1)} all-reduce(f32[64,64]{1,0:T(8,128)S(1)} %multiply_reduce_fusion.2), channel_id=1, replica_groups=mesh['segment'=8,'adapter'=32] {'adapter'}, use_global_device_ids=true, to_apply=%region_3.3 | all-reduce | flops 4096 | bytes 24576 | tf_op jit(solution)/shard_map/while/body/eval_jaxpr/psum | solution.py:51
  1325.0 76.8 %all-gather.6.cloned.1.call-done = bf16[32,2,8192]{2,1,0:T(2,128)(2,1)} async-done(((bf16[1,2,8192]{2,1,0:T(2,128)(2,1)}), bf16[32,2,8192]{2,1,0:T(2,128)(2,1)}) %all-gather.6.cloned.1.call-update) | async-done | bytes 1048592 | tf_op jit(solution)/shard_map/while/body/eval_jaxpr/all_gather | solution.py:73
  1407.4 112.5 %psum.14 = bf16[64,64]{1,0:T(8,128)(2,1)S(1)} all-reduce(f32[64,64]{1,0:T(8,128)S(1)} %multiply_reduce_fusion.2), channel_id=1, replica_groups=mesh['segment'=8,'adapter'=32] {'adapter'}, use_global_device_ids=true, to_apply=%region_3.3 | all-reduce | flops 4096 | bytes 24576 | tf_op jit(solution)/shard_map/while/body/eval_jaxpr/psum | solution.py:51
  1578.0 77.1 %all-gather.6.cloned.1.call-done = bf16[32,2,8192]{2,1,0:T(2,128)(2,1)} async-done(((bf16[1,2,8192]{2,1,0:T(2,128)(2,1)}), bf16[32,2,8192]{2,1,0:T(2,128)(2,1)}) %all-gather.6.cloned.1.call-update) | async-done | bytes 1048592 | tf_op jit(solution)/shard_map/while/body/eval_jaxpr/all_gather | solution.py:73
  1660.7 112.5 %psum.14 = bf16[64,64]{1,0:T(8,128)(2,1)S(1)} all-reduce(f32[64,64]{1,0:T(8,128)S(1)} %multiply_reduce_fusion.2), channel_id=1, replica_groups=mesh['segment'=8,'adapter'=32] {'adapter'}, use_global_device_ids=true, to_apply=%region_3.3 | all-reduce | flops 4096 | bytes 24576 | tf_op jit(solution)/shard_map/while/body/eval_jaxpr/psum | solution.py:51
  1801.9 28.1 %collective-permute-done = bf16[2,8192]{1,0:T(2,128)(2,1)S(1)} collective-permute-done((bf16[2,8192]{1,0:T(2,128)(2,1)}, bf16[2,8192]{1,0:T(2,128)(2,1)S(1)}, u32[]{:S(2)}, u32[]{:S(2)}) %collective-permute-start) | collective-permute-done | bytes 32800 | tf_op jit(solution)/shard_map/while/body/eval_jaxpr/ppermute | solution.py:10
  1831.4 77.1 %all-gather.6.cloned.1.call-done = bf16[32,2,8192]{2,1,0:T(2,128)(2,1)} async-done(((bf16[1,2,8192]{2,1,0:T(2,128)(2,1)}), bf16[32,2,8192]{2,1,0:T(2,128)(2,1)}) %all-gather.6.cloned.1.call-update) | async-done | bytes 1048592 | tf_op jit(solution)/shard_map/while/body/eval_jaxpr/all_gather | solution.py:73
  1914.1 112.5 %psum.14 = bf16[64,64]{1,0:T(8,128)(2,1)S(1)} all-reduce(f32[64,64]{1,0:T(8,128)S(1)} %multiply_reduce_fusion.2), channel_id=1, replica_groups=mesh['segment'=8,'adapter'=32] {'adapter'}, use_global_device_ids=true, to_apply=%region_3.3 | all-reduce | flops 4096 | bytes 24576 | tf_op jit(solution)/shard_map/while/body/eval_jaxpr/psum | solution.py:51
  2084.7 77.1 %all-gather.6.cloned.1.call-done = bf16[32,2,8192]{2,1,0:T(2,128)(2,1)} async-done(((bf16[1,2,8192]{2,1,0:T(2,128)(2,1)}), bf16[32,2,8192]{2,1,0:T(2,128)(2,1)}) %all-gather.6.cloned.1.call-update) | async-done | bytes 1048592 | tf_op jit(solution)/shard_map/while/body/eval_jaxpr/all_gather | solution.py:73
  2167.4 112.5 %psum.14 = bf16[64,64]{1,0:T(8,128)(2,1)S(1)} all-reduce(f32[64,64]{1,0:T(8,128)S(1)} %multiply_reduce_fusion.2), channel_id=1, replica_groups=mesh['segment'=8,'adapter'=32] {'adapter'}, use_global_device_ids=true, to_apply=%region_3.3 | all-reduce | flops 4096 | bytes 24576 | tf_op jit(solution)/shard_map/while/body/eval_jaxpr/psum | solution.py:51
  (276 shorter events, 471.2 us)
Async XLA Ops:
  53.3 82.9 %all-gather.6.cloned.1.call-start = ((), (), s32[]{:S(2)}) async-start(), calls=%async_computation.2 | async-start | bytes 1081344 | tf_op jit(solution)/shard_map/while/body/eval_jaxpr/all_gather | solution.py:73
  274.3 36.9 %collective-permute-start = (bf16[2,8192]{1,0:T(2,128)(2,1)}, bf16[2,8192]{1,0:T(2,128)(2,1)S(1)}, u32[]{:S(2)}, u32[]{:S(2)}) collective-permute-start(bf16[2,8192]{1,0:T(2,128)(2,1)} %fusion.40), channel_id=1, source_target_pairs={{0,32},{32,64},{64,96},{96,128},{128,160},{160,192},{192,224},{1,3... | collective-permute-start | bytes 98312 | tf_op jit(solution)/shard_map/while/body/eval_jaxpr/ppermute | solution.py:10
  311.1 78.4 %all-gather.6.cloned.1.call-start = ((), (), s32[]{:S(2)}) async-start(), calls=%async_computation.2 | async-start | bytes 1081344 | tf_op jit(solution)/shard_map/while/body/eval_jaxpr/all_gather | solution.py:73
  523.7 12.6 all-to-all-start.1
  527.6 36.9 %collective-permute-start = (bf16[2,8192]{1,0:T(2,128)(2,1)}, bf16[2,8192]{1,0:T(2,128)(2,1)S(1)}, u32[]{:S(2)}, u32[]{:S(2)}) collective-permute-start(bf16[2,8192]{1,0:T(2,128)(2,1)} %fusion.40), channel_id=1, source_target_pairs={{0,32},{32,64},{64,96},{96,128},{128,160},{160,192},{192,224},{1,3... | collective-permute-start | bytes 98312 | tf_op jit(solution)/shard_map/while/body/eval_jaxpr/ppermute | solution.py:10
  564.4 78.4 %all-gather.6.cloned.1.call-start = ((), (), s32[]{:S(2)}) async-start(), calls=%async_computation.2 | async-start | bytes 1081344 | tf_op jit(solution)/shard_map/while/body/eval_jaxpr/all_gather | solution.py:73
  777.0 12.6 all-to-all-start.1
  780.9 36.9 %collective-permute-start = (bf16[2,8192]{1,0:T(2,128)(2,1)}, bf16[2,8192]{1,0:T(2,128)(2,1)S(1)}, u32[]{:S(2)}, u32[]{:S(2)}) collective-permute-start(bf16[2,8192]{1,0:T(2,128)(2,1)} %fusion.40), channel_id=1, source_target_pairs={{0,32},{32,64},{64,96},{96,128},{128,160},{160,192},{192,224},{1,3... | collective-permute-start | bytes 98312 | tf_op jit(solution)/shard_map/while/body/eval_jaxpr/ppermute | solution.py:10
  817.7 78.1 %all-gather.6.cloned.1.call-start = ((), (), s32[]{:S(2)}) async-start(), calls=%async_computation.2 | async-start | bytes 1081344 | tf_op jit(solution)/shard_map/while/body/eval_jaxpr/all_gather | solution.py:73
  1030.0 12.6 all-to-all-start.1
  1033.9 36.9 %collective-permute-start = (bf16[2,8192]{1,0:T(2,128)(2,1)}, bf16[2,8192]{1,0:T(2,128)(2,1)S(1)}, u32[]{:S(2)}, u32[]{:S(2)}) collective-permute-start(bf16[2,8192]{1,0:T(2,128)(2,1)} %fusion.40), channel_id=1, source_target_pairs={{0,32},{32,64},{64,96},{96,128},{128,160},{160,192},{192,224},{1,3... | collective-permute-start | bytes 98312 | tf_op jit(solution)/shard_map/while/body/eval_jaxpr/ppermute | solution.py:10
  1070.7 78.1 %all-gather.6.cloned.1.call-start = ((), (), s32[]{:S(2)}) async-start(), calls=%async_computation.2 | async-start | bytes 1081344 | tf_op jit(solution)/shard_map/while/body/eval_jaxpr/all_gather | solution.py:73
  1286.9 36.9 %collective-permute-start = (bf16[2,8192]{1,0:T(2,128)(2,1)}, bf16[2,8192]{1,0:T(2,128)(2,1)S(1)}, u32[]{:S(2)}, u32[]{:S(2)}) collective-permute-start(bf16[2,8192]{1,0:T(2,128)(2,1)} %fusion.40), channel_id=1, source_target_pairs={{0,32},{32,64},{64,96},{96,128},{128,160},{160,192},{192,224},{1,3... | collective-permute-start | bytes 98312 | tf_op jit(solution)/shard_map/while/body/eval_jaxpr/ppermute | solution.py:10
  1323.7 78.1 %all-gather.6.cloned.1.call-start = ((), (), s32[]{:S(2)}) async-start(), calls=%async_computation.2 | async-start | bytes 1081344 | tf_op jit(solution)/shard_map/while/body/eval_jaxpr/all_gather | solution.py:73
  1536.0 12.6 all-to-all-start.1
  1539.9 36.9 %collective-permute-start = (bf16[2,8192]{1,0:T(2,128)(2,1)}, bf16[2,8192]{1,0:T(2,128)(2,1)S(1)}, u32[]{:S(2)}, u32[]{:S(2)}) collective-permute-start(bf16[2,8192]{1,0:T(2,128)(2,1)} %fusion.40), channel_id=1, source_target_pairs={{0,32},{32,64},{64,96},{96,128},{128,160},{160,192},{192,224},{1,3... | collective-permute-start | bytes 98312 | tf_op jit(solution)/shard_map/while/body/eval_jaxpr/ppermute | solution.py:10
  1576.7 78.4 %all-gather.6.cloned.1.call-start = ((), (), s32[]{:S(2)}) async-start(), calls=%async_computation.2 | async-start | bytes 1081344 | tf_op jit(solution)/shard_map/while/body/eval_jaxpr/all_gather | solution.py:73
  1793.2 36.9 %collective-permute-start = (bf16[2,8192]{1,0:T(2,128)(2,1)}, bf16[2,8192]{1,0:T(2,128)(2,1)S(1)}, u32[]{:S(2)}, u32[]{:S(2)}) collective-permute-start(bf16[2,8192]{1,0:T(2,128)(2,1)} %fusion.40), channel_id=1, source_target_pairs={{0,32},{32,64},{64,96},{96,128},{128,160},{160,192},{192,224},{1,3... | collective-permute-start | bytes 98312 | tf_op jit(solution)/shard_map/while/body/eval_jaxpr/ppermute | solution.py:10
  1830.1 78.4 %all-gather.6.cloned.1.call-start = ((), (), s32[]{:S(2)}) async-start(), calls=%async_computation.2 | async-start | bytes 1081344 | tf_op jit(solution)/shard_map/while/body/eval_jaxpr/all_gather | solution.py:73
  2042.6 12.6 all-to-all-start.1
  2046.5 36.9 %collective-permute-start = (bf16[2,8192]{1,0:T(2,128)(2,1)}, bf16[2,8192]{1,0:T(2,128)(2,1)S(1)}, u32[]{:S(2)}, u32[]{:S(2)}) collective-permute-start(bf16[2,8192]{1,0:T(2,128)(2,1)} %fusion.40), channel_id=1, source_target_pairs={{0,32},{32,64},{64,96},{96,128},{128,160},{160,192},{192,224},{1,3... | collective-permute-start | bytes 98312 | tf_op jit(solution)/shard_map/while/body/eval_jaxpr/ppermute | solution.py:10
  2083.4 78.4 %all-gather.6.cloned.1.call-start = ((), (), s32[]{:S(2)}) async-start(), calls=%async_computation.2 | async-start | bytes 1081344 | tf_op jit(solution)/shard_map/while/body/eval_jaxpr/all_gather | solution.py:73
  2295.9 12.6 all-to-all-start.1
  2299.8 36.9 %collective-permute-start = (bf16[2,8192]{1,0:T(2,128)(2,1)}, bf16[2,8192]{1,0:T(2,128)(2,1)S(1)}, u32[]{:S(2)}, u32[]{:S(2)}) collective-permute-start(bf16[2,8192]{1,0:T(2,128)(2,1)} %fusion.40), channel_id=1, source_target_pairs={{0,32},{32,64},{64,96},{96,128},{128,160},{160,192},{192,224},{1,3... | collective-permute-start | bytes 98312 | tf_op jit(solution)/shard_map/while/body/eval_jaxpr/ppermute | solution.py:10
  (9 other events, 215.0 us)
Sparse Core Ops, SparseCore 0:
  56.7 79.4 all-gather.5
  314.5 74.9 all-gather.5
  567.8 74.9 all-gather.5
  820.8 74.9 all-gather.5
  1073.8 74.9 all-gather.5
  1326.8 74.9 all-gather.5
  1580.1 74.9 all-gather.5
  1833.5 74.9 all-gather.5
  2086.8 74.9 all-gather.5
where the time goes:
time: 2350 us; the launch traced here: 2340 us
  blocking collectives  1150 us (49%)
  waiting for transfers between devices  1020 us (43%)
  matrix products  48 us (2%)
  starting transfers between devices  46.4 us (2%)
  local copies, waits for them, and re-layouts  35 us (1%)
  other arithmetic  29.7 us (1%)
    psum x9, blocking collectives, finish(): low_rank = lax.psum(local_terms, 'adapter').astype(jnp.bfloat16)  1010 us
    all_gather x9, waiting for transfers between devices, one_tick(): lax.all_gather(normalized_hidden, 'adapter', axis=0, tiled=True)  697 us
    ppermute x9, waiting for transfers between devices, passed_along(): return lax.ppermute(shard, axis, pairs)  253 us
    all_to_all x9, blocking collectives, one_tick(): lax.all_to_all(hidden_update, 'adapter', split_axis=0, concat_axis=1, til...  105 us
    all_to_all x9, waiting for transfers between devices, one_tick(): lax.all_to_all(new_hidden, 'adapter', split_axis=1, concat_axis=0, tiled=...  66.5 us
  transfers between devices with their start and end apart: 27, of which 27 were waited for; matrix products, arithmetic and copies ran while one was open for 0% of the time, Pallas kernels for 0%

commit v1 on v0

v1 whole, which is shorter than its diff:
```python
import jax
import jax.numpy as jnp
from jax import lax
from jax.experimental import pallas as pl
from jax.experimental.pallas import tpu as pltpu
from jax.sharding import PartitionSpec as P

GROUP = 4


def lane_group(shape, rank_most):
    return lax.broadcasted_iota(jnp.int32, shape, len(shape) - 1) // rank_most


def spread(value, rank_most):
    step = rank_most
    while step < value.shape[-1]:
        value = value + pltpu.roll(value, step, 1)
        step *= 2
    return value


def before_kernel(rank_most, h_ref, ids_ref, shrink_ref, out_ref):
    rows, cols = h_ref.shape
    packed = rows // GROUP
    h = h_ref[...]
    groups = lane_group((rows, cols), rank_most)
    wanted = ids_ref[...] - groups
    total = jnp.zeros((rows, cols), jnp.float32)
    for j in range(shrink_ref.shape[0] // cols):
        part = lax.dot_general(
            h,
            shrink_ref[j * cols : (j + 1) * cols, :],
            (((1,), (1,)), ((), ())),
            preferred_element_type=jnp.float32,
        )
        total = total + jnp.where(wanted == j * GROUP, part, 0.0)
    total = spread(total, rank_most)
    folded = jnp.zeros((packed, cols), jnp.float32)
    for g in range(GROUP):
        mine = groups[:packed] == g
        folded = jnp.where(mine, total[g * packed : (g + 1) * packed], folded)
    folded = folded.astype(jnp.bfloat16)
    for d in range(out_ref.shape[0]):
        out_ref[d, :rows, :] = h
        out_ref[d, rows:, :] = folded


def after_kernel(rank_most, h_ref, got_ref, ids_ref, rank_ref, base_ref, expand_ref, out_ref):
    rows, cols = h_ref.shape
    packed = rows // GROUP
    sources = got_ref.shape[0]
    groups = lane_group((rows, cols), rank_most)
    base = jnp.zeros((rows, cols), jnp.float32)
    squares = jnp.zeros((rows, cols), jnp.float32)
    partial = jnp.zeros((packed, cols), jnp.float32)
    for j in range(sources):
        block = got_ref[j, :rows, :]
        base = base + jnp.dot(
            block, base_ref[j * cols : (j + 1) * cols, :], preferred_element_type=jnp.float32
        )
        wide = block.astype(jnp.float32)
        squares = squares + wide * wide
        partial = partial + got_ref[j, rows:, :].astype(jnp.float32)
    mean_square = jnp.sum(squares, axis=-1, keepdims=True) / (sources * cols)
    inverse = lax.rsqrt(mean_square + 1e-05)
    low = jnp.concatenate(
        [
            spread(jnp.where(groups[:packed] == g, partial, 0.0), rank_most)
            for g in range(GROUP)
        ],
        axis=0,
    )
    rank = rank_ref[...]
    place = lax.broadcasted_iota(jnp.int32, (rows, cols), 1) - groups * rank_most
    factor = jnp.where(place.astype(jnp.float32) < rank, 32.0 / rank, 0.0)
    low = low * inverse * factor
    wanted = ids_ref[...] - groups
    added = jnp.zeros((rows, cols), jnp.float32)
    for j in range(expand_ref.shape[0] // cols):
        picked = jnp.where(wanted == j * GROUP, low, 0.0).astype(jnp.bfloat16)
        added = added + jnp.dot(
            picked, expand_ref[j * cols : (j + 1) * cols, :], preferred_element_type=jnp.float32
        )
    update = (base * inverse + added).astype(jnp.bfloat16)
    out_ref[...] = (h_ref[...].astype(jnp.float32) + update.astype(jnp.float32)).astype(
        jnp.bfloat16
    )


def in_vmem(count):
    return [pl.BlockSpec(memory_space=pltpu.VMEM)] * count


def on_device(tokens, adapter_ids, ranks, gain, base_weight, shrink_weight, expand_weight):
    micro_count, own_rows, model_width = tokens.shape
    cols = base_weight.shape[2]
    ad_count, _, rank_most = shrink_weight.shape[1:]
    total_adapters = expand_weight.shape[1]
    devices = lax.axis_size("adapter")
    segments = lax.axis_size("segment")
    planes = segments // 2
    segment = lax.axis_index("segment")
    owner = lax.axis_index("adapter")
    plane, core = segment // 2, segment % 2
    rows = own_rows * devices
    params = pltpu.CompilerParams(vmem_limit_bytes=40 * 1024 * 1024)

    by_dest = tokens.reshape(micro_count * own_rows, devices, cols).transpose(1, 0, 2)
    small = jnp.concatenate([adapter_ids.reshape(-1), ranks]).astype(jnp.bfloat16)
    small = jnp.pad(small, (0, cols - small.shape[0]))
    small = jnp.broadcast_to(small, (devices, micro_count * own_rows, cols))
    first = lax.all_to_all(
        jnp.concatenate([by_dest, small], axis=1), "adapter", 0, 0, tiled=True
    )
    count = micro_count * own_rows
    token_cols = (
        first[:, :count]
        .reshape(devices, micro_count, own_rows, cols)
        .transpose(1, 0, 2, 3)
        .reshape(micro_count, rows, cols)
    )
    all_ids = (
        first[:, count, :count]
        .reshape(devices, micro_count, own_rows)
        .transpose(1, 0, 2)
        .reshape(micro_count, rows)
        .astype(jnp.int32)
    )
    all_ranks = first[:, count, count : count + ad_count].reshape(-1).astype(jnp.float32)
    onehot = all_ids[:, :, None] == jnp.arange(total_adapters, dtype=jnp.int32)
    row_ranks = jnp.sum(jnp.where(onehot, all_ranks, 0.0), axis=-1, keepdims=True)

    shrink = shrink_weight[0].reshape(ad_count, devices, cols, rank_most).transpose(1, 0, 3, 2)
    shrink = lax.all_to_all(
        shrink.reshape(devices, ad_count * rank_most, cols), "adapter", 0, 0, tiled=True
    ).reshape(total_adapters * rank_most, cols)
    own_gain = lax.dynamic_slice_in_dim(gain[0], owner * cols, cols, 0)
    shrink = (shrink.astype(jnp.float32) * own_gain[None, :]).astype(jnp.bfloat16)
    base = (base_weight[0].astype(jnp.float32) * gain[0][:, None]).astype(jnp.bfloat16)
    expand = expand_weight[0].reshape(total_adapters * rank_most, cols)

    block_rows = rows + rows // GROUP

    def work(h, ids, rank):
        sent = pl.pallas_call(
            lambda *refs: before_kernel(rank_most, *refs),
            out_shape=jax.ShapeDtypeStruct((devices, block_rows, cols), jnp.bfloat16),
            in_specs=in_vmem(3),
            out_specs=in_vmem(1)[0],
            compiler_params=params,
        )(h, ids, shrink)
        got = lax.all_to_all(sent, "adapter", 0, 0, tiled=True)
        return pl.pallas_call(
            lambda *refs: after_kernel(rank_most, *refs),
            out_shape=jax.ShapeDtypeStruct((rows, cols), jnp.bfloat16),
            in_specs=in_vmem(6),
            out_specs=in_vmem(1)[0],
            compiler_params=params,
        )(h, got, ids, rank, base, expand)

    to_core = [(2 * p, 2 * p + 1) for p in range(planes)]
    to_plane = [(2 * p + 1, 2 * p + 2) for p in range(planes - 1)]

    def super_tick(k, carry):
        h, out = carry
        micro = k - plane
        valid = (micro >= 0) & (micro < micro_count)
        micro = jnp.clip(micro, 0, micro_count - 1)
        h = jnp.where(segment == 0, token_cols[micro], h)
        ids, rank = all_ids[micro][:, None], row_ranks[micro]
        for turn in range(2):
            active = valid & (core == turn)
            h = lax.cond(active, work, lambda h, ids, rank: h, h, ids, rank)
            out = jnp.where(active, lax.dynamic_update_index_in_dim(out, h, micro, 0), out)
            h = lax.ppermute(h, "segment", to_plane if turn else to_core)
        return h, out

    start = (
        jnp.zeros((rows, cols), jnp.bfloat16),
        jnp.zeros((micro_count, rows, cols), jnp.bfloat16),
    )
    return lax.fori_loop(0, planes + micro_count - 1, super_tick, start)[1][None]


def solution(mesh):
    in_specs = (
        P(None, "adapter", None),
        P(None, "adapter", None),
        P("adapter"),
        P("segment", None),
        P("segment", None, "adapter"),
        P("segment", "adapter", None, None),
        P("segment", None, None, "adapter"),
    )
    out_specs = P("segment", None, None, "adapter")
    return jax.shard_map(
        on_device, mesh=mesh, in_specs=in_specs, out_specs=out_specs, check_vma=False
    )
```

time: 2350 us -> 449 us (0.19)
  blocking collectives: 1150 us -> 0 us
  waiting for transfers between devices: 1020 us -> 359 us
  matrix products: 48 us -> 0 us
  local copies, waits for them, and re-layouts: 35 us -> 11.5 us
    psum x9 -> x0, blocking collectives: 1010 us -> none  [finish(): low_rank = lax.psum(local_terms, 'adapter').astype(jnp.bfloat16)]
    all_gather x9 -> x0, waiting for transfers between devices: 697 us -> none  [one_tick(): lax.all_gather(normalized_hidden, 'adapter', axis=0, tiled=True)]
    all_to_all x9 -> x0, blocking collectives: 105 us -> none  [one_tick(): lax.all_to_all(hidden_update, 'adapter', split_axis=0, concat_axis=1, til...]
    dot_general x18 -> x0, matrix products: 48 us -> none  [the longest x9 34.4 us: one_tick(): jnp.dot(lax.all_gather(normalized_hidden, 'adapter', axis=0, tiled=True),...]
    all_gather x1 -> x0, blocking collectives: 36.1 us -> none  [on_device(): lax.all_gather(adapter_ids, 'adapter', axis=1, tiled=True)[:, :, 0]]
    all_to_all x9 -> x4, waiting for transfers between devices: 66.5 us -> 90.5 us  [the longest x2 43 us: work(): got = lax.all_to_all(sent, 'adapter', 0, 0, tiled=True)]
    ppermute x9 -> x10, waiting for transfers between devices: 253 us -> 269 us  [super_tick(): h = lax.ppermute(h, 'segment', to_plane if turn else to_core)]
  transfers between devices with their start and end apart: 27 -> 14, of which waited for: 27 -> 9; matrix products, arithmetic and copies ran while one was open for 0% -> 5% of each run, Pallas kernels for 0% -> 0%
where the time goes in v1:
time: 449 us; the launch traced here: 447 us
  waiting for transfers between devices  359 us (80%)
  starting transfers between devices  36.4 us (8%)
  other arithmetic  25.7 us (6%)
  Pallas kernels  13.4 us (3%)
  local copies, waits for them, and re-layouts  11.5 us (3%)
    ppermute x10, waiting for transfers between devices, super_tick(): h = lax.ppermute(h, 'segment', to_plane if turn else to_core)  269 us
    all_to_all x2, waiting for transfers between devices, work(): got = lax.all_to_all(sent, 'adapter', 0, 0, tiled=True)  43 us
    all_to_all x1, waiting for transfers between devices, on_device(): lax.all_to_all(shrink.reshape(devices, ad_count * rank_most, cols), 'adap...  43 us
    select_n x10, other arithmetic, super_tick(): jnp.where(active, lax.dynamic_update_index_in_dim(out, h, micro, 0), out)  14 us
    all_to_all x1, starting transfers between devices, on_device(): lax.all_to_all(jnp.concatenate([by_dest, small], axis=1), 'adapter', 0, 0...  11.2 us
    all_to_all x2, starting transfers between devices, work(): got = lax.all_to_all(sent, 'adapter', 0, 0, tiled=True)  10.6 us
    ppermute x10, starting transfers between devices, super_tick(): h = lax.ppermute(h, 'segment', to_plane if turn else to_core)  9.66 us
    pallas_call x2, Pallas kernels, work(): pl.pallas_call(lambda *refs: after_kernel(rank_most, *refs), out_shape=ja...  9.5 us
  transfers between devices with their start and end apart: 14, of which 9 were waited for; matrix products, arithmetic and copies ran while one was open for 5% of the time, Pallas kernels for 0%

profile of v1, /device:TPU:7, one launch (start us, length us, event | category | flops | bytes accessed | tf_op | source)
XLA Modules:
  0.0 446.7 jit_solution(2068284792215283656)
XLA Ops:
  3.2 11.2 %all-to-all-start.2 = ((bf16[32,8,256]{2,1,0:T(8,128)(2,1)}), bf16[32,8,256]{2,1,0:T(8,128)(2,1)S(1)}, u32[]{:S(2)}, u32[]{:S(2)}) async-start(bf16[32,8,256]{2,1,0:T(8,128)(2,1)} %copy.59), calls=%async_computation.2 | async-start | bytes 262144 | tf_op jit(solution)/shard_map/all_to_all | solution.py:113
  14.4 2.2 copy.66
  16.6 2.5 copy.63
  19.1 4.5 all-to-all-done.2
  23.5 4.9 %all-to-all-start.3 = ((bf16[32,128,256]{2,1,0:T(8,128)(2,1)}), bf16[32,128,256]{2,1,0:T(8,128)(2,1)S(1)}, u32[]{:S(2)}, u32[]{:S(2)}) async-start(bf16[32,128,256]{2,1,0:T(8,128)(2,1)} %bitcast.54), calls=%async_computation.3 | async-start | bytes 4194304 | tf_op jit(solution)/shard_map/all_to_all | solution.py:135
  28.5 4.1 fusion.4
  34.2 43.0 %all-to-all-done.3 = bf16[32,128,256]{2,1,0:T(8,128)(2,1)S(1)} async-done(((bf16[32,128,256]{2,1,0:T(8,128)(2,1)}), bf16[32,128,256]{2,1,0:T(8,128)(2,1)S(1)}, u32[]{:S(2)}, u32[]{:S(2)}) %all-to-all-start.3) | async-done | bytes 2097184 | tf_op jit(solution)/shard_map/all_to_all | solution.py:135
  78.5 2.0 fusion.5
  81.1 365.5 %while.17 = (s32[]{:T(128)}, bf16[64,256]{1,0:T(8,128)(2,1)S(1)}, bf16[2,64,256]{2,1,0:T(8,128)(2,1)}, s32[]{:T(128)}, pred[]{:T(512)}, /*index=5*/pred[]{:T(512...) while((s32[]{:T(128)}, bf16[64,256]{1,0:T(8,128)(2,1)S(1)}, ...), condition=%wide.region_6.7_spmd, body=%wide.region_1.6_spmd.sunk | while | flops 49164 | bytes 8556021 | solution.py:183
  84.6 1.9 collective-permute-done
  92.0 4.0 collective-permute-done
  101.5 4.0 collective-permute-done
  111.0 251.7 %collective-permute-done = bf16[64,256]{1,0:T(8,128)(2,1)} collective-permute-done((bf16[64,256]{1,0:T(8,128)(2,1)S(1)}, bf16[64,256]{1,0:T(8,128)(2,1)}, u32[]{:S(2)}, u32[]{:S(2)}) %collective-permute-start) | collective-permute-done | bytes 32800 | tf_op jit(solution)/shard_map/while/body/eval_jaxpr/ppermute | solution.py:176
  362.7 36.0 %conditional.5 = (bf16[64,256]{1,0:T(8,128)(2,1)}) conditional(s32[]{:T(128)} %convert_element_type.86, bf16[64,256]{1,0:T(8,128)(2,1)} %collective-permute-done, (bf16[64,256]{1,0:T(8,128)(2,1)}, s32[64,1]{0,1:T(1,128)S(1)}, bf16[4096,256]{1,0:T(8,128)(2,1)S(1)}, f32[64,1]{0,1:T(1,128)S(1)}, bf16[8192,256]{1,0:T(8,128)(2,1)}, ...), branch_computations={%region_4.4_spmd, %region_5.5_spmd} | conditional | bytes 3998760 | solution.py:174
  363.6 1.9 branch_1_fun.6
  365.5 5.3 %all-to-all-start.1 = ((bf16[32,80,256]{2,1,0:T(8,128)(2,1)}), bf16[32,80,256]{2,1,0:T(8,128)(2,1)S(1)}, u32[]{:S(2)}, u32[]{:S(2)}) async-start(bf16[32,80,256]{2,1,0:T(8,128)(2,1)} %branch_1_fun.6), calls=%async_computation.1 | async-start | bytes 2621440 | tf_op jit(solution)/shard_map/while/body/eval_jaxpr/cond/branch_1_fun/all_to_all | solution.py:153
  370.9 23.1 %all-to-all-done.1.refs_1_ = bf16[32,80,256]{2,1,0:T(8,128)(2,1)S(1)} async-done(((bf16[32,80,256]{2,1,0:T(8,128)(2,1)}), bf16[32,80,256]{2,1,0:T(8,128)(2,1)S(1)}, u32[]{:S(2)}, u32[]{:S(2)}) %all-to-all-start.1) | async-done | bytes 1310752 | tf_op jit(solution)/shard_map/while/body/eval_jaxpr/cond/branch_1_fun/all_to_all | solution.py:153
  394.0 4.8 %branch_1_fun.7 = bf16[64,256]{1,0:T(8,128)(2,1)} custom-call(bf16[64,256]{1,0:T(8,128)(2,1)S(1)} %copy.85.refs_0_, bf16[32,80,256]{2,1,0:T(8,128)(2,1)S(1)} %all-to-all-done.1.refs_1_, s32[64,1]{1,0:T(8,128)S(1)} %copy.57.refs_1_.refs_2_, f32[64,1]{1,0:T(8,128)S(1)} %copy.58.refs_3_, bf16[8192,256]{1,0:T(8,128)(2,1)} %get-tuple-element.340.refs_4_, ...), custom_call_target="tpu_custom_call" | custom-call | tf_op jit(solution)/shard_map/while/body/eval_jaxpr/cond/branch_1_fun/pallas_call | solution.py:154
  404.3 7.4 %collective-permute-done = bf16[64,256]{1,0:T(8,128)(2,1)} collective-permute-done((bf16[64,256]{1,0:T(8,128)(2,1)S(1)}, bf16[64,256]{1,0:T(8,128)(2,1)}, u32[]{:S(2)}, u32[]{:S(2)}) %collective-permute-start) | collective-permute-done | bytes 32800 | tf_op jit(solution)/shard_map/while/body/eval_jaxpr/ppermute | solution.py:176
  411.7 32.9 %conditional.5 = (bf16[64,256]{1,0:T(8,128)(2,1)}) conditional(s32[]{:T(128)} %convert_element_type.86, bf16[64,256]{1,0:T(8,128)(2,1)} %collective-permute-done, (bf16[64,256]{1,0:T(8,128)(2,1)}, s32[64,1]{0,1:T(1,128)S(1)}, bf16[4096,256]{1,0:T(8,128)(2,1)S(1)}, f32[64,1]{0,1:T(1,128)S(1)}, bf16[8192,256]{1,0:T(8,128)(2,1)}, ...), branch_computations={%region_4.4_spmd, %region_5.5_spmd} | conditional | bytes 3998760 | solution.py:174
  412.5 1.9 branch_1_fun.6
  414.5 5.4 %all-to-all-start.1 = ((bf16[32,80,256]{2,1,0:T(8,128)(2,1)}), bf16[32,80,256]{2,1,0:T(8,128)(2,1)S(1)}, u32[]{:S(2)}, u32[]{:S(2)}) async-start(bf16[32,80,256]{2,1,0:T(8,128)(2,1)} %branch_1_fun.6), calls=%async_computation.1 | async-start | bytes 2621440 | tf_op jit(solution)/shard_map/while/body/eval_jaxpr/cond/branch_1_fun/all_to_all | solution.py:153
  419.9 19.9 %all-to-all-done.1.refs_1_ = bf16[32,80,256]{2,1,0:T(8,128)(2,1)S(1)} async-done(((bf16[32,80,256]{2,1,0:T(8,128)(2,1)}), bf16[32,80,256]{2,1,0:T(8,128)(2,1)S(1)}, u32[]{:S(2)}, u32[]{:S(2)}) %all-to-all-start.1) | async-done | bytes 1310752 | tf_op jit(solution)/shard_map/while/body/eval_jaxpr/cond/branch_1_fun/all_to_all | solution.py:153
  439.8 4.7 %branch_1_fun.7 = bf16[64,256]{1,0:T(8,128)(2,1)} custom-call(bf16[64,256]{1,0:T(8,128)(2,1)S(1)} %copy.85.refs_0_, bf16[32,80,256]{2,1,0:T(8,128)(2,1)S(1)} %all-to-all-done.1.refs_1_, s32[64,1]{1,0:T(8,128)S(1)} %copy.57.refs_1_.refs_2_, f32[64,1]{1,0:T(8,128)S(1)} %copy.58.refs_3_, bf16[8192,256]{1,0:T(8,128)(2,1)} %get-tuple-element.340.refs_4_, ...), custom_call_target="tpu_custom_call" | custom-call | tf_op jit(solution)/shard_map/while/body/eval_jaxpr/cond/branch_1_fun/pallas_call | solution.py:154
  (81 shorter events, 36.1 us)
Async XLA Ops:
  3.2 20.4 %all-to-all-start.2 = ((bf16[32,8,256]{2,1,0:T(8,128)(2,1)}), bf16[32,8,256]{2,1,0:T(8,128)(2,1)S(1)}, u32[]{:S(2)}, u32[]{:S(2)}) async-start(bf16[32,8,256]{2,1,0:T(8,128)(2,1)} %copy.59), calls=%async_computation.2 | async-start | bytes 262144 | tf_op jit(solution)/shard_map/all_to_all | solution.py:113
  23.5 4.9 %copy-start.1 = (f32[1,8192]{1,0:T(1,128)S(1)}, f32[1,8192]{1,0:T(1,128)}, u32[]{:S(2)}) copy-start(f32[1,8192]{1,0:T(1,128)} %param.16) | copy-start | bytes 98308
  23.5 53.6 %all-to-all-start.3 = ((bf16[32,128,256]{2,1,0:T(8,128)(2,1)}), bf16[32,128,256]{2,1,0:T(8,128)(2,1)S(1)}, u32[]{:S(2)}, u32[]{:S(2)}) async-start(bf16[32,128,256]{2,1,0:T(8,128)(2,1)} %bitcast.54), calls=%async_computation.3 | async-start | bytes 4194304 | tf_op jit(solution)/shard_map/all_to_all | solution.py:135
  77.1 1.3 copy-start
  81.9 4.6 %collective-permute-start = (bf16[64,256]{1,0:T(8,128)(2,1)S(1)}, bf16[64,256]{1,0:T(8,128)(2,1)}, u32[]{:S(2)}, u32[]{:S(2)}) collective-permute-start(bf16[64,256]{1,0:T(8,128)(2,1)S(1)} %get-tuple-element.661), channel_id=1, source_target_pairs={{0,32},{64,96},{128,160},{192,224},{1,33},{65,97},{129,161},{193,2... | collective-permute-start | bytes 98312 | tf_op jit(solution)/shard_map/while/body/eval_jaxpr/ppermute | solution.py:176
  86.5 2.1 collective-permute-start.1
  89.3 6.6 %collective-permute-start = (bf16[64,256]{1,0:T(8,128)(2,1)S(1)}, bf16[64,256]{1,0:T(8,128)(2,1)}, u32[]{:S(2)}, u32[]{:S(2)}) collective-permute-start(bf16[64,256]{1,0:T(8,128)(2,1)S(1)} %get-tuple-element.661), channel_id=1, source_target_pairs={{0,32},{64,96},{128,160},{192,224},{1,33},{65,97},{129,161},{193,2... | collective-permute-start | bytes 98312 | tf_op jit(solution)/shard_map/while/body/eval_jaxpr/ppermute | solution.py:176
  96.0 2.1 collective-permute-start.1
  98.8 6.6 %collective-permute-start = (bf16[64,256]{1,0:T(8,128)(2,1)S(1)}, bf16[64,256]{1,0:T(8,128)(2,1)}, u32[]{:S(2)}, u32[]{:S(2)}) collective-permute-start(bf16[64,256]{1,0:T(8,128)(2,1)S(1)} %get-tuple-element.661), channel_id=1, source_target_pairs={{0,32},{64,96},{128,160},{192,224},{1,33},{65,97},{129,161},{193,2... | collective-permute-start | bytes 98312 | tf_op jit(solution)/shard_map/while/body/eval_jaxpr/ppermute | solution.py:176
  105.5 2.1 collective-permute-start.1
  108.3 254.4 %collective-permute-start = (bf16[64,256]{1,0:T(8,128)(2,1)S(1)}, bf16[64,256]{1,0:T(8,128)(2,1)}, u32[]{:S(2)}, u32[]{:S(2)}) collective-permute-start(bf16[64,256]{1,0:T(8,128)(2,1)S(1)} %get-tuple-element.661), channel_id=1, source_target_pairs={{0,32},{64,96},{128,160},{192,224},{1,33},{65,97},{129,161},{193,2... | collective-permute-start | bytes 98312 | tf_op jit(solution)/shard_map/while/body/eval_jaxpr/ppermute | solution.py:176
  365.5 28.5 %all-to-all-start.1 = ((bf16[32,80,256]{2,1,0:T(8,128)(2,1)}), bf16[32,80,256]{2,1,0:T(8,128)(2,1)S(1)}, u32[]{:S(2)}, u32[]{:S(2)}) async-start(bf16[32,80,256]{2,1,0:T(8,128)(2,1)} %branch_1_fun.6), calls=%async_computation.1 | async-start | bytes 2621440 | tf_op jit(solution)/shard_map/while/body/eval_jaxpr/cond/branch_1_fun/all_to_all | solution.py:153
  398.8 2.1 collective-permute-start.1
  401.6 10.1 %collective-permute-start = (bf16[64,256]{1,0:T(8,128)(2,1)S(1)}, bf16[64,256]{1,0:T(8,128)(2,1)}, u32[]{:S(2)}, u32[]{:S(2)}) collective-permute-start(bf16[64,256]{1,0:T(8,128)(2,1)S(1)} %get-tuple-element.661), channel_id=1, source_target_pairs={{0,32},{64,96},{128,160},{192,224},{1,33},{65,97},{129,161},{193,2... | collective-permute-start | bytes 98312 | tf_op jit(solution)/shard_map/while/body/eval_jaxpr/ppermute | solution.py:176
  414.5 25.4 %all-to-all-start.1 = ((bf16[32,80,256]{2,1,0:T(8,128)(2,1)}), bf16[32,80,256]{2,1,0:T(8,128)(2,1)S(1)}, u32[]{:S(2)}, u32[]{:S(2)}) async-start(bf16[32,80,256]{2,1,0:T(8,128)(2,1)} %branch_1_fun.6), calls=%async_computation.1 | async-start | bytes 2621440 | tf_op jit(solution)/shard_map/while/body/eval_jaxpr/cond/branch_1_fun/all_to_all | solution.py:153
  444.6 2.1 collective-permute-start.1

commit v2 on v1

v2 whole, which is shorter than its diff:
```python
import jax
import jax.numpy as jnp
from jax import lax
from jax.experimental import pallas as pl
from jax.experimental.pallas import tpu as pltpu
from jax.sharding import PartitionSpec as P

GROUP = 4


def lane_group(shape, rank_most):
    return lax.broadcasted_iota(jnp.int32, shape, len(shape) - 1) // rank_most


def spread(value, rank_most):
    step = rank_most
    while step < value.shape[-1]:
        value = value + pltpu.roll(value, step, 1)
        step *= 2
    return value


def before_kernel(rank_most, h_ref, ids_ref, shrink_ref, out_ref):
    rows, cols = h_ref.shape
    packed = rows // GROUP
    h = h_ref[...]
    groups = lane_group((rows, cols), rank_most)
    wanted = ids_ref[...] - groups
    total = jnp.zeros((rows, cols), jnp.float32)
    for j in range(shrink_ref.shape[0] // cols):
        part = lax.dot_general(
            h,
            shrink_ref[j * cols : (j + 1) * cols, :],
            (((1,), (1,)), ((), ())),
            preferred_element_type=jnp.float32,
        )
        total = total + jnp.where(wanted == j * GROUP, part, 0.0)
    total = spread(total, rank_most)
    folded = jnp.zeros((packed, cols), jnp.float32)
    for g in range(GROUP):
        mine = groups[:packed] == g
        folded = jnp.where(mine, total[g * packed : (g + 1) * packed], folded)
    folded = folded.astype(jnp.bfloat16)
    for d in range(out_ref.shape[0]):
        out_ref[d, :rows, :] = h
        out_ref[d, rows:, :] = folded


def finish(rank_most, h_ref, base, low, ids_ref, expand_ref, out_ref):
    rows, cols = h_ref.shape
    wanted = ids_ref[...] - lane_group((rows, cols), rank_most)
    added = jnp.zeros((rows, cols), jnp.float32)
    for j in range(expand_ref.shape[0] // cols):
        picked = jnp.where(wanted == j * GROUP, low, 0.0).astype(jnp.bfloat16)
        added = added + jnp.dot(
            picked, expand_ref[j * cols : (j + 1) * cols, :], preferred_element_type=jnp.float32
        )
    update = (base + added).astype(jnp.bfloat16)
    out_ref[...] = (h_ref[...].astype(jnp.float32) + update.astype(jnp.float32)).astype(
        jnp.bfloat16
    )


def unpacked(rank_most, partial, cols):
    groups = lane_group(partial.shape, rank_most)
    return jnp.concatenate(
        [spread(jnp.where(groups == g, partial, 0.0), rank_most) for g in range(GROUP)], axis=0
    )


def after_kernel(rank_most, h_ref, got_ref, ids_ref, rank_ref, base_ref, expand_ref, out_ref):
    rows, cols = h_ref.shape
    packed = rows // GROUP
    sources = got_ref.shape[0]
    base = jnp.zeros((rows, cols), jnp.float32)
    squares = jnp.zeros((rows, cols), jnp.float32)
    partial = jnp.zeros((packed, cols), jnp.float32)
    for j in range(sources):
        block = got_ref[j, :rows, :]
        base = base + jnp.dot(
            block, base_ref[j * cols : (j + 1) * cols, :], preferred_element_type=jnp.float32
        )
        wide = block.astype(jnp.float32)
        squares = squares + wide * wide
        partial = partial + got_ref[j, rows:, :].astype(jnp.float32)
    mean_square = jnp.sum(squares, axis=-1, keepdims=True) / (sources * cols)
    inverse = lax.rsqrt(mean_square + 1e-05)
    low = unpacked(rank_most, partial, cols)
    rank = rank_ref[...]
    place = lax.broadcasted_iota(jnp.int32, (rows, cols), 1) % rank_most
    factor = jnp.where(place.astype(jnp.float32) < rank, 32.0 / rank, 0.0)
    finish(rank_most, h_ref, base * inverse, low * inverse * factor, ids_ref, expand_ref, out_ref)


def first_after_kernel(rank_most, h_ref, got_ref, ids_ref, base_ref, expand_ref, out_ref):
    partial = jnp.zeros(got_ref.shape[1:], jnp.float32)
    for j in range(got_ref.shape[0]):
        partial = partial + got_ref[j].astype(jnp.float32)
    low = unpacked(rank_most, partial, h_ref.shape[1])
    finish(rank_most, h_ref, base_ref[...], low, ids_ref, expand_ref, out_ref)


def in_vmem(count):
    return [pl.BlockSpec(memory_space=pltpu.VMEM)] * count


def on_device(tokens, adapter_ids, ranks, gain, base_weight, shrink_weight, expand_weight):
    micro_count, own_rows, model_width = tokens.shape
    cols = base_weight.shape[2]
    ad_count, _, rank_most = shrink_weight.shape[1:]
    total_adapters = expand_weight.shape[1]
    devices = lax.axis_size("adapter")
    segments = lax.axis_size("segment")
    segment = lax.axis_index("segment")
    owner = lax.axis_index("adapter")
    rows = own_rows * devices
    packed = rows // GROUP
    count = micro_count * own_rows
    params = pltpu.CompilerParams(vmem_limit_bytes=40 * 1024 * 1024)
    gain_row = gain[0]
    expand = expand_weight[0].reshape(total_adapters * rank_most, cols)

    def call(kernel, shape, *operands):
        return pl.pallas_call(
            lambda *refs: kernel(rank_most, *refs),
            out_shape=jax.ShapeDtypeStruct(shape, jnp.bfloat16),
            in_specs=in_vmem(len(operands)),
            out_specs=in_vmem(1)[0],
            compiler_params=params,
        )(*operands)

    def exchange(blocks):
        return lax.all_to_all(blocks, "adapter", 0, 0, tiled=True)

    def tables(small):
        ids = small[:, :count].reshape(devices, micro_count, own_rows).transpose(1, 0, 2)
        ids = ids.reshape(micro_count, rows).astype(jnp.int32)
        all_ranks = small[:, count : count + ad_count].reshape(-1).astype(jnp.float32)
        onehot = ids[:, :, None] == jnp.arange(total_adapters, dtype=jnp.int32)
        row_ranks = jnp.sum(jnp.where(onehot, all_ranks, 0.0), axis=-1, keepdims=True)
        return ids[:, :, None], row_ranks

    def first_layer(hidden, ids, rank):
        wide = hidden.astype(jnp.float32)
        mean_square = jnp.mean(wide * wide, axis=-1, keepdims=True)
        normed = (wide * lax.rsqrt(mean_square + 1e-05) * gain_row).astype(jnp.bfloat16)
        maps = shrink_weight[0].transpose(0, 2, 1).reshape(ad_count * rank_most, model_width)
        shrunk = lax.dot_general(
            normed, maps, (((1,), (1,)), ((), ())), preferred_element_type=jnp.float32
        ).reshape(rows, ad_count, rank_most)
        mine = (ids - owner * ad_count == jnp.arange(ad_count)).astype(jnp.float32)
        keep = jnp.arange(rank_most, dtype=jnp.float32)[None, :] < rank
        low = jnp.sum(shrunk * mine[:, :, None], axis=1) * jnp.where(keep, 32.0 / rank, 0.0)
        low = low.astype(jnp.bfloat16).reshape(GROUP, packed, rank_most)
        low = low.transpose(1, 0, 2).reshape(packed, cols)
        got = exchange(jnp.broadcast_to(low, (devices, packed, cols)))
        base = jnp.dot(normed, base_weight[0], preferred_element_type=jnp.float32)
        held = lax.dynamic_slice_in_dim(hidden, owner * cols, cols, 1)
        return call(first_after_kernel, (rows, cols), held, got, ids, base, expand)

    small = jnp.concatenate([adapter_ids.reshape(-1), ranks]).astype(jnp.bfloat16)

    def open_first():
        extra = jnp.pad(small, (0, 128 - small.shape[0]))
        extra = jnp.broadcast_to(extra, (own_rows, 128))
        block = jnp.concatenate([tokens[0], extra], axis=1)
        got = exchange(jnp.broadcast_to(block, (devices,) + block.shape))
        ids, row_ranks = tables(got[:, 0, model_width:])
        hidden = got[:, :, :model_width].reshape(rows, model_width)
        h = first_layer(hidden, ids[0], row_ranks[0])
        shrink = jnp.zeros((total_adapters * rank_most, cols), jnp.bfloat16)
        base = jnp.zeros((model_width, cols), jnp.bfloat16)
        return h, ids, row_ranks, shrink, base

    def open_other():
        maps = shrink_weight[0].reshape(ad_count, devices, cols, rank_most).transpose(1, 0, 3, 2)
        maps = maps.reshape(devices, ad_count * rank_most, cols)
        extra = jnp.broadcast_to(jnp.pad(small, (0, cols - small.shape[0])), (devices, 16, cols))
        got = exchange(jnp.concatenate([maps, extra], axis=1))
        ids, row_ranks = tables(got[:, ad_count * rank_most])
        shrink = got[:, : ad_count * rank_most].reshape(total_adapters * rank_most, cols)
        own_gain = lax.dynamic_slice_in_dim(gain_row, owner * cols, cols, 0)
        shrink = (shrink.astype(jnp.float32) * own_gain[None, :]).astype(jnp.bfloat16)
        base = (base_weight[0].astype(jnp.float32) * gain_row[:, None]).astype(jnp.bfloat16)
        h = jnp.zeros((rows, cols), jnp.bfloat16)
        return h, ids, row_ranks, shrink, base

    def work(h, ids, rank, shrink, base):
        sent = call(before_kernel, (devices, rows + packed, cols), h, ids, shrink)
        return call(after_kernel, (rows, cols), h, exchange(sent), ids, rank, base, expand)

    def next_first(h, ids, rank, shrink, base):
        block = tokens[1]
        got = exchange(jnp.broadcast_to(block, (devices,) + block.shape))
        return first_layer(got.reshape(rows, model_width), ids, rank)

    def idle(h, ids, rank, shrink, base):
        return jnp.zeros((rows, cols), jnp.bfloat16)

    h, ids, row_ranks, shrink, base = lax.cond(segment == 0, open_first, open_other)
    outs = [h, h]
    for stage in range(1, segments + 1):
        pairs = [(s, s + 1) for s in (stage - 1, stage - 2) if 0 <= s < segments - 1]
        h = lax.ppermute(h, "segment", pairs)
        leads, trails = segment == stage, segment == stage - 1
        operands = (
            h,
            jnp.where(leads, ids[0], ids[1]),
            jnp.where(leads, row_ranks[0], row_ranks[1]),
            shrink,
            base,
        )
        if stage == 1:
            branch = jnp.where(trails, 2, jnp.where(leads, 1, 0))
            h = lax.switch(branch, (idle, work, next_first), *operands)
        else:
            h = lax.cond(leads | trails, work, idle, *operands)
        outs = [jnp.where(leads, h, outs[0]), jnp.where(trails, h, outs[1])]
    return jnp.stack(outs)[None]


def solution(mesh):
    in_specs = (
        P(None, "adapter", None),
        P(None, "adapter", None),
        P("adapter"),
        P("segment", None),
        P("segment", None, "adapter"),
        P("segment", "adapter", None, None),
        P("segment", None, None, "adapter"),
    )
    out_specs = P("segment", None, None, "adapter")
    return jax.shard_map(
        on_device, mesh=mesh, in_specs=in_specs, out_specs=out_specs, check_vma=False
    )
```

time: 449 us -> 400 us (0.89)
  waiting for transfers between devices: 359 us -> 324 us
  other arithmetic: 25.7 us -> 13 us
  starting transfers between devices: 36.4 us -> 30 us
  local copies, waits for them, and re-layouts: 11.5 us -> 16.4 us
    ppermute x10 -> x8, waiting for transfers between devices: 269 us -> 238 us  [on_device(): h = lax.ppermute(h, 'segment', pairs)]
    select_n x15 -> x6, other arithmetic: 17.8 us -> 2.08 us  [the longest x3 2.06 us: on_device(): jnp.where(leads, row_ranks[0], row_ranks[1])]
    another operation x4 -> x29, local copies, waits for them, and re-layouts: 0.38 us -> 11.8 us
    all_to_all x4 -> x3, waiting for transfers between devices: 90.5 us -> 85.9 us  [exchange(): return lax.all_to_all(blocks, 'adapter', 0, 0, tiled=True)]
    all_to_all x4 -> x3, starting transfers between devices: 26.7 us -> 23.5 us  [exchange(): return lax.all_to_all(blocks, 'adapter', 0, 0, tiled=True)]
    ppermute x10 -> x8, starting transfers between devices: 9.66 us -> 6.48 us  [on_device(): h = lax.ppermute(h, 'segment', pairs)]
  transfers between devices with their start and end apart: 14 -> 11, of which waited for: 9 -> 5; matrix products, arithmetic and copies ran while one was open for 5% -> 2% of each run, Pallas kernels for 0% -> 0%
where the time goes in v2:
time: 400 us; the launch traced here: 399 us
  waiting for transfers between devices  324 us (81%)
  starting transfers between devices  30 us (8%)
  local copies, waits for them, and re-layouts  16.4 us (4%)
  Pallas kernels  15.2 us (4%)
  other arithmetic  13 us (3%)
    ppermute x8, waiting for transfers between devices, on_device(): h = lax.ppermute(h, 'segment', pairs)  238 us
    all_to_all x3, waiting for transfers between devices, exchange(): return lax.all_to_all(blocks, 'adapter', 0, 0, tiled=True)  85.9 us
    all_to_all x3, starting transfers between devices, exchange(): return lax.all_to_all(blocks, 'adapter', 0, 0, tiled=True)  23.5 us
    pallas_call x4, Pallas kernels, call(): pl.pallas_call(lambda *refs: kernel(rank_most, *refs), out_shape=jax.Shap...  15.2 us
    another operation x29, local copies, waits for them, and re-layouts  11.8 us
  transfers between devices with their start and end apart: 11, of which 5 were waited for; matrix products, arithmetic and copies ran while one was open for 2% of the time, Pallas kernels for 0%

profile of v2, /device:TPU:7, one launch (start us, length us, event | category | flops | bytes accessed | tf_op | source)
XLA Modules:
  0.0 399.0 jit_solution(8038490148129789968)
XLA Ops:
  1.5 79.2 %conditional.10 = (bf16[64,256]{1,0:T(8,128)(2,1)S(1)}, bf16[2,64,1]{1,0,2:T(2,128)(2,1)}, f32[2,64,1]{1,0,2:T(2,128)}, bf16[4096,256]{1,0:T(8,128)(2,1)}, bf16[...) conditional(s32[]{:T(128)} %convert_element_type.141, ...), branch_computations={%region_0.2_spmd, %region_2.6_spmd} | conditional | flops 406460288 | bytes 48931136
  1.5 4.8 %copy.246 = bf16[1,2,8192,64]{3,2,1,0:T(8,128)(2,1)} copy(bf16[1,2,8192,64]{2,3,1,0:T(8,128)(2,1)} %get-tuple-element.762) | data formatting | bytes 4194304 | tf_op jit(solution)/shard_map
  6.3 3.5 copy.232
  9.9 1.6 pad_maximum_fusion
  11.5 11.3 %all-to-all-start.8 = ((bf16[32,144,256]{2,1,0:T(8,128)(2,1)}), bf16[32,144,256]{2,1,0:T(8,128)(2,1)S(1)}, u32[]{:S(2)}, u32[]{:S(2)}) async-start(bf16[32,144,256]{2,1,0:T(8,128)(2,1)} %pad_maximum_fusion), calls=%async_computation.8 | async-start | bytes 4718592 | tf_op jit(solution)/shard_map/cond/branch_0_fun/all_to_all | solution.py:133
  22.9 4.2 %fusion = bf16[8192,256]{1,0:T(8,128)(2,1)} fusion(bf16[1,8192,256]{2,1,0:T(8,128)(2,1)} %get-tuple-element.264, f32[8192]{0:T(1024)S(1)} %bitcast.107), kind=kLoop, calls=%fused_computation.1 | loop fusion | flops 6291456 | bytes 8421376 | tf_op jit(solution)/shard_map/cond/branch_0_fun/convert_element_type | solution.py:184
  27.1 50.2 %all-to-all-done.8 = bf16[32,144,256]{2,1,0:T(8,128)(2,1)S(1)} async-done(((bf16[32,144,256]{2,1,0:T(8,128)(2,1)}), bf16[32,144,256]{2,1,0:T(8,128)(2,1)S(1)}, u32[]{:S(2)}, u32[]{:S(2)}) %all-to-all-start.8) | async-done | bytes 2359328 | tf_op jit(solution)/shard_map/cond/branch_0_fun/all_to_all | solution.py:133
  78.7 1.9 fusion.1
  89.0 1.3 collective-permute-start.6
  90.3 221.8 %collective-permute-done.6 = bf16[64,256]{1,0:T(8,128)(2,1)S(1)} collective-permute-done((bf16[64,256]{1,0:T(8,128)(2,1)}, bf16[64,256]{1,0:T(8,128)(2,1)S(1)}, u32[]{:S(2)}, u32[]{:S(2)}) %collective-permute-start.6) | collective-permute-done | bytes 32800 | tf_op jit(solution)/shard_map/ppermute | solution.py:204
  312.1 33.2 %conditional.33 = (bf16[64,256]{1,0:T(8,128)(2,1)}) conditional(s32[]{:T(128)} %convert_element_type.142, () %tuple.81, (pred[]{:T(512)}, s32[64,1]{0,1:T(1,128)S(1)}, s32[64,1]{0,1:T(1,128)S(1)}, bf16[64,256]{1,0:T(8,128)(2,1)S(1)}, bf16[4096,256]{1,0:T(8,128)(2,1)}, /*index=5*/f32[64,1]{0,1:T(1,128)S(1)}, f32[64,1]{0,1:T(1,128)S(1)}, ...), branch_computations={%region_21.22_spmd, %region_22.23_spmd} | conditional | flops 128 | bytes 12324422 | solution.py:217
  312.3 3.5 branch_1_fun.30
  315.9 5.4 %all-to-all-start.6 = ((bf16[32,80,256]{2,1,0:T(8,128)(2,1)}), bf16[32,80,256]{2,1,0:T(8,128)(2,1)S(1)}, u32[]{:S(2)}, u32[]{:S(2)}) async-start(bf16[32,80,256]{2,1,0:T(8,128)(2,1)} %branch_1_fun.30), calls=%async_computation.6 | async-start | bytes 2621440 | tf_op jit(solution)/shard_map/cond/branch_1_fun/all_to_all | solution.py:133
  322.7 0.8 broadcast_select_fusion.10.refs_3_
  323.4 17.8 %all-to-all-done.6.refs_1_ = bf16[32,80,256]{2,1,0:T(8,128)(2,1)S(1)} async-done(((bf16[32,80,256]{2,1,0:T(8,128)(2,1)}), bf16[32,80,256]{2,1,0:T(8,128)(2,1)S(1)}, u32[]{:S(2)}, u32[]{:S(2)}) %all-to-all-start.6) | async-done | bytes 1310752 | tf_op jit(solution)/shard_map/cond/branch_1_fun/all_to_all | solution.py:133
  341.3 4.1 %branch_1_fun.31 = bf16[64,256]{1,0:T(8,128)(2,1)} custom-call(bf16[64,256]{1,0:T(8,128)(2,1)S(1)} %get-tuple-element.332.refs_0_, bf16[32,80,256]{2,1,0:T(8,128)(2,1)S(1)} %all-to-all-done.6.refs_1_, s32[64,1]{1,0:T(8,128)S(1)} %broadcast_select_fusion.11.refs_1_.refs_2_, f32[64,1]{1,0:T(8,128)S(1)} %broadcast_select_fusion.10.refs_3_, ...), custom_call_target="tpu_custom_call" | custom-call | tf_op jit(solution)/shard_map/cond/branch_1_fun/pallas_call | solution.py:124
  345.3 1.3 collective-permute-start.7
  346.6 16.3 %collective-permute-done.7 = bf16[64,256]{1,0:T(8,128)(2,1)S(1)} collective-permute-done((bf16[64,256]{1,0:T(8,128)(2,1)}, bf16[64,256]{1,0:T(8,128)(2,1)S(1)}, u32[]{:S(2)}, u32[]{:S(2)}) %collective-permute-start.7) | collective-permute-done | bytes 32800 | tf_op jit(solution)/shard_map/ppermute | solution.py:204
  362.9 34.5 %conditional.34 = (bf16[64,256]{1,0:T(8,128)(2,1)}) conditional(s32[]{:T(128)} %convert_element_type.140, () %tuple.78, (pred[]{:T(512)}, s32[64,1]{0,1:T(1,128)S(1)}, s32[64,1]{0,1:T(1,128)S(1)}, bf16[64,256]{1,0:T(8,128)(2,1)S(1)}, bf16[4096,256]{1,0:T(8,128)(2,1)}, /*index=5*/f32[64,1]{0,1:T(1,128)S(1)}, f32[64,1]{0,1:T(1,128)S(1)}, ...), branch_computations={%region_23.24_spmd, %region_24.25_spmd} | conditional | flops 128 | bytes 12324422 | solution.py:217
  363.1 3.5 branch_1_fun.32
  366.7 6.7 %all-to-all-start.7 = ((bf16[32,80,256]{2,1,0:T(8,128)(2,1)}), bf16[32,80,256]{2,1,0:T(8,128)(2,1)S(1)}, u32[]{:S(2)}, u32[]{:S(2)}) async-start(bf16[32,80,256]{2,1,0:T(8,128)(2,1)} %branch_1_fun.32), calls=%async_computation.7 | async-start | bytes 2621440 | tf_op jit(solution)/shard_map/cond/branch_1_fun/all_to_all | solution.py:133
  375.6 17.8 %all-to-all-done.7.refs_1_ = bf16[32,80,256]{2,1,0:T(8,128)(2,1)S(1)} async-done(((bf16[32,80,256]{2,1,0:T(8,128)(2,1)}), bf16[32,80,256]{2,1,0:T(8,128)(2,1)S(1)}, u32[]{:S(2)}, u32[]{:S(2)}) %all-to-all-start.7) | async-done | bytes 1310752 | tf_op jit(solution)/shard_map/cond/branch_1_fun/all_to_all | solution.py:133
  393.4 4.1 %branch_1_fun.33 = bf16[64,256]{1,0:T(8,128)(2,1)} custom-call(bf16[64,256]{1,0:T(8,128)(2,1)S(1)} %get-tuple-element.341.refs_0_, bf16[32,80,256]{2,1,0:T(8,128)(2,1)S(1)} %all-to-all-done.7.refs_1_, s32[64,1]{1,0:T(8,128)S(1)} %broadcast_select_fusion.13.refs_1_.refs_2_, f32[64,1]{1,0:T(8,128)S(1)} %broadcast_select_fusion.12.refs_3_, ...), custom_call_target="tpu_custom_call" | custom-call | tf_op jit(solution)/shard_map/cond/branch_1_fun/pallas_call | solution.py:124
  397.5 0.9 select_bitcast_fusion.1
  (79 shorter events, 19.3 us)
Async XLA Ops:
  11.5 11.4 %copy-start.12 = (f32[1,8192]{1,0:T(1,128)S(1)}, f32[1,8192]{1,0:T(1,128)}, u32[]{:S(2)}) copy-start(f32[1,8192]{1,0:T(1,128)} %get-tuple-element.265) | copy-start | bytes 98308 | tf_op jit(solution)/shard_map/conditional
  11.5 65.8 %all-to-all-start.8 = ((bf16[32,144,256]{2,1,0:T(8,128)(2,1)}), bf16[32,144,256]{2,1,0:T(8,128)(2,1)S(1)}, u32[]{:S(2)}, u32[]{:S(2)}) async-start(bf16[32,144,256]{2,1,0:T(8,128)(2,1)} %pad_maximum_fusion), calls=%async_computation.8 | async-start | bytes 4718592 | tf_op jit(solution)/shard_map/cond/branch_0_fun/all_to_all | solution.py:133
  78.0 0.6 copy-start.15
  78.3 0.5 copy-start.19
  78.3 2.4 copy-start.23
  78.3 2.4 copy-start.21
  80.7 1.2 collective-permute-start
  82.5 0.7 collective-permute-start.1
  83.8 0.7 collective-permute-start.2
  85.1 0.7 collective-permute-start.3
  86.4 0.7 collective-permute-start.4
  87.7 0.7 collective-permute-start.5
  89.0 223.1 %collective-permute-start.6 = (bf16[64,256]{1,0:T(8,128)(2,1)}, bf16[64,256]{1,0:T(8,128)(2,1)S(1)}, u32[]{:S(2)}, u32[]{:S(2)}) collective-permute-start(bf16[64,256]{1,0:T(8,128)(2,1)} %get-tuple-element.947), channel_id=1, source_target_pairs={{192,224},{160,192},{193,225},{161,193},{194,226},{162,194},{195,2... | collective-permute-start | bytes 98312 | tf_op jit(solution)/shard_map/ppermute | solution.py:204
  315.9 25.4 %copy-start.8 = (bf16[4096,256]{1,0:T(8,128)(2,1)S(1)}, bf16[4096,256]{1,0:T(8,128)(2,1)}, u32[]{:S(2)}) copy-start(bf16[4096,256]{1,0:T(8,128)(2,1)} %get-tuple-element.340.refs_5_) | copy-start | bytes 6291460 | tf_op jit(solution)/shard_map/cond
  315.9 25.4 %all-to-all-start.6 = ((bf16[32,80,256]{2,1,0:T(8,128)(2,1)}), bf16[32,80,256]{2,1,0:T(8,128)(2,1)S(1)}, u32[]{:S(2)}, u32[]{:S(2)}) async-start(bf16[32,80,256]{2,1,0:T(8,128)(2,1)} %branch_1_fun.30), calls=%async_computation.6 | async-start | bytes 2621440 | tf_op jit(solution)/shard_map/cond/branch_1_fun/all_to_all | solution.py:133
  345.3 17.6 %collective-permute-start.7 = (bf16[64,256]{1,0:T(8,128)(2,1)}, bf16[64,256]{1,0:T(8,128)(2,1)S(1)}, u32[]{:S(2)}, u32[]{:S(2)}) collective-permute-start(bf16[64,256]{1,0:T(8,128)(2,1)} %get-tuple-element.948), channel_id=1, source_target_pairs={{192,224},{193,225},{194,226},{195,227},{196,228},{197,229},{198,2... | collective-permute-start | bytes 98312 | tf_op jit(solution)/shard_map/ppermute | solution.py:204
  366.7 26.7 %copy-start.9 = (bf16[4096,256]{1,0:T(8,128)(2,1)S(1)}, bf16[4096,256]{1,0:T(8,128)(2,1)}, u32[]{:S(2)}) copy-start(bf16[4096,256]{1,0:T(8,128)(2,1)} %get-tuple-element.349.refs_5_) | copy-start | bytes 6291460 | tf_op jit(solution)/shard_map/cond
  366.7 26.7 %all-to-all-start.7 = ((bf16[32,80,256]{2,1,0:T(8,128)(2,1)}), bf16[32,80,256]{2,1,0:T(8,128)(2,1)S(1)}, u32[]{:S(2)}, u32[]{:S(2)}) async-start(bf16[32,80,256]{2,1,0:T(8,128)(2,1)} %branch_1_fun.32), calls=%async_computation.7 | async-start | bytes 2621440 | tf_op jit(solution)/shard_map/cond/branch_1_fun/all_to_all | solution.py:133

commit v3 on v2

--- a/solution.py
+++ b/solution.py
@@ -92,12 +92,51 @@
     finish(rank_most, h_ref, base * inverse, low * inverse * factor, ids_ref, expand_ref, out_ref)
 
 
+def first_kernel(rank_most, hidden_ref, base_ref, maps_ref, gain_ref, wanted_ref, rank_ref, base_out, sent_out):
+    rows, width = hidden_ref.shape
+    cols, held = base_ref.shape[1], maps_ref.shape[0]
+    packed = rows // GROUP
+    base = jnp.zeros((rows, cols), jnp.float32)
+    shrunk = jnp.zeros((rows, held), jnp.float32)
+    squares = jnp.zeros((rows, cols), jnp.float32)
+    for j in range(width // cols):
+        part = slice(j * cols, (j + 1) * cols)
+        wide = hidden_ref[:, part].astype(jnp.float32)
+        squares = squares + wide * wide
+        scaled = (wide * gain_ref[:, part]).astype(jnp.bfloat16)
+        base = base + jnp.dot(scaled, base_ref[part, :], preferred_element_type=jnp.float32)
+        shrunk = shrunk + lax.dot_general(
+            scaled, maps_ref[:, part], (((1,), (1,)), ((), ())), preferred_element_type=jnp.float32
+        )
+    inverse = lax.rsqrt(jnp.sum(squares, axis=-1, keepdims=True) / width + 1e-05)
+    base_out[...] = base * inverse
+    groups = lane_group((rows, held), rank_most)
+    place = lax.broadcasted_iota(jnp.int32, (rows, held), 1) % rank_most
+    rank = rank_ref[...]
+    factor = jnp.where(place.astype(jnp.float32) < rank, 32.0 / rank, 0.0)
+    low = jnp.where(wanted_ref[...] == groups, shrunk * inverse * factor, 0.0)
+    low = spread(low, rank_most)
+    low = jnp.concatenate([low] * (cols // held), axis=1)
+    groups = lane_group((packed, cols), rank_most)
+    folded = jnp.zeros((packed, cols), jnp.float32)
+    for g in range(GROUP):
+        folded = jnp.where(groups == g, low[g * packed : (g + 1) * packed], folded)
+    folded = folded.astype(jnp.bfloat16)
+    for d in range(sent_out.shape[0]):
+        sent_out[d] = folded
+
+
 def first_after_kernel(rank_most, h_ref, got_ref, ids_ref, base_ref, expand_ref, out_ref):
     partial = jnp.zeros(got_ref.shape[1:], jnp.float32)
     for j in range(got_ref.shape[0]):
         partial = partial + got_ref[j].astype(jnp.float32)
     low = unpacked(rank_most, partial, h_ref.shape[1])
     finish(rank_most, h_ref, base_ref[...], low, ids_ref, expand_ref, out_ref)
+
+
+def unused_kernel(rank_most, *refs):
+    for ref in refs:
+        ref[:16, :] = jnp.zeros((16, ref.shape[1]), ref.dtype)
 
 
 def in_vmem(count):
@@ -116,18 +155,20 @@
     rows = own_rows * devices
     packed = rows // GROUP
     count = micro_count * own_rows
-    params = pltpu.CompilerParams(vmem_limit_bytes=40 * 1024 * 1024)
+    params = pltpu.CompilerParams(vmem_limit_bytes=14 * 1024 * 1024)
     gain_row = gain[0]
     expand = expand_weight[0].reshape(total_adapters * rank_most, cols)
 
-    def call(kernel, shape, *operands):
+    def call(kernel, shapes, *operands):
         return pl.pallas_call(
             lambda *refs: kernel(rank_most, *refs),
-            out_shape=jax.ShapeDtypeStruct(shape, jnp.bfloat16),
+            out_shape=[jax.ShapeDtypeStruct(*shape) for shape in shapes],
             in_specs=in_vmem(len(operands)),
-            out_specs=in_vmem(1)[0],
+            out_specs=in_vmem(len(shapes)),
             compiler_params=params,
         )(*operands)
+
+    state = ((rows, cols), jnp.bfloat16)
 
     def exchange(blocks):
         return lax.all_to_all(blocks, "adapter", 0, 0, tiled=True)
@@ -140,39 +181,42 @@
         row_ranks = jnp.sum(jnp.where(onehot, all_ranks, 0.0), axis=-1, keepdims=True)
         return ids[:, :, None], row_ranks
 
-    def first_layer(hidden, ids, rank):
-        wide = hidden.astype(jnp.float32)
-        mean_square = jnp.mean(wide * wide, axis=-1, keepdims=True)
-        normed = (wide * lax.rsqrt(mean_square + 1e-05) * gain_row).astype(jnp.bfloat16)
+    small = jnp.concatenate([adapter_ids.reshape(-1), ranks]).astype(jnp.bfloat16)
+
+    def gather_rows(micro):
+        extra = jnp.broadcast_to(jnp.pad(small, (0, 128 - small.shape[0])), (own_rows, 128))
+        block = jnp.concatenate([tokens[micro], extra], axis=1)
+        return exchange(jnp.broadcast_to(block, (devices,) + block.shape))
+
+    def first_layer(got, ids, rank):
+        hidden = got[:, :, :model_width].reshape(rows, model_width)
         maps = shrink_weight[0].transpose(0, 2, 1).reshape(ad_count * rank_most, model_width)
-        shrunk = lax.dot_general(
-            normed, maps, (((1,), (1,)), ((), ())), preferred_element_type=jnp.float32
-        ).reshape(rows, ad_count, rank_most)
-        mine = (ids - owner * ad_count == jnp.arange(ad_count)).astype(jnp.float32)
-        keep = jnp.arange(rank_most, dtype=jnp.float32)[None, :] < rank
-        low = jnp.sum(shrunk * mine[:, :, None], axis=1) * jnp.where(keep, 32.0 / rank, 0.0)
-        low = low.astype(jnp.bfloat16).reshape(GROUP, packed, rank_most)
-        low = low.transpose(1, 0, 2).reshape(packed, cols)
-        got = exchange(jnp.broadcast_to(low, (devices, packed, cols)))
-        base = jnp.dot(normed, base_weight[0], preferred_element_type=jnp.float32)
+        base, sent = call(
+            first_kernel,
+            [((rows, cols), jnp.float32), ((devices, packed, cols), jnp.bfloat16)],
+            hidden,
+            base_weight[0],
+            maps,
+            gain,
+            ids - owner * ad_count,
+            rank,
+        )
         held = lax.dynamic_slice_in_dim(hidden, owner * cols, cols, 1)
-        return call(first_after_kernel, (rows, cols), held, got, ids, base, expand)
-
-    small = jnp.concatenate([adapter_ids.reshape(-1), ranks]).astype(jnp.bfloat16)
-
-    def open_first():
-        extra = jnp.pad(small, (0, 128 - small.shape[0]))
-        extra = jnp.broadcast_to(extra, (own_rows, 128))
-        block = jnp.concatenate([tokens[0], extra], axis=1)
-        got = exchange(jnp.broadcast_to(block, (devices,) + block.shape))
+        return call(first_after_kernel, [state], held, exchange(sent), ids, base, expand)[0]
+
+    def open_first(got):
         ids, row_ranks = tables(got[:, 0, model_width:])
-        hidden = got[:, :, :model_width].reshape(rows, model_width)
-        h = first_layer(hidden, ids[0], row_ranks[0])
-        shrink = jnp.zeros((total_adapters * rank_most, cols), jnp.bfloat16)
-        base = jnp.zeros((model_width, cols), jnp.bfloat16)
+        h = first_layer(got, ids[0], row_ranks[0])
+        shrink, base = call(
+            unused_kernel,
+            [
+                ((total_adapters * rank_most, cols), jnp.bfloat16),
+                ((model_width, cols), jnp.bfloat16),
+            ],
+        )
         return h, ids, row_ranks, shrink, base
 
-    def open_other():
+    def open_other(got):
         maps = shrink_weight[0].reshape(ad_count, devices, cols, rank_most).transpose(1, 0, 3, 2)
         maps = maps.reshape(devices, ad_count * rank_most, cols)
         extra = jnp.broadcast_to(jnp.pad(small, (0, cols - small.shape[0])), (devices, 16, cols))
@@ -185,19 +229,28 @@
         h = jnp.zeros((rows, cols), jnp.bfloat16)
         return h, ids, row_ranks, shrink, base
 
-    def work(h, ids, rank, shrink, base):
-        sent = call(before_kernel, (devices, rows + packed, cols), h, ids, shrink)
-        return call(after_kernel, (rows, cols), h, exchange(sent), ids, rank, base, expand)
-
-    def next_first(h, ids, rank, shrink, base):
-        block = tokens[1]
-        got = exchange(jnp.broadcast_to(block, (devices,) + block.shape))
-        return first_layer(got.reshape(rows, model_width), ids, rank)
-
-    def idle(h, ids, rank, shrink, base):
+    def work(h, ids, rank, shrink, base, later):
+        blocks = ((devices, rows + packed, cols), jnp.bfloat16)
+        (sent,) = call(before_kernel, [blocks], h, ids, shrink)
+        return call(after_kernel, [state], h, exchange(sent), ids, rank, base, expand)[0]
+
+    def next_first(h, ids, rank, shrink, base, later):
+        return first_layer(later, ids, rank)
+
+    def idle(h, ids, rank, shrink, base, later):
         return jnp.zeros((rows, cols), jnp.bfloat16)
 
-    h, ids, row_ranks, shrink, base = lax.cond(segment == 0, open_first, open_other)
+    got = lax.cond(
+        segment == 0,
+        lambda: gather_rows(0),
+        lambda: lax.cond(
+            segment == 2,
+            lambda: gather_rows(1),
+            lambda: jnp.zeros((devices, own_rows, model_width + 128), jnp.bfloat16),
+        ),
+    )
+    later = lax.ppermute(got, "segment", [(2, 0)])
+    h, ids, row_ranks, shrink, base = lax.cond(segment == 0, open_first, open_other, got)
     outs = [h, h]
     for stage in range(1, segments + 1):
         pairs = [(s, s + 1) for s in (stage - 1, stage - 2) if 0 <= s < segments - 1]
@@ -209,6 +262,7 @@
             jnp.where(leads, row_ranks[0], row_ranks[1]),
             shrink,
             base,
+            later,
         )
         if stage == 1:
             branch = jnp.where(trails, 2, jnp.where(leads, 1, 0))

time: 400 us -> 412 us (1.030)
  local copies, waits for them, and re-layouts: 16.4 us -> 28.4 us
    ppermute x8, waiting for transfers between devices: 238 us -> 226 us  [on_device(): h = lax.ppermute(h, 'segment', pairs)]
    all_to_all x3, waiting for transfers between devices: 85.9 us -> 95 us  [exchange(): return lax.all_to_all(blocks, 'adapter', 0, 0, tiled=True)]
    another operation x29 -> x26, local copies, waits for them, and re-layouts: 11.8 us -> 18.5 us
  transfers between devices with their start and end apart: 11 -> 12, of which waited for: 5 -> 5; matrix products, arithmetic and copies ran while one was open for 2% -> 9% of each run, Pallas kernels for 0% -> 0%
where the time goes in v3:
time: 412 us; the launch traced here: 411 us
  waiting for transfers between devices  321 us (78%)
  starting transfers between devices  29.9 us (7%)
  local copies, waits for them, and re-layouts  28.4 us (7%)
  other arithmetic  16.3 us (4%)
  Pallas kernels  15.2 us (4%)
    ppermute x8, waiting for transfers between devices, on_device(): h = lax.ppermute(h, 'segment', pairs)  226 us
    all_to_all x3, waiting for transfers between devices, exchange(): return lax.all_to_all(blocks, 'adapter', 0, 0, tiled=True)  95 us
    all_to_all x3, starting transfers between devices, exchange(): return lax.all_to_all(blocks, 'adapter', 0, 0, tiled=True)  21.7 us
    another operation x26, local copies, waits for them, and re-layouts  18.5 us
    pallas_call x4, Pallas kernels, call(): pl.pallas_call(lambda *refs: kernel(rank_most, *refs), out_shape=[jax.Sha...  15.2 us
  transfers between devices with their start and end apart: 12, of which 5 were waited for; matrix products, arithmetic and copies ran while one was open for 9% of the time, Pallas kernels for 0%

profile of v3, /device:TPU:7, one launch (start us, length us, event | category | flops | bytes accessed | tf_op | source)
XLA Modules:
  0.0 410.8 jit_solution(14545938833262516218)
XLA Ops:
  1.5 1.5 conditional.12
  1.5 1.5 conditional.1
  3.1 1.7 collective-permute-start.1
  4.7 92.5 %conditional.13 = (bf16[64,256]{1,0:T(8,128)(2,1)}, bf16[2,64,1]{1,0,2:T(2,128)(2,1)}, f32[2,64,1]{1,0,2:T(2,128)}, bf16[4096,256]{1,0:T(8,128)(2,1)}, bf16[8192...) conditional(s32[]{:T(128)} %convert_element_type.98, ...), branch_computations={%region_4.6_spmd, %region_6.8_spmd} | conditional | flops 14180548 | bytes 37375364
  4.7 4.8 %copy.252 = bf16[1,2,8192,64]{3,2,1,0:T(8,128)(2,1)} copy(bf16[1,2,8192,64]{2,3,1,0:T(8,128)(2,1)} %get-tuple-element.758) | data formatting | bytes 4194304 | tf_op jit(solution)/shard_map
  9.6 4.8 %copy.238 = bf16[2,32,256,64]{2,3,0,1:T(8,128)(2,1)} copy(bf16[2,32,256,64]{3,2,1,0:T(8,128)(2,1)} %bitcast.83) | data formatting | bytes 4194304 | tf_op jit(solution)/shard_map/cond/branch_0_fun/reshape;cond/branch_0_fun/squeeze | solution.py:220
  14.4 3.2 pad_maximum_fusion.2
  17.6 11.3 %all-to-all-start.11 = ((bf16[32,144,256]{2,1,0:T(8,128)(2,1)}), bf16[32,144,256]{2,1,0:T(8,128)(2,1)}, u32[]{:S(2)}, u32[]{:S(2)}) async-start(bf16[32,144,256]{2,1,0:T(8,128)(2,1)} %pad_maximum_fusion.2), calls=%async_computation.11 | async-start | bytes 4718592 | tf_op jit(solution)/shard_map/cond/branch_0_fun/all_to_all | solution.py:174
  29.0 4.2 %fusion.2 = bf16[8192,256]{1,0:T(8,128)(2,1)} fusion(bf16[1,8192,256]{2,1,0:T(8,128)(2,1)} %get-tuple-element.289, f32[8192]{0:T(1024)S(1)} %bitcast.85), kind=kLoop, calls=%fused_computation.9 | loop fusion | flops 6291456 | bytes 8421376 | tf_op jit(solution)/shard_map/cond/branch_0_fun/convert_element_type | solution.py:228
  33.2 50.2 %all-to-all-done.11 = bf16[32,144,256]{2,1,0:T(8,128)(2,1)} async-done(((bf16[32,144,256]{2,1,0:T(8,128)(2,1)}), bf16[32,144,256]{2,1,0:T(8,128)(2,1)}, u32[]{:S(2)}, u32[]{:S(2)}) %all-to-all-start.11) | async-done | bytes 2359328 | tf_op jit(solution)/shard_map/cond/branch_0_fun/all_to_all | solution.py:174
  91.7 1.7 slice.111
  93.4 1.9 fusion.3
  107.3 218.9 %collective-permute-done.7 = bf16[64,256]{1,0:T(8,128)(2,1)S(1)} collective-permute-done((bf16[64,256]{1,0:T(8,128)(2,1)}, bf16[64,256]{1,0:T(8,128)(2,1)S(1)}, u32[]{:S(2)}, u32[]{:S(2)}) %collective-permute-start.7) | collective-permute-done | bytes 32800 | tf_op jit(solution)/shard_map/ppermute | solution.py:257
  326.2 42.2 %conditional.36 = (bf16[64,256]{1,0:T(8,128)(2,1)}) conditional(s32[]{:T(128)} %convert_element_type.99, () %tuple.95, (pred[]{:T(512)}, s32[64,1]{0,1:T(1,128)S(1)}, s32[64,1]{0,1:T(1,128)S(1)}, bf16[64,256]{1,0:T(8,128)(2,1)S(1)}, bf16[4096,256]{1,0:T(8,128)(2,1)}, /*index=5*/f32[64,1]{0,1:T(1,128)S(1)}, f32[64,1]{0,1:T(1,128)S(1)}, ...), branch_computations={%region_21.22_spmd, %region_22.23_spmd} | conditional | flops 128 | bytes 3935786 | solution.py:271
  326.4 3.5 branch_1_fun.34
  329.9 5.3 %all-to-all-start.9 = ((bf16[32,80,256]{2,1,0:T(8,128)(2,1)}), bf16[32,80,256]{2,1,0:T(8,128)(2,1)S(1)}, u32[]{:S(2)}, u32[]{:S(2)}) async-start(bf16[32,80,256]{2,1,0:T(8,128)(2,1)} %branch_1_fun.34), calls=%async_computation.9 | async-start | bytes 2621440 | tf_op jit(solution)/shard_map/cond/branch_1_fun/all_to_all | solution.py:174
  337.4 27.0 %all-to-all-done.9.refs_1_ = bf16[32,80,256]{2,1,0:T(8,128)(2,1)S(1)} async-done(((bf16[32,80,256]{2,1,0:T(8,128)(2,1)}), bf16[32,80,256]{2,1,0:T(8,128)(2,1)S(1)}, u32[]{:S(2)}, u32[]{:S(2)}) %all-to-all-start.9) | async-done | bytes 1310752 | tf_op jit(solution)/shard_map/cond/branch_1_fun/all_to_all | solution.py:174
  364.4 4.1 branch_1_fun.35
  369.7 6.6 %collective-permute-done.8 = bf16[64,256]{1,0:T(8,128)(2,1)S(1)} collective-permute-done((bf16[64,256]{1,0:T(8,128)(2,1)}, bf16[64,256]{1,0:T(8,128)(2,1)S(1)}, u32[]{:S(2)}, u32[]{:S(2)}) %collective-permute-start.8) | collective-permute-done | bytes 32800 | tf_op jit(solution)/shard_map/ppermute | solution.py:257
  376.4 32.9 %conditional.37 = (bf16[64,256]{1,0:T(8,128)(2,1)}) conditional(s32[]{:T(128)} %convert_element_type.97, () %tuple.90, (pred[]{:T(512)}, s32[64,1]{0,1:T(1,128)S(1)}, s32[64,1]{0,1:T(1,128)S(1)}, bf16[64,256]{1,0:T(8,128)(2,1)S(1)}, bf16[4096,256]{1,0:T(8,128)(2,1)}, /*index=5*/f32[64,1]{0,1:T(1,128)S(1)}, f32[64,1]{0,1:T(1,128)S(1)}, ...), branch_computations={%region_23.24_spmd, %region_24.25_spmd} | conditional | flops 128 | bytes 3935786 | solution.py:271
  376.6 3.5 branch_1_fun.36
  380.1 5.1 %all-to-all-start.10 = ((bf16[32,80,256]{2,1,0:T(8,128)(2,1)}), bf16[32,80,256]{2,1,0:T(8,128)(2,1)S(1)}, u32[]{:S(2)}, u32[]{:S(2)}) async-start(bf16[32,80,256]{2,1,0:T(8,128)(2,1)} %branch_1_fun.36), calls=%async_computation.10 | async-start | bytes 2621440 | tf_op jit(solution)/shard_map/cond/branch_1_fun/all_to_all | solution.py:174
  387.4 17.8 %all-to-all-done.10.refs_1_ = bf16[32,80,256]{2,1,0:T(8,128)(2,1)S(1)} async-done(((bf16[32,80,256]{2,1,0:T(8,128)(2,1)}), bf16[32,80,256]{2,1,0:T(8,128)(2,1)S(1)}, u32[]{:S(2)}, u32[]{:S(2)}) %all-to-all-start.10) | async-done | bytes 1310752 | tf_op jit(solution)/shard_map/cond/branch_1_fun/all_to_all | solution.py:174
  405.2 4.1 branch_1_fun.37
  (80 shorter events, 33.7 us)
Async XLA Ops:
  1.5 3.2 copy-start
  1.5 3.2 copy-start.1
  3.1 96.4 %collective-permute-start.1 = (bf16[32,2,8320]{2,1,0:T(2,128)(2,1)}, bf16[32,2,8320]{2,1,0:T(2,128)(2,1)}, u32[]{:S(2)}, u32[]{:S(2)}) collective-permute-start(bf16[32,2,8320]{2,1,0:T(2,128)(2,1)} %get-tuple-element.954), channel_id=1, source_target_pairs={{64,0},{65,1},{66,2},{67,3},{68,4},{69,5},{70,6},{71,7},{72,8},{73... | collective-permute-start | bytes 3194888 | tf_op jit(solution)/shard_map/ppermute | solution.py:252
  17.6 65.7 %all-to-all-start.11 = ((bf16[32,144,256]{2,1,0:T(8,128)(2,1)}), bf16[32,144,256]{2,1,0:T(8,128)(2,1)}, u32[]{:S(2)}, u32[]{:S(2)}) async-start(bf16[32,144,256]{2,1,0:T(8,128)(2,1)} %pad_maximum_fusion.2), calls=%async_computation.11 | async-start | bytes 4718592 | tf_op jit(solution)/shard_map/cond/branch_0_fun/all_to_all | solution.py:174
  85.0 8.4 %copy-start.7 = (f32[2,64]{1,0:T(2,128)}, f32[2,64]{1,0:T(2,128)S(1)}, u32[]{:S(2)}) copy-start(f32[2,64]{1,0:T(2,128)S(1)} %select_reduce_fusion) | copy-start | bytes 1540 | tf_op jit(solution)/shard_map/conditional
  97.2 2.2 collective-permute-start
  100.1 0.7 collective-permute-start.2
  100.8 0.7 collective-permute-start.3
  102.1 0.7 collective-permute-start.4
  103.4 0.7 collective-permute-start.5
  104.7 0.7 collective-permute-start.6
  106.0 220.2 %collective-permute-start.7 = (bf16[64,256]{1,0:T(8,128)(2,1)}, bf16[64,256]{1,0:T(8,128)(2,1)S(1)}, u32[]{:S(2)}, u32[]{:S(2)}) collective-permute-start(bf16[64,256]{1,0:T(8,128)(2,1)} %get-tuple-element.960), channel_id=1, source_target_pairs={{192,224},{160,192},{193,225},{161,193},{194,226},{162,194},{195,2... | collective-permute-start | bytes 98312 | tf_op jit(solution)/shard_map/ppermute | solution.py:257
  329.9 34.4 %all-to-all-start.9 = ((bf16[32,80,256]{2,1,0:T(8,128)(2,1)}), bf16[32,80,256]{2,1,0:T(8,128)(2,1)S(1)}, u32[]{:S(2)}, u32[]{:S(2)}) async-start(bf16[32,80,256]{2,1,0:T(8,128)(2,1)} %branch_1_fun.34), calls=%async_computation.9 | async-start | bytes 2621440 | tf_op jit(solution)/shard_map/cond/branch_1_fun/all_to_all | solution.py:174
  368.4 7.9 %collective-permute-start.8 = (bf16[64,256]{1,0:T(8,128)(2,1)}, bf16[64,256]{1,0:T(8,128)(2,1)S(1)}, u32[]{:S(2)}, u32[]{:S(2)}) collective-permute-start(bf16[64,256]{1,0:T(8,128)(2,1)} %get-tuple-element.961), channel_id=1, source_target_pairs={{192,224},{193,225},{194,226},{195,227},{196,228},{197,229},{198,2... | collective-permute-start | bytes 98312 | tf_op jit(solution)/shard_map/ppermute | solution.py:257
  380.1 25.1 %all-to-all-start.10 = ((bf16[32,80,256]{2,1,0:T(8,128)(2,1)}), bf16[32,80,256]{2,1,0:T(8,128)(2,1)S(1)}, u32[]{:S(2)}, u32[]{:S(2)}) async-start(bf16[32,80,256]{2,1,0:T(8,128)(2,1)} %branch_1_fun.36), calls=%async_computation.10 | async-start | bytes 2621440 | tf_op jit(solution)/shard_map/cond/branch_1_fun/all_to_all | solution.py:174

commit v4 on v2

v4 whole, which is shorter than its diff:
```python
import jax
import jax.numpy as jnp
from jax import lax
from jax.experimental import pallas as pl
from jax.experimental.pallas import tpu as pltpu
from jax.sharding import PartitionSpec as P

GROUP = 4
CHUNKS = 8
LANES = 128


def lane_group(shape, rank_most):
    return lax.broadcasted_iota(jnp.int32, shape, len(shape) - 1) // rank_most


def spread(value, rank_most):
    step = rank_most
    while step < value.shape[-1]:
        value = value + pltpu.roll(value, step, 1)
        step *= 2
    return value


def fold(rank_most, wide, cols):
    packed = wide.shape[0] // GROUP
    groups = lane_group((packed, cols), rank_most)
    folded = jnp.zeros((packed, cols), jnp.float32)
    for g in range(GROUP):
        folded = jnp.where(groups == g, wide[g * packed : (g + 1) * packed], folded)
    return folded.astype(jnp.bfloat16)


def unfold(rank_most, folded):
    groups = lane_group(folded.shape, rank_most)
    return jnp.concatenate(
        [spread(jnp.where(groups == g, folded, 0.0), rank_most) for g in range(GROUP)], axis=0
    )


def scaling(rank_most, rank, shape):
    place = lax.broadcasted_iota(jnp.int32, shape, 1) % rank_most
    return jnp.where(place.astype(jnp.float32) < rank, 32.0 / rank, 0.0)


def fetches(source, target, sems, axis=0):
    size = source.shape[axis] // CHUNKS
    copies = []
    for c in range(CHUNKS):
        part = (slice(None),) * axis + (pl.ds(c * size, size),)
        copies.append(pltpu.make_async_copy(source.at[part], target.at[part], sems.at[c]))
    for copy in copies:
        copy.start()
    return copies


def inverse_rms(squares, width):
    return lax.rsqrt(jnp.sum(squares, axis=-1, keepdims=True) / width + 1e-05)


def table_kernel(rank_most, info_ref, first_ref, second_ref):
    info = info_ref[...].astype(jnp.float32)
    rows = info.shape[0]
    lane = lax.broadcasted_iota(jnp.int32, info.shape, 1)
    ranks = jnp.broadcast_to(info[:, 2:3], info.shape).astype(jnp.bfloat16)
    numbers = lax.broadcasted_iota(jnp.int32, (rows, rows), 1).astype(jnp.float32)
    for micro, ref in enumerate((first_ref, second_ref)):
        ids = info[:, micro : micro + 1]
        onehot = jnp.where(ids == numbers, 1.0, 0.0).astype(jnp.bfloat16)
        rank = jnp.dot(onehot, ranks, preferred_element_type=jnp.float32)
        ref[...] = jnp.where(lane == 0, ids, rank)


def pack_kernel(rank_most, maps_ref, info_ref, out_ref):
    held, cols = maps_ref.shape[0], out_ref.shape[2]
    for d in range(out_ref.shape[0]):
        out_ref[d, :held, :] = maps_ref[:, d * cols : (d + 1) * cols]
        out_ref[d, held:, :] = info_ref[...]


def first_kernel(
    rank_most, hidden_ref, base_hbm, maps_hbm, gain_ref, table_ref, owner_ref, order_hbm,
    base_out, sent_out, base_ref, maps_ref, base_sems, maps_sems,
):
    rows = hidden_ref.shape[0]
    width, cols = base_ref.shape
    held = maps_ref.shape[0]
    base_copies = fetches(base_hbm, base_ref, base_sems)
    maps_copies = fetches(maps_hbm, maps_ref, maps_sems, axis=1)
    base = jnp.zeros((rows, cols), jnp.float32)
    shrunk = jnp.zeros((rows, held), jnp.float32)
    squares = jnp.zeros((rows, cols), jnp.float32)
    steps = width // cols
    for j in range(steps):
        if j % (steps // CHUNKS) == 0:
            base_copies[j // (steps // CHUNKS)].wait()
            maps_copies[j // (steps // CHUNKS)].wait()
        part = slice(j * cols, (j + 1) * cols)
        wide = hidden_ref[:, part].astype(jnp.float32)
        squares = squares + wide * wide
        scaled = (wide * gain_ref[:, part]).astype(jnp.bfloat16)
        base = base + jnp.dot(scaled, base_ref[part, :], preferred_element_type=jnp.float32)
        shrunk = shrunk + lax.dot_general(
            scaled, maps_ref[:, part], (((1,), (1,)), ((), ())), preferred_element_type=jnp.float32
        )
    inverse = inverse_rms(squares, width)
    base_out[...] = base * inverse
    groups = lane_group((rows, held), rank_most)
    first = owner_ref[0] * (held // rank_most)
    wanted = table_ref[:, 0:1] == (first + groups).astype(jnp.float32)
    factor = scaling(rank_most, table_ref[:, 1:2], (rows, held))
    low = spread(jnp.where(wanted, shrunk * inverse * factor, 0.0), rank_most)
    folded = fold(rank_most, jnp.concatenate([low] * (cols // held), axis=1), cols)
    for d in range(sent_out.shape[0]):
        sent_out[d] = folded


def finish(rank_most, h_ref, base, low, table_ref, expand_ref, out_ref):
    rows, cols = h_ref.shape
    wanted = table_ref[:, 0:1] - lane_group((rows, cols), rank_most).astype(jnp.float32)
    added = jnp.zeros((rows, cols), jnp.float32)
    for j in range(expand_ref.shape[0] // cols):
        picked = jnp.where(wanted == j * GROUP, low, 0.0).astype(jnp.bfloat16)
        added = added + jnp.dot(
            picked, expand_ref[j * cols : (j + 1) * cols, :], preferred_element_type=jnp.float32
        )
    update = (base + added).astype(jnp.bfloat16)
    out_ref[...] = (h_ref[...].astype(jnp.float32) + update.astype(jnp.float32)).astype(
        jnp.bfloat16
    )


def first_after_kernel(rank_most, h_ref, got_ref, table_ref, base_ref, expand_ref, out_ref):
    partial = jnp.zeros(got_ref.shape[1:], jnp.float32)
    for j in range(got_ref.shape[0]):
        partial = partial + got_ref[j].astype(jnp.float32)
    low = unfold(rank_most, partial)
    finish(rank_most, h_ref, base_ref[...], low, table_ref, expand_ref, out_ref)


def before_kernel(rank_most, h_ref, table_ref, shrink_hbm, out_ref, shrink_ref, sems):
    rows, cols = h_ref.shape
    copies = fetches(shrink_hbm, shrink_ref, sems)
    h = h_ref[...]
    wanted = table_ref[:, 0:1] - lane_group((rows, cols), rank_most).astype(jnp.float32)
    total = jnp.zeros((rows, cols), jnp.float32)
    steps = shrink_ref.shape[0] // cols
    for j in range(steps):
        if j % (steps // CHUNKS) == 0:
            copies[j // (steps // CHUNKS)].wait()
        part = lax.dot_general(
            h,
            shrink_ref[j * cols : (j + 1) * cols, :],
            (((1,), (1,)), ((), ())),
            preferred_element_type=jnp.float32,
        )
        total = total + jnp.where(wanted == j * GROUP, part, 0.0)
    folded = fold(rank_most, spread(total, rank_most), cols)
    for d in range(out_ref.shape[0]):
        out_ref[d, :rows, :] = h
        out_ref[d, rows:, :] = folded


def after_kernel(
    rank_most, h_ref, got_ref, table_ref, base_hbm, expand_ref, out_ref, base_ref, sems
):
    rows, cols = h_ref.shape
    copies = fetches(base_hbm, base_ref, sems)
    sources = got_ref.shape[0]
    base = jnp.zeros((rows, cols), jnp.float32)
    squares = jnp.zeros((rows, cols), jnp.float32)
    partial = jnp.zeros((rows // GROUP, cols), jnp.float32)
    for j in range(sources):
        if j % (sources // CHUNKS) == 0:
            copies[j // (sources // CHUNKS)].wait()
        block = got_ref[j, :rows, :]
        base = base + jnp.dot(
            block, base_ref[j * cols : (j + 1) * cols, :], preferred_element_type=jnp.float32
        )
        wide = block.astype(jnp.float32)
        squares = squares + wide * wide
        partial = partial + got_ref[j, rows:, :].astype(jnp.float32)
    inverse = inverse_rms(squares, sources * cols)
    factor = scaling(rank_most, table_ref[:, 1:2], (rows, cols))
    low = unfold(rank_most, partial) * inverse * factor
    finish(rank_most, h_ref, base * inverse, low, table_ref, expand_ref, out_ref)


def unused_kernel(rank_most, *refs):
    for ref in refs:
        ref[:16, :] = jnp.zeros((16, ref.shape[1]), ref.dtype)


def on_device(tokens, adapter_ids, ranks, gain, base_weight, shrink_weight, expand_weight):
    micro_count, own_rows, model_width = tokens.shape
    cols = base_weight.shape[2]
    ad_count, _, rank_most = shrink_weight.shape[1:]
    total_adapters = expand_weight.shape[1]
    devices = lax.axis_size("adapter")
    segments = lax.axis_size("segment")
    segment = lax.axis_index("segment")
    owner = lax.axis_index("adapter")
    rows = own_rows * devices
    packed = rows // GROUP
    held = ad_count * rank_most
    all_held = total_adapters * rank_most
    gain_row = gain[0]
    expand = expand_weight[0].reshape(all_held, cols)
    maps = shrink_weight[0].transpose(0, 2, 1).reshape(held, model_width)

    half, full = jnp.bfloat16, jnp.float32
    state = ((rows, cols), half)
    vmem = pl.BlockSpec(memory_space=pltpu.VMEM)
    hbm = pl.BlockSpec(memory_space=pl.ANY)
    smem = pl.BlockSpec(memory_space=pltpu.SMEM)
    fetched = pltpu.SemaphoreType.DMA((CHUNKS,))

    def call(kernel, shapes, *operands, specs=None, scratch=()):
        return pl.pallas_call(
            lambda *refs: kernel(rank_most, *refs),
            out_shape=[jax.ShapeDtypeStruct(*shape) for shape in shapes],
            in_specs=specs or [vmem] * len(operands),
            out_specs=[vmem] * len(shapes),
            scratch_shapes=scratch,
            compiler_params=pltpu.CompilerParams(vmem_limit_bytes=14 * 1024 * 1024),
        )(*operands)

    def exchange(blocks):
        return lax.all_to_all(blocks, "adapter", 0, 0, tiled=True)

    info = jnp.concatenate([adapter_ids[0], adapter_ids[1], ranks[:, None]], axis=1)
    info = jnp.pad(info.astype(half), ((0, 0), (0, LANES - info.shape[1])))

    def tables(info):
        return call(table_kernel, [((rows, LANES), full)] * 2, info)

    def gather_rows(micro):
        block = jnp.concatenate([tokens[micro], info], axis=1)
        got = exchange(jnp.broadcast_to(block, (devices,) + block.shape))
        return got.reshape(rows, model_width + LANES)

    def first_layer(hidden, table, order):
        base, sent = call(
            first_kernel,
            [((rows, cols), full), ((devices, packed, cols), half)],
            hidden,
            base_weight[0],
            maps,
            gain,
            table,
            owner.astype(jnp.int32).reshape(1),
            order,
            specs=[vmem, hbm, hbm, vmem, vmem, smem, hbm],
            scratch=[
                pltpu.VMEM((model_width, cols), half),
                pltpu.VMEM((held, model_width), half),
                fetched,
                fetched,
            ],
        )
        own = lax.dynamic_slice_in_dim(hidden, owner * cols, cols, 1)
        return call(first_after_kernel, [state], own, exchange(sent), table, base, expand)[0]

    def open_first(hidden):
        table, next_table = tables(hidden[:, model_width:])
        h = first_layer(hidden, table, hidden)
        shrink, base = call(
            unused_kernel, [((all_held, cols), half), ((model_width, cols), half)]
        )
        return h, table, next_table, shrink, base

    def open_other(hidden):
        extra = jnp.pad(info, ((0, 16 - own_rows), (0, cols - LANES)))
        (sent,) = call(pack_kernel, [((devices, held + 16, cols), half)], maps, extra)
        got = exchange(sent)
        table, next_table = tables(got[:, held : held + own_rows, :LANES].reshape(rows, LANES))
        shrink = got[:, :held].reshape(all_held, cols)
        own_gain = lax.dynamic_slice_in_dim(gain_row, owner * cols, cols, 0)
        shrink = (shrink.astype(full) * own_gain[None, :]).astype(half)
        base = (base_weight[0].astype(full) * gain_row[:, None]).astype(half)
        return jnp.zeros((rows, cols), half), table, next_table, shrink, base

    block_shape = (devices, rows + packed, cols)

    def spread_out(h, table, shrink):
        (sent,) = call(
            before_kernel,
            [(block_shape, half)],
            h,
            table,
            shrink,
            specs=[vmem, vmem, hbm],
            scratch=[pltpu.VMEM((all_held, cols), half), fetched],
        )
        return exchange(sent)

    def project(h, got, table, base):
        return call(
            after_kernel,
            [state],
            h,
            got,
            table,
            base,
            expand,
            specs=[vmem, vmem, vmem, hbm, vmem],
            scratch=[pltpu.VMEM((model_width, cols), half), fetched],
        )[0]

    def nothing():
        return jnp.zeros((rows, cols), half)

    hidden = lax.cond(
        segment == 0,
        lambda: gather_rows(0),
        lambda: lax.cond(
            segment == 2,
            lambda: gather_rows(1),
            lambda: jnp.zeros((rows, model_width + LANES), half),
        ),
    )
    later = lax.ppermute(hidden, "segment", [(2, 0)])
    h, table, next_table, shrink, base = lax.cond(segment == 0, open_first, open_other, hidden)
    outs = [h, h]
    for stage in range(1, segments + 1):
        pairs = [(s, s + 1) for s in (stage - 1, stage - 2) if 0 <= s < segments - 1]
        h = lax.ppermute(h, "segment", pairs)
        leads, trails = segment == stage, segment == stage - 1
        now = jnp.where(leads, table, next_table)
        if stage == 1:
            got = lax.cond(
                leads,
                lambda: spread_out(h, now, shrink),
                lambda: jnp.zeros(block_shape, half),
            )
            over = lax.ppermute(got[0, :16, :LANES], "segment", [(1, 0)])
            branch = jnp.where(trails, 2, jnp.where(leads, 1, 0))
            h = lax.switch(
                branch,
                (nothing, lambda: project(h, got, now, base), lambda: first_layer(later, now, over)),
            )
        else:
            h = lax.cond(
                leads | trails,
                lambda: project(h, spread_out(h, now, shrink), now, base),
                nothing,
            )
        outs = [jnp.where(leads, h, outs[0]), jnp.where(trails, h, outs[1])]
    return jnp.stack(outs)[None]


def solution(mesh):
    in_specs = (
        P(None, "adapter", None),
        P(None, "adapter", None),
        P("adapter"),
        P("segment", None),
        P("segment", None, "adapter"),
        P("segment", "adapter", None, None),
        P("segment", None, None, "adapter"),
    )
    out_specs = P("segment", None, None, "adapter")
    return jax.shard_map(
        on_device, mesh=mesh, in_specs=in_specs, out_specs=out_specs, check_vma=False
    )
```

time: 400 us -> 375 us (0.938)
  blocking collectives: 0 us -> 54.6 us
  waiting for transfers between devices: 324 us -> 270 us
  local copies, waits for them, and re-layouts: 16.4 us -> 3.89 us
  starting transfers between devices: 30 us -> 20.4 us
  other arithmetic: 13 us -> 8.9 us
    all_to_all x0 -> x2, blocking collectives: none -> 54.6 us  [exchange(): return lax.all_to_all(blocks, 'adapter', 0, 0, tiled=True)]
    all_to_all x3 -> x1, waiting for transfers between devices: 85.9 us -> 50.2 us  [exchange(): return lax.all_to_all(blocks, 'adapter', 0, 0, tiled=True)]
    ppermute x8, waiting for transfers between devices: 238 us -> 220 us  [on_device(): h = lax.ppermute(h, 'segment', pairs)]
    all_to_all x3 -> x1, starting transfers between devices: 23.5 us -> 11.3 us  [exchange(): return lax.all_to_all(blocks, 'adapter', 0, 0, tiled=True)]
    another operation x29 -> x10, local copies, waits for them, and re-layouts: 11.8 us -> 1.26 us
    pallas_call x4 -> x6, Pallas kernels: 15.2 us -> 16.2 us  [call(): pl.pallas_call(lambda *refs: kernel(rank_most, *refs), out_shape=[jax.Sha...]
  transfers between devices with their start and end apart: 11 -> 11, of which waited for: 5 -> 3; matrix products, arithmetic and copies ran while one was open for 2% -> 2% of each run, Pallas kernels for 0% -> 1%
where the time goes in v4:
time: 375 us
  waiting for transfers between devices  270 us (72%)
  blocking collectives  54.6 us (15%)
  starting transfers between devices  20.4 us (5%)
  Pallas kernels  16.2 us (4%)
  other arithmetic  8.9 us (2%)
  local copies, waits for them, and re-layouts  3.89 us (1%)
    ppermute x8, waiting for transfers between devices, on_device(): h = lax.ppermute(h, 'segment', pairs)  220 us
    all_to_all x2, blocking collectives, exchange(): return lax.all_to_all(blocks, 'adapter', 0, 0, tiled=True)  54.6 us
    all_to_all x1, waiting for transfers between devices, exchange(): return lax.all_to_all(blocks, 'adapter', 0, 0, tiled=True)  50.2 us
    pallas_call x6, Pallas kernels, call(): pl.pallas_call(lambda *refs: kernel(rank_most, *refs), out_shape=[jax.Sha...  16.2 us
    all_to_all x1, starting transfers between devices, exchange(): return lax.all_to_all(blocks, 'adapter', 0, 0, tiled=True)  11.3 us
  transfers between devices with their start and end apart: 11, of which 3 were waited for; matrix products, arithmetic and copies ran while one was open for 2% of the time, Pallas kernels for 1%

profile of v4, /device:TPU:7, one launch (start us, length us, event | category | flops | bytes accessed | tf_op | source)
XLA Modules:
  0.0 374.6 jit_solution(7597938185681030416)
XLA Ops:
  1.4 1.1 conditional.12
  1.4 1.1 conditional
  1.4 1.1 broadcast.23
  2.5 1.7 collective-permute-start.1
  4.1 74.4 %conditional.13 = (bf16[64,256]{1,0:T(8,128)(2,1)S(1)}, f32[64,128]{1,0:T(8,128)}, f32[64,128]{1,0:T(8,128)S(1)}, bf16[4096,256]{1,0:T(8,128)(2,1)}, bf16[8192,256]{1,0:T(8,128)(2,1)}) conditional(s32[]{:T(128)} %convert_element_type.55, (bf16[2,128]{0,1:T(8,128)(2,1)S(1)}, bf16[128,8192]{1,0:T(8,128)(2,1)}, s32[]{:T(128)}, f32[1,8192]{1,0:T(1,128)S(1)}, ...), branch_computations={%region_4.5_spmd, %region_5.6_spmd} | conditional | flops 9437188 | bytes 23966334 | solution.py:323
  4.2 3.3 branch_0_fun.2
  7.5 11.3 %all-to-all-start.3 = ((bf16[32,144,256]{2,1,0:T(8,128)(2,1)}), bf16[32,144,256]{2,1,0:T(8,128)(2,1)}, u32[]{:S(2)}, u32[]{:S(2)}) async-start(bf16[32,144,256]{2,1,0:T(8,128)(2,1)} %branch_0_fun.2), calls=%async_computation.3 | async-start | bytes 4718592 | tf_op jit(solution)/shard_map/cond/branch_0_fun/all_to_all | solution.py:229
  18.8 4.2 %fusion = bf16[8192,256]{1,0:T(8,128)(2,1)} fusion(bf16[1,8192,256]{2,1,0:T(8,128)(2,1)} %get-tuple-element.234, f32[8192]{0:T(1024)S(1)} %bitcast.53), kind=kLoop, calls=%fused_computation.5 | loop fusion | flops 6291456 | bytes 8421376 | tf_op jit(solution)/shard_map/cond/branch_0_fun/convert_element_type | solution.py:280
  23.0 50.2 %all-to-all-done.3 = bf16[32,144,256]{2,1,0:T(8,128)(2,1)} async-done(((bf16[32,144,256]{2,1,0:T(8,128)(2,1)}), bf16[32,144,256]{2,1,0:T(8,128)(2,1)}, u32[]{:S(2)}, u32[]{:S(2)}) %all-to-all-start.3) | async-done | bytes 2359328 | tf_op jit(solution)/shard_map/cond/branch_0_fun/all_to_all | solution.py:229
  73.2 0.9 slice.29
  74.9 1.7 slice.30
  76.6 1.9 fusion.1
  83.9 1.3 collective-permute-start.8
  85.2 208.9 %collective-permute-done.8 = bf16[64,256]{1,0:T(8,128)(2,1)S(1)} collective-permute-done((bf16[64,256]{1,0:T(8,128)(2,1)S(1)}, bf16[64,256]{1,0:T(8,128)(2,1)S(1)}, u32[]{:S(2)}, u32[]{:S(2)}) %collective-permute-start.8) | collective-permute-done | bytes 32800 | tf_op jit(solution)/shard_map/ppermute | solution.py:327
  294.1 36.4 %conditional.21 = (bf16[64,256]{1,0:T(8,128)(2,1)S(1)}) conditional(s32[]{:T(128)} %convert_element_type.56, () %tuple.87, (pred[]{:T(512)}, f32[64,128]{1,0:T(8,128)}, f32[64,128]{1,0:T(8,128)S(1)}, bf16[64,256]{1,0:T(8,128)(2,1)S(1)}, bf16[4096,256]{1,0:T(8,128)(2,1)}, /*index=5*/bf16[8192,256]{1,0:T(8,128)(2,1)}, ...), branch_computations={%region_21.22_spmd, %region_22.23_spmd} | conditional | flops 8192 | bytes 2719753 | solution.py:343
  294.9 2.8 branch_1_fun.36
  297.8 29.5 %all_to_all.60.refs_1_ = bf16[32,80,256]{2,1,0:T(8,128)(2,1)S(1)} all-to-all(bf16[32,80,256]{2,1,0:T(8,128)(2,1)S(1)} %branch_1_fun.36), channel_id=1, replica_groups=mesh['segment'=8,'adapter'=32] {'adapter'}, dimensions={0} | all-to-all | bytes 2621440 | tf_op jit(solution)/shard_map/cond/branch_1_fun/all_to_all | solution.py:229
  327.3 3.2 branch_1_fun.37
  330.5 1.3 collective-permute-start.9
  331.8 10.9 %collective-permute-done.9 = bf16[64,256]{1,0:T(8,128)(2,1)S(1)} collective-permute-done((bf16[64,256]{1,0:T(8,128)(2,1)S(1)}, bf16[64,256]{1,0:T(8,128)(2,1)S(1)}, u32[]{:S(2)}, u32[]{:S(2)}) %collective-permute-start.9) | collective-permute-done | bytes 32800 | tf_op jit(solution)/shard_map/ppermute | solution.py:327
  342.7 31.2 %conditional.22 = (bf16[64,256]{1,0:T(8,128)(2,1)S(1)}) conditional(s32[]{:T(128)} %convert_element_type.54, () %tuple.82, (pred[]{:T(512)}, f32[64,128]{1,0:T(8,128)}, f32[64,128]{1,0:T(8,128)S(1)}, bf16[64,256]{1,0:T(8,128)(2,1)S(1)}, bf16[4096,256]{1,0:T(8,128)(2,1)}, /*index=5*/bf16[8192,256]{1,0:T(8,128)(2,1)}, ...), branch_computations={%region_23.24_spmd, %region_24.25_spmd} | conditional | flops 8192 | bytes 2719753 | solution.py:343
  342.8 2.8 branch_1_fun.38
  345.6 25.1 %all_to_all.61.refs_1_ = bf16[32,80,256]{2,1,0:T(8,128)(2,1)S(1)} all-to-all(bf16[32,80,256]{2,1,0:T(8,128)(2,1)S(1)} %branch_1_fun.38), channel_id=1, replica_groups=mesh['segment'=8,'adapter'=32] {'adapter'}, dimensions={0} | all-to-all | bytes 2621440 | tf_op jit(solution)/shard_map/cond/branch_1_fun/all_to_all | solution.py:229
  370.7 3.2 branch_1_fun.39
  (52 shorter events, 9.0 us)
Async XLA Ops:
  1.4 2.8 copy-start
  1.4 2.8 copy-start.1
  2.5 77.6 %collective-permute-start.1 = (bf16[64,8320]{1,0:T(8,128)(2,1)}, bf16[64,8320]{1,0:T(8,128)(2,1)}, u32[]{:S(2)}, u32[]{:S(2)}) collective-permute-start(bf16[64,8320]{1,0:T(8,128)(2,1)} %get-tuple-element.350), channel_id=1, source_target_pairs={{64,0},{65,1},{66,2},{67,3},{68,4},{69,5},{70,6},{71,7},{72,8},{73... | collective-permute-start | bytes 3194888 | tf_op jit(solution)/shard_map/ppermute | solution.py:322
  7.5 65.7 %all-to-all-start.3 = ((bf16[32,144,256]{2,1,0:T(8,128)(2,1)}), bf16[32,144,256]{2,1,0:T(8,128)(2,1)}, u32[]{:S(2)}, u32[]{:S(2)}) async-start(bf16[32,144,256]{2,1,0:T(8,128)(2,1)} %branch_0_fun.2), calls=%async_computation.3 | async-start | bytes 4718592 | tf_op jit(solution)/shard_map/cond/branch_0_fun/all_to_all | solution.py:229
  78.5 0.7 copy-start.2
  78.5 0.7 collective-permute-start
  79.4 0.7 collective-permute-start.2
  80.1 0.9 collective-permute-start.3
  81.0 0.7 collective-permute-start.4
  81.7 0.7 collective-permute-start.5
  82.5 0.7 collective-permute-start.6
  83.2 0.7 collective-permute-start.7
  83.9 210.2 %collective-permute-start.8 = (bf16[64,256]{1,0:T(8,128)(2,1)S(1)}, bf16[64,256]{1,0:T(8,128)(2,1)S(1)}, u32[]{:S(2)}, u32[]{:S(2)}) collective-permute-start(bf16[64,256]{1,0:T(8,128)(2,1)S(1)} %get-tuple-element.357), channel_id=1, source_target_pairs={{192,224},{160,192},{193,225},{161,193},{194,226},{162,194},{195,2... | collective-permute-start | bytes 98312 | tf_op jit(solution)/shard_map/ppermute | solution.py:327
  330.5 12.2 %collective-permute-start.9 = (bf16[64,256]{1,0:T(8,128)(2,1)S(1)}, bf16[64,256]{1,0:T(8,128)(2,1)S(1)}, u32[]{:S(2)}, u32[]{:S(2)}) collective-permute-start(bf16[64,256]{1,0:T(8,128)(2,1)S(1)} %get-tuple-element.358), channel_id=1, source_target_pairs={{192,224},{193,225},{194,226},{195,227},{196,228},{197,229},{198,2... | collective-permute-start | bytes 98312 | tf_op jit(solution)/shard_map/ppermute | solution.py:327
  342.7 31.2 %copy-start.3 = (bf16[64,256]{1,0:T(8,128)(2,1)S(1)}, bf16[64,256]{1,0:T(8,128)(2,1)}, u32[]{:S(2)}) copy-start(bf16[64,256]{1,0:T(8,128)(2,1)} %copy-done.2) | copy-start | bytes 98308

commit v5 on v4

--- a/solution.py
+++ b/solution.py
@@ -58,28 +58,33 @@
     return lax.rsqrt(jnp.sum(squares, axis=-1, keepdims=True) / width + 1e-05)
 
 
-def table_kernel(rank_most, info_ref, first_ref, second_ref):
+def table_kernel(rank_most, info_ref, table_ref):
     info = info_ref[...].astype(jnp.float32)
     rows = info.shape[0]
     lane = lax.broadcasted_iota(jnp.int32, info.shape, 1)
     ranks = jnp.broadcast_to(info[:, 2:3], info.shape).astype(jnp.bfloat16)
     numbers = lax.broadcasted_iota(jnp.int32, (rows, rows), 1).astype(jnp.float32)
-    for micro, ref in enumerate((first_ref, second_ref)):
+    table = jnp.zeros(info.shape, jnp.float32)
+    for micro in range(2):
         ids = info[:, micro : micro + 1]
         onehot = jnp.where(ids == numbers, 1.0, 0.0).astype(jnp.bfloat16)
         rank = jnp.dot(onehot, ranks, preferred_element_type=jnp.float32)
-        ref[...] = jnp.where(lane == 0, ids, rank)
-
-
-def pack_kernel(rank_most, maps_ref, info_ref, out_ref):
-    held, cols = maps_ref.shape[0], out_ref.shape[2]
-    for d in range(out_ref.shape[0]):
-        out_ref[d, :held, :] = maps_ref[:, d * cols : (d + 1) * cols]
-        out_ref[d, held:, :] = info_ref[...]
+        table = jnp.where(lane == 2 * micro, ids, table)
+        table = jnp.where(lane == 2 * micro + 1, rank, table)
+    table_ref[...] = table
+
+
+def ids_and_rank(table_ref, micro_ref):
+    table = table_ref[...]
+    first = micro_ref[0] == 0
+    return (
+        jnp.where(first, table[:, 0:1], table[:, 2:3]),
+        jnp.where(first, table[:, 1:2], table[:, 3:4]),
+    )
 
 
 def first_kernel(
-    rank_most, hidden_ref, base_hbm, maps_hbm, gain_ref, table_ref, owner_ref, order_hbm,
+    rank_most, hidden_ref, base_hbm, maps_hbm, gain_ref, table_ref, micro_ref, owner_ref, order_hbm,
     base_out, sent_out, base_ref, maps_ref, base_sems, maps_sems,
 ):
     rows = hidden_ref.shape[0]
@@ -107,17 +112,16 @@
     base_out[...] = base * inverse
     groups = lane_group((rows, held), rank_most)
     first = owner_ref[0] * (held // rank_most)
-    wanted = table_ref[:, 0:1] == (first + groups).astype(jnp.float32)
-    factor = scaling(rank_most, table_ref[:, 1:2], (rows, held))
+    ids, rank = ids_and_rank(table_ref, micro_ref)
+    wanted = ids == (first + groups).astype(jnp.float32)
+    factor = scaling(rank_most, rank, (rows, held))
     low = spread(jnp.where(wanted, shrunk * inverse * factor, 0.0), rank_most)
-    folded = fold(rank_most, jnp.concatenate([low] * (cols // held), axis=1), cols)
-    for d in range(sent_out.shape[0]):
-        sent_out[d] = folded
-
-
-def finish(rank_most, h_ref, base, low, table_ref, expand_ref, out_ref):
+    sent_out[...] = fold(rank_most, jnp.concatenate([low] * (cols // held), axis=1), cols)
+
+
+def finish(rank_most, h_ref, base, low, ids, expand_ref, out_ref):
     rows, cols = h_ref.shape
-    wanted = table_ref[:, 0:1] - lane_group((rows, cols), rank_most).astype(jnp.float32)
+    wanted = ids - lane_group((rows, cols), rank_most).astype(jnp.float32)
     added = jnp.zeros((rows, cols), jnp.float32)
     for j in range(expand_ref.shape[0] // cols):
         picked = jnp.where(wanted == j * GROUP, low, 0.0).astype(jnp.bfloat16)
@@ -130,19 +134,25 @@
     )
 
 
-def first_after_kernel(rank_most, h_ref, got_ref, table_ref, base_ref, expand_ref, out_ref):
+def first_after_kernel(
+    rank_most, h_ref, got_ref, table_ref, micro_ref, base_ref, expand_ref, out_ref
+):
     partial = jnp.zeros(got_ref.shape[1:], jnp.float32)
     for j in range(got_ref.shape[0]):
         partial = partial + got_ref[j].astype(jnp.float32)
     low = unfold(rank_most, partial)
-    finish(rank_most, h_ref, base_ref[...], low, table_ref, expand_ref, out_ref)
-
-
-def before_kernel(rank_most, h_ref, table_ref, shrink_hbm, out_ref, shrink_ref, sems):
+    ids, _ = ids_and_rank(table_ref, micro_ref)
+    finish(rank_most, h_ref, base_ref[...], low, ids, expand_ref, out_ref)
+
+
+def before_kernel(
+    rank_most, h_ref, table_ref, micro_ref, shrink_hbm, out_ref, shrink_ref, sems
+):
     rows, cols = h_ref.shape
     copies = fetches(shrink_hbm, shrink_ref, sems)
     h = h_ref[...]
-    wanted = table_ref[:, 0:1] - lane_group((rows, cols), rank_most).astype(jnp.float32)
+    ids, _ = ids_and_rank(table_ref, micro_ref)
+    wanted = ids - lane_group((rows, cols), rank_most).astype(jnp.float32)
     total = jnp.zeros((rows, cols), jnp.float32)
     steps = shrink_ref.shape[0] // cols
     for j in range(steps):
@@ -155,14 +165,12 @@
             preferred_element_type=jnp.float32,
         )
         total = total + jnp.where(wanted == j * GROUP, part, 0.0)
-    folded = fold(rank_most, spread(total, rank_most), cols)
-    for d in range(out_ref.shape[0]):
-        out_ref[d, :rows, :] = h
-        out_ref[d, rows:, :] = folded
+    out_ref[:rows, :] = h
+    out_ref[rows:, :] = fold(rank_most, spread(total, rank_most), cols)
 
 
 def after_kernel(
-    rank_most, h_ref, got_ref, table_ref, base_hbm, expand_ref, out_ref, base_ref, sems
+    rank_most, h_ref, got_ref, table_ref, micro_ref, base_hbm, expand_ref, out_ref, base_ref, sems
 ):
     rows, cols = h_ref.shape
     copies = fetches(base_hbm, base_ref, sems)
@@ -181,9 +189,9 @@
         squares = squares + wide * wide
         partial = partial + got_ref[j, rows:, :].astype(jnp.float32)
     inverse = inverse_rms(squares, sources * cols)
-    factor = scaling(rank_most, table_ref[:, 1:2], (rows, cols))
-    low = unfold(rank_most, partial) * inverse * factor
-    finish(rank_most, h_ref, base * inverse, low, table_ref, expand_ref, out_ref)
+    ids, rank = ids_and_rank(table_ref, micro_ref)
+    low = unfold(rank_most, partial) * inverse * scaling(rank_most, rank, (rows, cols))
+    finish(rank_most, h_ref, base * inverse, low, ids, expand_ref, out_ref)
 
 
 def unused_kernel(rank_most, *refs):
@@ -228,29 +236,35 @@
     def exchange(blocks):
         return lax.all_to_all(blocks, "adapter", 0, 0, tiled=True)
 
+    def gather(block):
+        return exchange(jnp.broadcast_to(block, (devices,) + block.shape))
+
     info = jnp.concatenate([adapter_ids[0], adapter_ids[1], ranks[:, None]], axis=1)
     info = jnp.pad(info.astype(half), ((0, 0), (0, LANES - info.shape[1])))
 
     def tables(info):
-        return call(table_kernel, [((rows, LANES), full)] * 2, info)
+        return call(table_kernel, [((rows, LANES), full)], info)[0]
+
+    def number(value):
+        return jnp.asarray(value, jnp.int32).reshape(1)
 
     def gather_rows(micro):
         block = jnp.concatenate([tokens[micro], info], axis=1)
-        got = exchange(jnp.broadcast_to(block, (devices,) + block.shape))
-        return got.reshape(rows, model_width + LANES)
-
-    def first_layer(hidden, table, order):
+        return gather(block).reshape(rows, model_width + LANES)
+
+    def first_layer(hidden, table, micro, order):
         base, sent = call(
             first_kernel,
-            [((rows, cols), full), ((devices, packed, cols), half)],
+            [((rows, cols), full), ((packed, cols), half)],
             hidden,
             base_weight[0],
             maps,
             gain,
             table,
-            owner.astype(jnp.int32).reshape(1),
+            micro,
+            number(owner),
             order,
-            specs=[vmem, hbm, hbm, vmem, vmem, smem, hbm],
+            specs=[vmem, hbm, hbm, vmem, vmem, smem, smem, hbm],
             scratch=[
                 pltpu.VMEM((model_width, cols), half),
                 pltpu.VMEM((held, model_width), half),
@@ -259,51 +273,65 @@
             ],
         )
         own = lax.dynamic_slice_in_dim(hidden, owner * cols, cols, 1)
-        return call(first_after_kernel, [state], own, exchange(sent), table, base, expand)[0]
+        return call(
+            first_after_kernel,
+            [state],
+            own,
+            gather(sent),
+            table,
+            micro,
+            base,
+            expand,
+            specs=[vmem, vmem, vmem, smem, vmem, vmem],
+        )[0]
 
     def open_first(hidden):
-        table, next_table = tables(hidden[:, model_width:])
-        h = first_layer(hidden, table, hidden)
+        table = tables(hidden[:, model_width:])
+        h = first_layer(hidden, table, number(0), hidden)
         shrink, base = call(
             unused_kernel, [((all_held, cols), half), ((model_width, cols), half)]
         )
-        return h, table, next_table, shrink, base
+        return h, table, shrink, base
 
     def open_other(hidden):
+        by_dest = shrink_weight[0].reshape(ad_count, devices, cols, rank_most)
+        by_dest = by_dest.transpose(1, 0, 3, 2).reshape(devices, held, cols)
         extra = jnp.pad(info, ((0, 16 - own_rows), (0, cols - LANES)))
-        (sent,) = call(pack_kernel, [((devices, held + 16, cols), half)], maps, extra)
-        got = exchange(sent)
-        table, next_table = tables(got[:, held : held + own_rows, :LANES].reshape(rows, LANES))
+        extra = jnp.broadcast_to(extra, (devices, 16, cols))
+        got = exchange(jnp.concatenate([by_dest, extra], axis=1))
+        base = (base_weight[0].astype(full) * gain_row[:, None]).astype(half)
+        table = tables(got[:, held : held + own_rows, :LANES].reshape(rows, LANES))
         shrink = got[:, :held].reshape(all_held, cols)
         own_gain = lax.dynamic_slice_in_dim(gain_row, owner * cols, cols, 0)
         shrink = (shrink.astype(full) * own_gain[None, :]).astype(half)
-        base = (base_weight[0].astype(full) * gain_row[:, None]).astype(half)
-        return jnp.zeros((rows, cols), half), table, next_table, shrink, base
+        return jnp.zeros((rows, cols), half), table, shrink, base
 
     block_shape = (devices, rows + packed, cols)
 
-    def spread_out(h, table, shrink):
+    def spread_out(h, table, micro, shrink):
         (sent,) = call(
             before_kernel,
-            [(block_shape, half)],
+            [((rows + packed, cols), half)],
             h,
             table,
+            micro,
             shrink,
-            specs=[vmem, vmem, hbm],
+            specs=[vmem, vmem, smem, hbm],
             scratch=[pltpu.VMEM((all_held, cols), half), fetched],
         )
-        return exchange(sent)
-
-    def project(h, got, table, base):
+        return gather(sent)
+
+    def project(h, got, table, micro, base):
         return call(
             after_kernel,
             [state],
             h,
             got,
             table,
+            micro,
             base,
             expand,
-            specs=[vmem, vmem, vmem, hbm, vmem],
+            specs=[vmem, vmem, vmem, smem, hbm, vmem],
             scratch=[pltpu.VMEM((model_width, cols), half), fetched],
         )[0]
 
@@ -320,29 +348,29 @@
         ),
     )
     later = lax.ppermute(hidden, "segment", [(2, 0)])
-    h, table, next_table, shrink, base = lax.cond(segment == 0, open_first, open_other, hidden)
+    h, table, shrink, base = lax.cond(segment == 0, open_first, open_other, hidden)
     outs = [h, h]
     for stage in range(1, segments + 1):
         pairs = [(s, s + 1) for s in (stage - 1, stage - 2) if 0 <= s < segments - 1]
         h = lax.ppermute(h, "segment", pairs)
         leads, trails = segment == stage, segment == stage - 1
-        now = jnp.where(leads, table, next_table)
+        now = number(jnp.where(leads, 0, 1))
         if stage == 1:
             got = lax.cond(
                 leads,
-                lambda: spread_out(h, now, shrink),
+                lambda: spread_out(h, table, now, shrink),
                 lambda: jnp.zeros(block_shape, half),
             )
             over = lax.ppermute(got[0, :16, :LANES], "segment", [(1, 0)])
             branch = jnp.where(trails, 2, jnp.where(leads, 1, 0))
             h = lax.switch(
                 branch,
-                (nothing, lambda: project(h, got, now, base), lambda: first_layer(later, now, over)),
+                (nothing, lambda: project(h, got, table, now, base), lambda: first_layer(later, table, now, over)),
             )
         else:
             h = lax.cond(
                 leads | trails,
-                lambda: project(h, spread_out(h, now, shrink), now, base),
+                lambda: project(h, spread_out(h, table, now, shrink), table, now, base),
                 nothing,
             )
         outs = [jnp.where(leads, h, outs[0]), jnp.where(trails, h, outs[1])]

time: 375 us -> 380 us (1.013)
  local copies, waits for them, and re-layouts: 3.89 us -> 13.7 us
  blocking collectives: 54.6 us -> 50 us
    transpose x0 -> x1, local copies, waits for them, and re-layouts: none -> 4.83 us  [open_other(): by_dest = by_dest.transpose(1, 0, 3, 2).reshape(devices, held, cols)]
    another operation x10 -> x11, local copies, waits for them, and re-layouts: 1.26 us -> 6.05 us
    all_to_all x2, blocking collectives: 54.6 us -> 50 us  [exchange(): return lax.all_to_all(blocks, 'adapter', 0, 0, tiled=True)]
    pallas_call x6 -> x5, Pallas kernels: 16.2 us -> 15.8 us  [call(): pl.pallas_call(lambda *refs: kernel(rank_most, *refs), out_shape=[jax.Sha...]
  transfers between devices with their start and end apart: 11 -> 11, of which waited for: 3 -> 3; matrix products, arithmetic and copies ran while one was open for 2% -> 6% of each run, Pallas kernels for 1% -> 0%
where the time goes in v5:
time: 380 us; the launch traced here: 379 us
  waiting for transfers between devices  267 us (70%)
  blocking collectives  50 us (13%)
  starting transfers between devices  20.2 us (5%)
  Pallas kernels  15.8 us (4%)
  local copies, waits for them, and re-layouts  13.7 us (4%)
  other arithmetic  11.3 us (3%)
    ppermute x8, waiting for transfers between devices, on_device(): h = lax.ppermute(h, 'segment', pairs)  217 us
    all_to_all x1, waiting for transfers between devices, exchange(): return lax.all_to_all(blocks, 'adapter', 0, 0, tiled=True)  50.2 us
    all_to_all x2, blocking collectives, exchange(): return lax.all_to_all(blocks, 'adapter', 0, 0, tiled=True)  50 us
    pallas_call x5, Pallas kernels, call(): pl.pallas_call(lambda *refs: kernel(rank_most, *refs), out_shape=[jax.Sha...  15.8 us
    all_to_all x1, starting transfers between devices, exchange(): return lax.all_to_all(blocks, 'adapter', 0, 0, tiled=True)  11.3 us
  transfers between devices with their start and end apart: 11, of which 3 were waited for; matrix products, arithmetic and copies ran while one was open for 6% of the time, Pallas kernels for 0%

profile of v5, /device:TPU:7, one launch (start us, length us, event | category | flops | bytes accessed | tf_op | source)
XLA Modules:
  0.0 379.1 jit_solution(2950986235365355843)
XLA Ops:
  1.4 1.1 conditional.12
  1.4 1.1 conditional
  2.5 1.6 collective-permute-start.1
  4.1 84.0 %conditional.13 = (bf16[64,256]{1,0:T(8,128)(2,1)S(1)}, f32[64,128]{1,0:T(8,128)}, bf16[4096,256]{1,0:T(8,128)(2,1)}, bf16[8192,256]{1,0:T(8,128)(2,1)}) conditional(s32[]{:T(128)} %convert_element_type.61, (bf16[1,2,8192,64]{2,3,1,0:T(8,128)(2,1)}, bf16[2,128]{0,1:T(8,128)(2,1)S(1)}, s32[]{:T(128)}, f32[1,8192]{1,0:T(1,128)S(1)}, ...), branch_computations={%region_4.5_spmd, %region_5.6_spmd} | conditional | flops 14155780 | bytes 37343860 | solution.py:351
  4.1 4.8 %copy.11 = bf16[1,2,8192,64]{3,2,1,0:T(8,128)(2,1)} copy(bf16[1,2,8192,64]{2,3,1,0:T(8,128)(2,1)} %get-tuple-element.327) | data formatting | bytes 4194304 | tf_op jit(solution)/shard_map
  8.9 4.8 %copy.8 = bf16[32,2,64,256]{3,2,1,0:T(8,128)(2,1)} copy(bf16[32,2,64,256]{2,3,0,1:T(8,128)(2,1)} %bitcast.64) | data formatting | bytes 4194304 | tf_op jit(solution)/shard_map/cond/branch_0_fun/transpose | solution.py:298
  13.9 3.2 pad_maximum_fusion.2
  17.1 11.3 %all-to-all-start.10 = ((bf16[32,144,256]{2,1,0:T(8,128)(2,1)}), bf16[32,144,256]{2,1,0:T(8,128)(2,1)}, u32[]{:S(2)}, u32[]{:S(2)}) async-start(bf16[32,144,256]{2,1,0:T(8,128)(2,1)} %pad_maximum_fusion.2), calls=%async_computation.10 | async-start | bytes 4718592 | tf_op jit(solution)/shard_map/cond/branch_0_fun/all_to_all | solution.py:237
  28.4 4.2 %fusion = bf16[8192,256]{1,0:T(8,128)(2,1)} fusion(bf16[1,8192,256]{2,1,0:T(8,128)(2,1)} %get-tuple-element.238, f32[8192]{0:T(1024)S(1)} %bitcast.66), kind=kLoop, calls=%fused_computation.5 | loop fusion | flops 6291456 | bytes 8421376 | tf_op jit(solution)/shard_map/cond/branch_0_fun/convert_element_type | solution.py:302
  32.6 50.2 %all-to-all-done.10 = bf16[32,144,256]{2,1,0:T(8,128)(2,1)} async-done(((bf16[32,144,256]{2,1,0:T(8,128)(2,1)}), bf16[32,144,256]{2,1,0:T(8,128)(2,1)}, u32[]{:S(2)}, u32[]{:S(2)}) %all-to-all-start.10) | async-done | bytes 2359328 | tf_op jit(solution)/shard_map/cond/branch_0_fun/all_to_all | solution.py:237
  84.5 1.7 slice.30
  86.2 1.9 fusion.1
  93.5 1.3 collective-permute-start.8
  94.8 201.2 %collective-permute-done.8 = bf16[64,256]{1,0:T(8,128)(2,1)S(1)} collective-permute-done((bf16[64,256]{1,0:T(8,128)(2,1)S(1)}, bf16[64,256]{1,0:T(8,128)(2,1)S(1)}, u32[]{:S(2)}, u32[]{:S(2)}) %collective-permute-start.8) | collective-permute-done | bytes 32800 | tf_op jit(solution)/shard_map/ppermute | solution.py:355
  296.0 32.9 %conditional.21 = (bf16[64,256]{1,0:T(8,128)(2,1)S(1)}) conditional(s32[]{:T(128)} %convert_element_type.55, () %tuple.83, (pred[]{:T(512)}, bf16[64,256]{1,0:T(8,128)(2,1)S(1)}, f32[64,128]{1,0:T(8,128)}, bf16[4096,256]{1,0:T(8,128)(2,1)}, bf16[8192,256]{1,0:T(8,128)(2,1)}, /*index=5*/bf16[4096,256]{1,0:T(8,128)(2,1)S(1)}) %tuple.143), branch_computations={%region_21.22_spmd, %region_22.23_spmd} | conditional | flops 1 | bytes 3973141 | solution.py:371
  296.0 3.5 branch_1_fun.36
  299.6 25.1 %all_to_all.60.refs_1_ = bf16[32,80,256]{2,1,0:T(8,128)(2,1)S(1)} all-to-all(bf16[32,80,256]{2,1,0:T(8,128)(2,1)S(1)} %broadcast_in_dim.43), channel_id=1, replica_groups=mesh['segment'=8,'adapter'=32] {'adapter'}, dimensions={0} | all-to-all | bytes 2621440 | tf_op jit(solution)/shard_map/cond/branch_1_fun/all_to_all | solution.py:237
  324.7 4.0 %branch_1_fun.37 = bf16[64,256]{1,0:T(8,128)(2,1)S(1)} custom-call(bf16[64,256]{1,0:T(8,128)(2,1)S(1)} %get-tuple-element.301.refs_0_, bf16[32,80,256]{2,1,0:T(8,128)(2,1)S(1)} %all_to_all.60.refs_1_, f32[64,128]{1,0:T(8,128)} %get-tuple-element.302.refs_1_.refs_2_, s32[1]{0:T(128)} %bitcast.22.refs_2_.refs_3_, ...), custom_call_target="tpu_custom_call" | custom-call | tf_op jit(solution)/shard_map/cond/branch_1_fun/pallas_call | solution.py:227
  328.9 1.3 collective-permute-start.9
  330.2 15.6 %collective-permute-done.9 = bf16[64,256]{1,0:T(8,128)(2,1)S(1)} collective-permute-done((bf16[64,256]{1,0:T(8,128)(2,1)S(1)}, bf16[64,256]{1,0:T(8,128)(2,1)S(1)}, u32[]{:S(2)}, u32[]{:S(2)}) %collective-permute-start.9) | collective-permute-done | bytes 32800 | tf_op jit(solution)/shard_map/ppermute | solution.py:355
  345.8 32.6 %conditional.22 = (bf16[64,256]{1,0:T(8,128)(2,1)S(1)}) conditional(s32[]{:T(128)} %convert_element_type.54, () %tuple.82, (pred[]{:T(512)}, bf16[64,256]{1,0:T(8,128)(2,1)S(1)}, f32[64,128]{1,0:T(8,128)}, bf16[4096,256]{1,0:T(8,128)(2,1)}, bf16[8192,256]{1,0:T(8,128)(2,1)}, /*index=5*/bf16[4096,256]{1,0:T(8,128)(2,1)S(1)}) %tuple.144), branch_computations={%region_23.24_spmd, %region_24.25_spmd} | conditional | flops 1 | bytes 3973141 | solution.py:371
  345.8 3.5 branch_1_fun.38
  349.5 24.9 %all_to_all.61.refs_1_ = bf16[32,80,256]{2,1,0:T(8,128)(2,1)S(1)} all-to-all(bf16[32,80,256]{2,1,0:T(8,128)(2,1)S(1)} %broadcast_in_dim.44), channel_id=1, replica_groups=mesh['segment'=8,'adapter'=32] {'adapter'}, dimensions={0} | all-to-all | bytes 2621440 | tf_op jit(solution)/shard_map/cond/branch_1_fun/all_to_all | solution.py:237
  374.4 4.0 %branch_1_fun.39 = bf16[64,256]{1,0:T(8,128)(2,1)S(1)} custom-call(bf16[64,256]{1,0:T(8,128)(2,1)S(1)} %get-tuple-element.307.refs_0_, bf16[32,80,256]{2,1,0:T(8,128)(2,1)S(1)} %all_to_all.61.refs_1_, f32[64,128]{1,0:T(8,128)} %get-tuple-element.308.refs_1_.refs_2_, s32[1]{0:T(128)} %bitcast.23.refs_2_.refs_3_, ...), custom_call_target="tpu_custom_call" | custom-call | tf_op jit(solution)/shard_map/cond/branch_1_fun/pallas_call | solution.py:227
  (50 shorter events, 10.3 us)
Async XLA Ops:
  1.4 2.8 copy-start
  1.4 2.7 copy-start.1
  2.5 87.1 %collective-permute-start.1 = (bf16[64,8320]{1,0:T(8,128)(2,1)}, bf16[64,8320]{1,0:T(8,128)(2,1)}, u32[]{:S(2)}, u32[]{:S(2)}) collective-permute-start(bf16[64,8320]{1,0:T(8,128)(2,1)} %get-tuple-element.347), channel_id=1, source_target_pairs={{64,0},{65,1},{66,2},{67,3},{68,4},{69,5},{70,6},{71,7},{72,8},{73... | collective-permute-start | bytes 3194888 | tf_op jit(solution)/shard_map/ppermute | solution.py:350
  17.1 65.7 %all-to-all-start.10 = ((bf16[32,144,256]{2,1,0:T(8,128)(2,1)}), bf16[32,144,256]{2,1,0:T(8,128)(2,1)}, u32[]{:S(2)}, u32[]{:S(2)}) async-start(bf16[32,144,256]{2,1,0:T(8,128)(2,1)} %pad_maximum_fusion.2), calls=%async_computation.10 | async-start | bytes 4718592 | tf_op jit(solution)/shard_map/cond/branch_0_fun/all_to_all | solution.py:237
  88.1 0.7 collective-permute-start
  88.9 0.7 collective-permute-start.2
  89.8 0.7 collective-permute-start.3
  90.6 0.7 collective-permute-start.4
  91.3 0.7 collective-permute-start.5
  92.0 0.7 collective-permute-start.6
  92.7 0.7 collective-permute-start.7
  93.5 202.5 %collective-permute-start.8 = (bf16[64,256]{1,0:T(8,128)(2,1)S(1)}, bf16[64,256]{1,0:T(8,128)(2,1)S(1)}, u32[]{:S(2)}, u32[]{:S(2)}) collective-permute-start(bf16[64,256]{1,0:T(8,128)(2,1)S(1)} %get-tuple-element.354), channel_id=1, source_target_pairs={{192,224},{160,192},{193,225},{161,193},{194,226},{162,194},{195,2... | collective-permute-start | bytes 98312 | tf_op jit(solution)/shard_map/ppermute | solution.py:355
  328.9 16.9 %collective-permute-start.9 = (bf16[64,256]{1,0:T(8,128)(2,1)S(1)}, bf16[64,256]{1,0:T(8,128)(2,1)S(1)}, u32[]{:S(2)}, u32[]{:S(2)}) collective-permute-start(bf16[64,256]{1,0:T(8,128)(2,1)S(1)} %get-tuple-element.355), channel_id=1, source_target_pairs={{192,224},{193,225},{194,226},{195,227},{196,228},{197,229},{198,2... | collective-permute-start | bytes 98312 | tf_op jit(solution)/shard_map/ppermute | solution.py:355

commit v6 on v5

--- a/solution.py
+++ b/solution.py
@@ -58,33 +58,25 @@
     return lax.rsqrt(jnp.sum(squares, axis=-1, keepdims=True) / width + 1e-05)
 
 
-def table_kernel(rank_most, info_ref, table_ref):
+def table_kernel(rank_most, info_ref, first_ref, second_ref):
     info = info_ref[...].astype(jnp.float32)
     rows = info.shape[0]
     lane = lax.broadcasted_iota(jnp.int32, info.shape, 1)
     ranks = jnp.broadcast_to(info[:, 2:3], info.shape).astype(jnp.bfloat16)
     numbers = lax.broadcasted_iota(jnp.int32, (rows, rows), 1).astype(jnp.float32)
-    table = jnp.zeros(info.shape, jnp.float32)
-    for micro in range(2):
+    for micro, ref in enumerate((first_ref, second_ref)):
         ids = info[:, micro : micro + 1]
         onehot = jnp.where(ids == numbers, 1.0, 0.0).astype(jnp.bfloat16)
         rank = jnp.dot(onehot, ranks, preferred_element_type=jnp.float32)
-        table = jnp.where(lane == 2 * micro, ids, table)
-        table = jnp.where(lane == 2 * micro + 1, rank, table)
-    table_ref[...] = table
-
-
-def ids_and_rank(table_ref, micro_ref):
-    table = table_ref[...]
-    first = micro_ref[0] == 0
-    return (
-        jnp.where(first, table[:, 0:1], table[:, 2:3]),
-        jnp.where(first, table[:, 1:2], table[:, 3:4]),
-    )
+        ref[...] = jnp.where(lane == 0, ids, rank)
+
+
+def ids_and_rank(table_ref):
+    return table_ref[:, 0:1], table_ref[:, 1:2]
 
 
 def first_kernel(
-    rank_most, hidden_ref, base_hbm, maps_hbm, gain_ref, table_ref, micro_ref, owner_ref, order_hbm,
+    rank_most, hidden_ref, base_hbm, maps_hbm, gain_ref, table_ref, owner_ref, order_hbm,
     base_out, sent_out, base_ref, maps_ref, base_sems, maps_sems,
 ):
     rows = hidden_ref.shape[0]
@@ -112,7 +104,7 @@
     base_out[...] = base * inverse
     groups = lane_group((rows, held), rank_most)
     first = owner_ref[0] * (held // rank_most)
-    ids, rank = ids_and_rank(table_ref, micro_ref)
+    ids, rank = ids_and_rank(table_ref)
     wanted = ids == (first + groups).astype(jnp.float32)
     factor = scaling(rank_most, rank, (rows, held))
     low = spread(jnp.where(wanted, shrunk * inverse * factor, 0.0), rank_most)
@@ -135,23 +127,23 @@
 
 
 def first_after_kernel(
-    rank_most, h_ref, got_ref, table_ref, micro_ref, base_ref, expand_ref, out_ref
+    rank_most, h_ref, got_ref, table_ref, base_ref, expand_ref, out_ref
 ):
     partial = jnp.zeros(got_ref.shape[1:], jnp.float32)
     for j in range(got_ref.shape[0]):
         partial = partial + got_ref[j].astype(jnp.float32)
     low = unfold(rank_most, partial)
-    ids, _ = ids_and_rank(table_ref, micro_ref)
+    ids, _ = ids_and_rank(table_ref)
     finish(rank_most, h_ref, base_ref[...], low, ids, expand_ref, out_ref)
 
 
 def before_kernel(
-    rank_most, h_ref, table_ref, micro_ref, shrink_hbm, out_ref, shrink_ref, sems
+    rank_most, h_ref, table_ref, shrink_hbm, out_ref, shrink_ref, sems
 ):
     rows, cols = h_ref.shape
     copies = fetches(shrink_hbm, shrink_ref, sems)
     h = h_ref[...]
-    ids, _ = ids_and_rank(table_ref, micro_ref)
+    ids, _ = ids_and_rank(table_ref)
     wanted = ids - lane_group((rows, cols), rank_most).astype(jnp.float32)
     total = jnp.zeros((rows, cols), jnp.float32)
     steps = shrink_ref.shape[0] // cols
@@ -170,7 +162,7 @@
 
 
 def after_kernel(
-    rank_most, h_ref, got_ref, table_ref, micro_ref, base_hbm, expand_ref, out_ref, base_ref, sems
+    rank_most, h_ref, got_ref, table_ref, base_hbm, expand_ref, out_ref, base_ref, sems
 ):
     rows, cols = h_ref.shape
     copies = fetches(base_hbm, base_ref, sems)
@@ -189,7 +181,7 @@
         squares = squares + wide * wide
         partial = partial + got_ref[j, rows:, :].astype(jnp.float32)
     inverse = inverse_rms(squares, sources * cols)
-    ids, rank = ids_and_rank(table_ref, micro_ref)
+    ids, rank = ids_and_rank(table_ref)
     low = unfold(rank_most, partial) * inverse * scaling(rank_most, rank, (rows, cols))
     finish(rank_most, h_ref, base * inverse, low, ids, expand_ref, out_ref)
 
@@ -243,7 +235,7 @@
     info = jnp.pad(info.astype(half), ((0, 0), (0, LANES - info.shape[1])))
 
     def tables(info):
-        return call(table_kernel, [((rows, LANES), full)], info)[0]
+        return call(table_kernel, [((rows, LANES), full)] * 2, info)
 
     def number(value):
         return jnp.asarray(value, jnp.int32).reshape(1)
@@ -252,7 +244,7 @@
         block = jnp.concatenate([tokens[micro], info], axis=1)
         return gather(block).reshape(rows, model_width + LANES)
 
-    def first_layer(hidden, table, micro, order):
+    def first_layer(hidden, table, order):
         base, sent = call(
             first_kernel,
             [((rows, cols), full), ((packed, cols), half)],
@@ -261,10 +253,9 @@
             maps,
             gain,
             table,
-            micro,
             number(owner),
             order,
-            specs=[vmem, hbm, hbm, vmem, vmem, smem, smem, hbm],
+            specs=[vmem, hbm, hbm, vmem, vmem, smem, hbm],
             scratch=[
                 pltpu.VMEM((model_width, cols), half),
                 pltpu.VMEM((held, model_width), half),
@@ -279,19 +270,17 @@
             own,
             gather(sent),
             table,
-            micro,
             base,
             expand,
-            specs=[vmem, vmem, vmem, smem, vmem, vmem],
         )[0]
 
     def open_first(hidden):
-        table = tables(hidden[:, model_width:])
-        h = first_layer(hidden, table, number(0), hidden)
+        table, next_table = tables(hidden[:, model_width:])
+        h = first_layer(hidden, table, hidden)
         shrink, base = call(
             unused_kernel, [((all_held, cols), half), ((model_width, cols), half)]
         )
-        return h, table, shrink, base
+        return h, table, next_table, shrink, base
 
     def open_other(hidden):
         by_dest = shrink_weight[0].reshape(ad_count, devices, cols, rank_most)
@@ -300,38 +289,36 @@
         extra = jnp.broadcast_to(extra, (devices, 16, cols))
         got = exchange(jnp.concatenate([by_dest, extra], axis=1))
         base = (base_weight[0].astype(full) * gain_row[:, None]).astype(half)
-        table = tables(got[:, held : held + own_rows, :LANES].reshape(rows, LANES))
+        table, next_table = tables(got[:, held : held + own_rows, :LANES].reshape(rows, LANES))
         shrink = got[:, :held].reshape(all_held, cols)
         own_gain = lax.dynamic_slice_in_dim(gain_row, owner * cols, cols, 0)
         shrink = (shrink.astype(full) * own_gain[None, :]).astype(half)
-        return jnp.zeros((rows, cols), half), table, shrink, base
+        return jnp.zeros((rows, cols), half), table, next_table, shrink, base
 
     block_shape = (devices, rows + packed, cols)
 
-    def spread_out(h, table, micro, shrink):
+    def spread_out(h, table, shrink):
         (sent,) = call(
             before_kernel,
             [((rows + packed, cols), half)],
             h,
             table,
-            micro,
             shrink,
-            specs=[vmem, vmem, smem, hbm],
+            specs=[vmem, vmem, hbm],
             scratch=[pltpu.VMEM((all_held, cols), half), fetched],
         )
         return gather(sent)
 
-    def project(h, got, table, micro, base):
+    def project(h, got, table, base):
         return call(
             after_kernel,
             [state],
             h,
             got,
             table,
-            micro,
             base,
             expand,
-            specs=[vmem, vmem, vmem, smem, hbm, vmem],
+            specs=[vmem, vmem, vmem, hbm, vmem],
             scratch=[pltpu.VMEM((model_width, cols), half), fetched],
         )[0]
 
@@ -348,29 +335,29 @@
         ),
     )
     later = lax.ppermute(hidden, "segment", [(2, 0)])
-    h, table, shrink, base = lax.cond(segment == 0, open_first, open_other, hidden)
+    h, table, next_table, shrink, base = lax.cond(segment == 0, open_first, open_other, hidden)
     outs = [h, h]
     for stage in range(1, segments + 1):
         pairs = [(s, s + 1) for s in (stage - 1, stage - 2) if 0 <= s < segments - 1]
         h = lax.ppermute(h, "segment", pairs)
         leads, trails = segment == stage, segment == stage - 1
-        now = number(jnp.where(leads, 0, 1))
+        now = lax.optimization_barrier(jnp.where(leads, table, next_table))
         if stage == 1:
             got = lax.cond(
                 leads,
-                lambda: spread_out(h, table, now, shrink),
+                lambda: spread_out(h, now, shrink),
                 lambda: jnp.zeros(block_shape, half),
             )
             over = lax.ppermute(got[0, :16, :LANES], "segment", [(1, 0)])
             branch = jnp.where(trails, 2, jnp.where(leads, 1, 0))
             h = lax.switch(
                 branch,
-                (nothing, lambda: project(h, got, table, now, base), lambda: first_layer(later, table, now, over)),
+                (nothing, lambda: project(h, got, now, base), lambda: first_layer(later, now, over)),
             )
         else:
             h = lax.cond(
                 leads | trails,
-                lambda: project(h, spread_out(h, table, now, shrink), table, now, base),
+                lambda: project(h, spread_out(h, now, shrink), now, base),
                 nothing,
             )
         outs = [jnp.where(leads, h, outs[0]), jnp.where(trails, h, outs[1])]

time: 380 us -> 370 us (0.974)
  waiting for transfers between devices: 267 us -> 258 us
    ppermute x8, waiting for transfers between devices: 217 us -> 207 us  [on_device(): h = lax.ppermute(h, 'segment', pairs)]
where the time goes in v6:
time: 370 us; the launch traced here: 369 us
  waiting for transfers between devices  258 us (70%)
  blocking collectives  50.2 us (14%)
  starting transfers between devices  20.3 us (5%)
  local copies, waits for them, and re-layouts  14.4 us (4%)
  other arithmetic  12.8 us (3%)
  Pallas kernels  12.8 us (3%)
    ppermute x8, waiting for transfers between devices, on_device(): h = lax.ppermute(h, 'segment', pairs)  207 us
    all_to_all x2, blocking collectives, exchange(): return lax.all_to_all(blocks, 'adapter', 0, 0, tiled=True)  50.2 us
    all_to_all x1, waiting for transfers between devices, exchange(): return lax.all_to_all(blocks, 'adapter', 0, 0, tiled=True)  50.2 us
    pallas_call x5, Pallas kernels, call(): pl.pallas_call(lambda *refs: kernel(rank_most, *refs), out_shape=[jax.Sha...  12.8 us
    all_to_all x1, starting transfers between devices, exchange(): return lax.all_to_all(blocks, 'adapter', 0, 0, tiled=True)  11.3 us
  transfers between devices with their start and end apart: 11, of which 3 were waited for; matrix products, arithmetic and copies ran while one was open for 6% of the time, Pallas kernels for 0%

profile of v6, /device:TPU:7, one launch (start us, length us, event | category | flops | bytes accessed | tf_op | source)
XLA Modules:
  0.0 368.7 jit_solution(13547272386971253067)
XLA Ops:
  1.4 1.1 conditional.12
  2.5 1.7 collective-permute-start.1
  4.1 84.0 %conditional.13 = (bf16[64,256]{1,0:T(8,128)(2,1)S(1)}, f32[64,128]{1,0:T(8,128)}, f32[64,128]{1,0:T(8,128)S(1)}, bf16[4096,256]{1,0:T(8,128)(2,1)}, bf16[8192,256]{1,0:T(8,128)(2,1)}) conditional(s32[]{:T(128)} %convert_element_type.61, (bf16[1,2,8192,64]{2,3,1,0:T(8,128)(2,1)}, bf16[2,128]{0,1:T(8,128)(2,1)S(1)}, s32[]{:T(128)}, ...), branch_computations={%region_4.5_spmd, %region_5.6_spmd} | conditional | flops 14155780 | bytes 37343868 | solution.py:338
  4.1 4.8 %copy.11 = bf16[1,2,8192,64]{3,2,1,0:T(8,128)(2,1)} copy(bf16[1,2,8192,64]{2,3,1,0:T(8,128)(2,1)} %get-tuple-element.275) | data formatting | bytes 4194304 | tf_op jit(solution)/shard_map
  8.9 4.8 %copy.8 = bf16[32,2,64,256]{3,2,1,0:T(8,128)(2,1)} copy(bf16[32,2,64,256]{2,3,0,1:T(8,128)(2,1)} %bitcast.56) | data formatting | bytes 4194304 | tf_op jit(solution)/shard_map/cond/branch_0_fun/transpose | solution.py:287
  13.9 3.2 pad_maximum_fusion.2
  17.1 11.3 %all-to-all-start.10 = ((bf16[32,144,256]{2,1,0:T(8,128)(2,1)}), bf16[32,144,256]{2,1,0:T(8,128)(2,1)}, u32[]{:S(2)}, u32[]{:S(2)}) async-start(bf16[32,144,256]{2,1,0:T(8,128)(2,1)} %pad_maximum_fusion.2), calls=%async_computation.10 | async-start | bytes 4718592 | tf_op jit(solution)/shard_map/cond/branch_0_fun/all_to_all | solution.py:229
  28.4 4.2 %fusion = bf16[8192,256]{1,0:T(8,128)(2,1)} fusion(bf16[1,8192,256]{2,1,0:T(8,128)(2,1)} %get-tuple-element.192, f32[8192]{0:T(1024)S(1)} %bitcast.58), kind=kLoop, calls=%fused_computation.5 | loop fusion | flops 6291456 | bytes 8421376 | tf_op jit(solution)/shard_map/cond/branch_0_fun/convert_element_type | solution.py:291
  32.6 50.2 %all-to-all-done.10 = bf16[32,144,256]{2,1,0:T(8,128)(2,1)} async-done(((bf16[32,144,256]{2,1,0:T(8,128)(2,1)}), bf16[32,144,256]{2,1,0:T(8,128)(2,1)}, u32[]{:S(2)}, u32[]{:S(2)}) %all-to-all-start.10) | async-done | bytes 2359328 | tf_op jit(solution)/shard_map/cond/branch_0_fun/all_to_all | solution.py:229
  84.5 1.7 slice.30
  86.2 1.9 fusion.1
  88.8 1.4 broadcast_select_fusion
  95.7 1.3 collective-permute-start.8
  97.0 192.0 %collective-permute-done.8 = bf16[64,256]{1,0:T(8,128)(2,1)S(1)} collective-permute-done((bf16[64,256]{1,0:T(8,128)(2,1)S(1)}, bf16[64,256]{1,0:T(8,128)(2,1)S(1)}, u32[]{:S(2)}, u32[]{:S(2)}) %collective-permute-start.8) | collective-permute-done | bytes 32800 | tf_op jit(solution)/shard_map/ppermute | solution.py:342
  289.0 31.2 %conditional.21 = (bf16[64,256]{1,0:T(8,128)(2,1)S(1)}) conditional(s32[]{:T(128)} %convert_element_type.55, () %tuple.83, (bf16[64,256]{1,0:T(8,128)(2,1)S(1)}, f32[64,128]{1,0:T(8,128)S(1)}, bf16[4096,256]{1,0:T(8,128)(2,1)}, bf16[8192,256]{1,0:T(8,128)(2,1)}, bf16[4096,256]{1,0:T(8,128)(2,1)S(1)}) %tuple.150), branch_computations={%region_21.22_spmd, %region_22.23_spmd} | conditional | bytes 3973128 | solution.py:358
  289.0 2.8 branch_1_fun.36
  291.8 25.1 %all_to_all.60.refs_1_ = bf16[32,80,256]{2,1,0:T(8,128)(2,1)S(1)} all-to-all(bf16[32,80,256]{2,1,0:T(8,128)(2,1)S(1)} %broadcast_in_dim.43), channel_id=1, replica_groups=mesh['segment'=8,'adapter'=32] {'adapter'}, dimensions={0} | all-to-all | bytes 2621440 | tf_op jit(solution)/shard_map/cond/branch_1_fun/all_to_all | solution.py:229
  316.9 3.2 branch_1_fun.37
  320.1 1.3 collective-permute-start.9
  321.4 15.4 %collective-permute-done.9 = bf16[64,256]{1,0:T(8,128)(2,1)S(1)} collective-permute-done((bf16[64,256]{1,0:T(8,128)(2,1)S(1)}, bf16[64,256]{1,0:T(8,128)(2,1)S(1)}, u32[]{:S(2)}, u32[]{:S(2)}) %collective-permute-start.9) | collective-permute-done | bytes 32800 | tf_op jit(solution)/shard_map/ppermute | solution.py:342
  336.8 31.2 %conditional.22 = (bf16[64,256]{1,0:T(8,128)(2,1)S(1)}) conditional(s32[]{:T(128)} %convert_element_type.54, () %tuple.82, (bf16[64,256]{1,0:T(8,128)(2,1)S(1)}, f32[64,128]{1,0:T(8,128)S(1)}, bf16[4096,256]{1,0:T(8,128)(2,1)}, bf16[8192,256]{1,0:T(8,128)(2,1)}, bf16[4096,256]{1,0:T(8,128)(2,1)S(1)}) %tuple.151), branch_computations={%region_23.24_spmd, %region_24.25_spmd} | conditional | bytes 3973128 | solution.py:358
  336.8 2.8 branch_1_fun.38
  339.7 25.1 %all_to_all.61.refs_1_ = bf16[32,80,256]{2,1,0:T(8,128)(2,1)S(1)} all-to-all(bf16[32,80,256]{2,1,0:T(8,128)(2,1)S(1)} %broadcast_in_dim.44), channel_id=1, replica_groups=mesh['segment'=8,'adapter'=32] {'adapter'}, dimensions={0} | all-to-all | bytes 2621440 | tf_op jit(solution)/shard_map/cond/branch_1_fun/all_to_all | solution.py:229
  364.8 3.2 branch_1_fun.39
  (65 shorter events, 12.1 us)
Async XLA Ops:
  1.4 2.8 copy-start
  1.4 2.8 copy-start.1
  2.5 89.2 %collective-permute-start.1 = (bf16[64,8320]{1,0:T(8,128)(2,1)}, bf16[64,8320]{1,0:T(8,128)(2,1)}, u32[]{:S(2)}, u32[]{:S(2)}) collective-permute-start(bf16[64,8320]{1,0:T(8,128)(2,1)} %get-tuple-element.305), channel_id=1, source_target_pairs={{64,0},{65,1},{66,2},{67,3},{68,4},{69,5},{70,6},{71,7},{72,8},{73... | collective-permute-start | bytes 3194888 | tf_op jit(solution)/shard_map/ppermute | solution.py:337
  17.1 65.7 %all-to-all-start.10 = ((bf16[32,144,256]{2,1,0:T(8,128)(2,1)}), bf16[32,144,256]{2,1,0:T(8,128)(2,1)}, u32[]{:S(2)}, u32[]{:S(2)}) async-start(bf16[32,144,256]{2,1,0:T(8,128)(2,1)} %pad_maximum_fusion.2), calls=%async_computation.10 | async-start | bytes 4718592 | tf_op jit(solution)/shard_map/cond/branch_0_fun/all_to_all | solution.py:229
  88.1 2.1 copy-start.8
  88.1 2.1 collective-permute-start
  90.2 0.6 copy-start.7
  91.0 0.7 collective-permute-start.2
  91.9 0.7 collective-permute-start.3
  92.6 0.8 copy-start.5
  92.6 0.7 collective-permute-start.4
  93.3 0.8 copy-start.4
  93.3 0.7 collective-permute-start.5
  94.1 0.8 copy-start.3
  94.1 0.7 collective-permute-start.6
  94.8 0.8 copy-start.2
  94.8 0.8 collective-permute-start.7
  95.7 193.3 %collective-permute-start.8 = (bf16[64,256]{1,0:T(8,128)(2,1)S(1)}, bf16[64,256]{1,0:T(8,128)(2,1)S(1)}, u32[]{:S(2)}, u32[]{:S(2)}) collective-permute-start(bf16[64,256]{1,0:T(8,128)(2,1)S(1)} %get-tuple-element.312), channel_id=1, source_target_pairs={{192,224},{160,192},{193,225},{161,193},{194,226},{162,194},{195,2... | collective-permute-start | bytes 98312 | tf_op jit(solution)/shard_map/ppermute | solution.py:342
  320.1 16.7 %collective-permute-start.9 = (bf16[64,256]{1,0:T(8,128)(2,1)S(1)}, bf16[64,256]{1,0:T(8,128)(2,1)S(1)}, u32[]{:S(2)}, u32[]{:S(2)}) collective-permute-start(bf16[64,256]{1,0:T(8,128)(2,1)S(1)} %get-tuple-element.313), channel_id=1, source_target_pairs={{192,224},{193,225},{194,226},{195,227},{196,228},{197,229},{198,2... | collective-permute-start | bytes 98312 | tf_op jit(solution)/shard_map/ppermute | solution.py:342
  336.8 31.2 %copy-start.9 = (bf16[64,256]{1,0:T(8,128)(2,1)S(1)}, bf16[64,256]{1,0:T(8,128)(2,1)}, u32[]{:S(2)}) copy-start(bf16[64,256]{1,0:T(8,128)(2,1)} %copy-done.8) | copy-start | bytes 98308

commit v7 on v6

--- a/solution.py
+++ b/solution.py
@@ -44,9 +44,10 @@
 
 
 def fetches(source, target, sems, axis=0):
-    size = source.shape[axis] // CHUNKS
+    pieces = sems.shape[0]
+    size = source.shape[axis] // pieces
     copies = []
-    for c in range(CHUNKS):
+    for c in range(pieces):
         part = (slice(None),) * axis + (pl.ds(c * size, size),)
         copies.append(pltpu.make_async_copy(source.at[part], target.at[part], sems.at[c]))
     for copy in copies:
@@ -111,15 +112,14 @@
     sent_out[...] = fold(rank_most, jnp.concatenate([low] * (cols // held), axis=1), cols)
 
 
-def finish(rank_most, h_ref, base, low, ids, expand_ref, out_ref):
+def finish(rank_most, h_ref, base, low, ids, expand_ref, out_ref, start=0):
     rows, cols = h_ref.shape
     wanted = ids - lane_group((rows, cols), rank_most).astype(jnp.float32)
     added = jnp.zeros((rows, cols), jnp.float32)
-    for j in range(expand_ref.shape[0] // cols):
+    for j in range((expand_ref.shape[0] - start) // cols):
         picked = jnp.where(wanted == j * GROUP, low, 0.0).astype(jnp.bfloat16)
-        added = added + jnp.dot(
-            picked, expand_ref[j * cols : (j + 1) * cols, :], preferred_element_type=jnp.float32
-        )
+        part = slice(start + j * cols, start + (j + 1) * cols)
+        added = added + jnp.dot(picked, expand_ref[part, :], preferred_element_type=jnp.float32)
     update = (base + added).astype(jnp.bfloat16)
     out_ref[...] = (h_ref[...].astype(jnp.float32) + update.astype(jnp.float32)).astype(
         jnp.bfloat16
@@ -137,19 +137,13 @@
     finish(rank_most, h_ref, base_ref[...], low, ids, expand_ref, out_ref)
 
 
-def before_kernel(
-    rank_most, h_ref, table_ref, shrink_hbm, out_ref, shrink_ref, sems
-):
+def before_kernel(rank_most, h_ref, table_ref, shrink_ref, out_ref):
     rows, cols = h_ref.shape
-    copies = fetches(shrink_hbm, shrink_ref, sems)
     h = h_ref[...]
     ids, _ = ids_and_rank(table_ref)
     wanted = ids - lane_group((rows, cols), rank_most).astype(jnp.float32)
     total = jnp.zeros((rows, cols), jnp.float32)
-    steps = shrink_ref.shape[0] // cols
-    for j in range(steps):
-        if j % (steps // CHUNKS) == 0:
-            copies[j // (steps // CHUNKS)].wait()
+    for j in range(shrink_ref.shape[0] // cols):
         part = lax.dot_general(
             h,
             shrink_ref[j * cols : (j + 1) * cols, :],
@@ -162,10 +156,10 @@
 
 
 def after_kernel(
-    rank_most, h_ref, got_ref, table_ref, base_hbm, expand_ref, out_ref, base_ref, sems
+    rank_most, h_ref, got_ref, table_ref, wide_hbm, out_ref, wide_ref, sems
 ):
     rows, cols = h_ref.shape
-    copies = fetches(base_hbm, base_ref, sems)
+    copies = fetches(wide_hbm, wide_ref, sems)
     sources = got_ref.shape[0]
     base = jnp.zeros((rows, cols), jnp.float32)
     squares = jnp.zeros((rows, cols), jnp.float32)
@@ -175,7 +169,7 @@
             copies[j // (sources // CHUNKS)].wait()
         block = got_ref[j, :rows, :]
         base = base + jnp.dot(
-            block, base_ref[j * cols : (j + 1) * cols, :], preferred_element_type=jnp.float32
+            block, wide_ref[j * cols : (j + 1) * cols, :], preferred_element_type=jnp.float32
         )
         wide = block.astype(jnp.float32)
         squares = squares + wide * wide
@@ -183,7 +177,9 @@
     inverse = inverse_rms(squares, sources * cols)
     ids, rank = ids_and_rank(table_ref)
     low = unfold(rank_most, partial) * inverse * scaling(rank_most, rank, (rows, cols))
-    finish(rank_most, h_ref, base * inverse, low, ids, expand_ref, out_ref)
+    for copy in copies[CHUNKS:]:
+        copy.wait()
+    finish(rank_most, h_ref, base * inverse, low, ids, wide_ref, out_ref, sources * cols)
 
 
 def unused_kernel(rank_most, *refs):
@@ -204,6 +200,7 @@
     packed = rows // GROUP
     held = ad_count * rank_most
     all_held = total_adapters * rank_most
+    wide_rows = model_width + all_held
     gain_row = gain[0]
     expand = expand_weight[0].reshape(all_held, cols)
     maps = shrink_weight[0].transpose(0, 2, 1).reshape(held, model_width)
@@ -277,10 +274,10 @@
     def open_first(hidden):
         table, next_table = tables(hidden[:, model_width:])
         h = first_layer(hidden, table, hidden)
-        shrink, base = call(
-            unused_kernel, [((all_held, cols), half), ((model_width, cols), half)]
-        )
-        return h, table, next_table, shrink, base
+        shrink, wide = call(
+            unused_kernel, [((all_held, cols), half), ((wide_rows, cols), half)]
+        )
+        return h, table, next_table, shrink, wide
 
     def open_other(hidden):
         by_dest = shrink_weight[0].reshape(ad_count, devices, cols, rank_most)
@@ -289,11 +286,12 @@
         extra = jnp.broadcast_to(extra, (devices, 16, cols))
         got = exchange(jnp.concatenate([by_dest, extra], axis=1))
         base = (base_weight[0].astype(full) * gain_row[:, None]).astype(half)
+        wide = jnp.concatenate([base, expand], axis=0)
         table, next_table = tables(got[:, held : held + own_rows, :LANES].reshape(rows, LANES))
         shrink = got[:, :held].reshape(all_held, cols)
         own_gain = lax.dynamic_slice_in_dim(gain_row, owner * cols, cols, 0)
         shrink = (shrink.astype(full) * own_gain[None, :]).astype(half)
-        return jnp.zeros((rows, cols), half), table, next_table, shrink, base
+        return jnp.zeros((rows, cols), half), table, next_table, shrink, wide
 
     block_shape = (devices, rows + packed, cols)
 
@@ -304,22 +302,22 @@
             h,
             table,
             shrink,
-            specs=[vmem, vmem, hbm],
-            scratch=[pltpu.VMEM((all_held, cols), half), fetched],
         )
         return gather(sent)
 
-    def project(h, got, table, base):
+    def project(h, got, table, wide):
         return call(
             after_kernel,
             [state],
             h,
             got,
             table,
-            base,
-            expand,
-            specs=[vmem, vmem, vmem, hbm, vmem],
-            scratch=[pltpu.VMEM((model_width, cols), half), fetched],
+            wide,
+            specs=[vmem, vmem, vmem, hbm],
+            scratch=[
+                pltpu.VMEM((wide_rows, cols), half),
+                pltpu.SemaphoreType.DMA((wide_rows * CHUNKS // model_width,)),
+            ],
         )[0]
 
     def nothing():
@@ -335,7 +333,7 @@
         ),
     )
     later = lax.ppermute(hidden, "segment", [(2, 0)])
-    h, table, next_table, shrink, base = lax.cond(segment == 0, open_first, open_other, hidden)
+    h, table, next_table, shrink, wide = lax.cond(segment == 0, open_first, open_other, hidden)
     outs = [h, h]
     for stage in range(1, segments + 1):
         pairs = [(s, s + 1) for s in (stage - 1, stage - 2) if 0 <= s < segments - 1]
@@ -352,12 +350,12 @@
             branch = jnp.where(trails, 2, jnp.where(leads, 1, 0))
             h = lax.switch(
                 branch,
-                (nothing, lambda: project(h, got, now, base), lambda: first_layer(later, now, over)),
+                (nothing, lambda: project(h, got, now, wide), lambda: first_layer(later, now, over)),
             )
         else:
             h = lax.cond(
                 leads | trails,
-                lambda: project(h, spread_out(h, now, shrink), now, base),
+                lambda: project(h, spread_out(h, now, shrink), now, wide),
                 nothing,
             )
         outs = [jnp.where(leads, h, outs[0]), jnp.where(trails, h, outs[1])]

time: 370 us -> 355 us (0.959)
  waiting for transfers between devices: 258 us -> 236 us
  other arithmetic: 12.8 us -> 27.5 us
  local copies, waits for them, and re-layouts: 14.4 us -> 9.28 us
    concatenate x0 -> x1, other arithmetic: none -> 18.8 us  [open_other(): wide = jnp.concatenate([base, expand], axis=0)]
    all_to_all x1, waiting for transfers between devices: 50.2 us -> 32.4 us  [exchange(): return lax.all_to_all(blocks, 'adapter', 0, 0, tiled=True)]
    ppermute x8, waiting for transfers between devices: 207 us -> 203 us  [on_device(): h = lax.ppermute(h, 'segment', pairs)]
  transfers between devices with their start and end apart: 11 -> 11, of which waited for: 3 -> 3; matrix products, arithmetic and copies ran while one was open for 6% -> 9% of each run, Pallas kernels for 0% -> 0%
where the time goes in v7:
time: 355 us; the launch traced here: 354 us
  waiting for transfers between devices  236 us (66%)
  blocking collectives  50.2 us (14%)
  other arithmetic  27.5 us (8%)
  starting transfers between devices  20.2 us (6%)
  Pallas kernels  9.73 us (3%)
  local copies, waits for them, and re-layouts  9.28 us (3%)
    ppermute x8, waiting for transfers between devices, on_device(): h = lax.ppermute(h, 'segment', pairs)  203 us
    all_to_all x2, blocking collectives, exchange(): return lax.all_to_all(blocks, 'adapter', 0, 0, tiled=True)  50.2 us
    all_to_all x1, waiting for transfers between devices, exchange(): return lax.all_to_all(blocks, 'adapter', 0, 0, tiled=True)  32.4 us
    concatenate x1, other arithmetic, open_other(): wide = jnp.concatenate([base, expand], axis=0)  18.8 us
    all_to_all x1, starting transfers between devices, exchange(): return lax.all_to_all(blocks, 'adapter', 0, 0, tiled=True)  11.4 us
    pallas_call x5, Pallas kernels, call(): pl.pallas_call(lambda *refs: kernel(rank_most, *refs), out_shape=[jax.Sha...  9.73 us
  transfers between devices with their start and end apart: 11, of which 3 were waited for; matrix products, arithmetic and copies ran while one was open for 9% of the time, Pallas kernels for 0%

profile of v7, /device:TPU:7, one launch (start us, length us, event | category | flops | bytes accessed | tf_op | source)
XLA Modules:
  0.0 353.9 jit_solution(9892220895656135115)
XLA Ops:
  1.4 1.1 conditional.12
  1.4 1.1 conditional
  1.4 1.1 broadcast.23
  2.5 1.6 collective-permute-start.1
  4.1 76.1 %conditional.13 = (bf16[64,256]{1,0:T(8,128)(2,1)S(1)}, f32[64,128]{1,0:T(8,128)}, f32[64,128]{1,0:T(8,128)S(1)}, bf16[4096,256]{1,0:T(8,128)(2,1)S(1)}, bf16[12288,256]{1,0:T(8,128)(2,1)}) conditional(s32[]{:T(128)} %convert_element_type.61, (bf16[1,2,8192,64]{2,3,1,0:T(8,128)(2,1)S(1)}, bf16[2,128]{0,1:T(8,128)(2,1)S(1)}, s32[]{:T(128)}, ...), branch_computations={%region_4.5_spmd, %region_5.6_spmd} | conditional | flops 26738692 | bytes 58315416 | solution.py:336
  4.1 3.2 copy.11
  7.3 3.5 %copy.8 = bf16[32,2,64,256]{3,2,1,0:T(8,128)(2,1)S(1)} copy(bf16[32,2,64,256]{2,3,0,1:T(8,128)(2,1)} %bitcast.49) | data formatting | bytes 4194304 | tf_op jit(solution)/shard_map/cond/branch_0_fun/transpose | solution.py:284
  11.0 1.6 pad_maximum_fusion.3
  12.6 11.4 %all-to-all-start.10 = ((bf16[32,144,256]{2,1,0:T(8,128)(2,1)}), bf16[32,144,256]{2,1,0:T(8,128)(2,1)S(1)}, u32[]{:S(2)}, u32[]{:S(2)}) async-start(bf16[32,144,256]{2,1,0:T(8,128)(2,1)} %pad_maximum_fusion.3), calls=%async_computation.10 | async-start | bytes 4718592 | tf_op jit(solution)/shard_map/cond/branch_0_fun/all_to_all | solution.py:226
  24.1 3.0 fusion
  27.1 18.8 %pad_maximum_fusion.2 = bf16[12288,256]{1,0:T(8,128)(2,1)} fusion(bf16[4096,256]{1,0:T(8,128)(2,1)S(1)} %copy-done.1, bf16[8192,256]{1,0:T(8,128)(2,1)S(1)} %fusion), kind=kLoop, calls=%fused_computation.6 | loop fusion | flops 12582912 | bytes 12582912 | tf_op jit(solution)/shard_map/cond/branch_0_fun/concatenate | solution.py:289
  45.9 32.4 %all-to-all-done.10 = bf16[32,144,256]{2,1,0:T(8,128)(2,1)S(1)} async-done(((bf16[32,144,256]{2,1,0:T(8,128)(2,1)}), bf16[32,144,256]{2,1,0:T(8,128)(2,1)S(1)}, u32[]{:S(2)}, u32[]{:S(2)}) %all-to-all-start.10) | async-done | bytes 2359328 | tf_op jit(solution)/shard_map/cond/branch_0_fun/all_to_all | solution.py:226
  80.9 1.4 broadcast_select_fusion
  87.7 1.3 collective-permute-start.8
  89.1 187.8 %collective-permute-done.8 = bf16[64,256]{1,0:T(8,128)(2,1)S(1)} collective-permute-done((bf16[64,256]{1,0:T(8,128)(2,1)S(1)}, bf16[64,256]{1,0:T(8,128)(2,1)S(1)}, u32[]{:S(2)}, u32[]{:S(2)}) %collective-permute-start.8) | collective-permute-done | bytes 32800 | tf_op jit(solution)/shard_map/ppermute | solution.py:340
  276.8 29.6 %conditional.21 = (bf16[64,256]{1,0:T(8,128)(2,1)S(1)}) conditional(s32[]{:T(128)} %convert_element_type.55, () %tuple.83, (bf16[64,256]{1,0:T(8,128)(2,1)S(1)}, f32[64,128]{1,0:T(8,128)S(1)}, bf16[4096,256]{1,0:T(8,128)(2,1)S(1)}, bf16[12288,256]{1,0:T(8,128)(2,1)}) %tuple.103), branch_computations={%region_21.22_spmd, %region_22.23_spmd} | conditional | bytes 3973128 | solution.py:356
  276.8 0.8 branch_1_fun.36
  277.7 25.1 %all_to_all.60.refs_1_ = bf16[32,80,256]{2,1,0:T(8,128)(2,1)S(1)} all-to-all(bf16[32,80,256]{2,1,0:T(8,128)(2,1)S(1)} %broadcast_in_dim.43), channel_id=1, replica_groups=mesh['segment'=8,'adapter'=32] {'adapter'}, dimensions={0} | all-to-all | bytes 2621440 | tf_op jit(solution)/shard_map/cond/branch_1_fun/all_to_all | solution.py:226
  302.8 3.6 %branch_1_fun.37 = bf16[64,256]{1,0:T(8,128)(2,1)S(1)} custom-call(bf16[64,256]{1,0:T(8,128)(2,1)S(1)} %get-tuple-element.230.refs_0_, bf16[32,80,256]{2,1,0:T(8,128)(2,1)S(1)} %all_to_all.60.refs_1_, f32[64,128]{1,0:T(8,128)S(1)} %get-tuple-element.231.refs_1_.refs_2_, bf16[12288,256]{1,0:T(8,128)(2,1)} %get-tuple-element.233.refs_3_), custom_call_target="tpu_custom_call" | custom-call | tf_op jit(solution)/shard_map/cond/branch_1_fun/pallas_call | solution.py:216
  306.5 1.3 collective-permute-start.9
  307.8 15.7 %collective-permute-done.9 = bf16[64,256]{1,0:T(8,128)(2,1)S(1)} collective-permute-done((bf16[64,256]{1,0:T(8,128)(2,1)S(1)}, bf16[64,256]{1,0:T(8,128)(2,1)S(1)}, u32[]{:S(2)}, u32[]{:S(2)}) %collective-permute-start.9) | collective-permute-done | bytes 32800 | tf_op jit(solution)/shard_map/ppermute | solution.py:340
  323.5 29.7 %conditional.22 = (bf16[64,256]{1,0:T(8,128)(2,1)S(1)}) conditional(s32[]{:T(128)} %convert_element_type.54, () %tuple.82, (bf16[64,256]{1,0:T(8,128)(2,1)S(1)}, f32[64,128]{1,0:T(8,128)S(1)}, bf16[4096,256]{1,0:T(8,128)(2,1)S(1)}, bf16[12288,256]{1,0:T(8,128)(2,1)}) %tuple.104), branch_computations={%region_23.24_spmd, %region_24.25_spmd} | conditional | bytes 3973128 | solution.py:356
  324.4 25.1 %all_to_all.61.refs_1_ = bf16[32,80,256]{2,1,0:T(8,128)(2,1)S(1)} all-to-all(bf16[32,80,256]{2,1,0:T(8,128)(2,1)S(1)} %broadcast_in_dim.44), channel_id=1, replica_groups=mesh['segment'=8,'adapter'=32] {'adapter'}, dimensions={0} | all-to-all | bytes 2621440 | tf_op jit(solution)/shard_map/cond/branch_1_fun/all_to_all | solution.py:226
  349.5 3.6 %branch_1_fun.39 = bf16[64,256]{1,0:T(8,128)(2,1)S(1)} custom-call(bf16[64,256]{1,0:T(8,128)(2,1)S(1)} %get-tuple-element.234.refs_0_, bf16[32,80,256]{2,1,0:T(8,128)(2,1)S(1)} %all_to_all.61.refs_1_, f32[64,128]{1,0:T(8,128)S(1)} %get-tuple-element.235.refs_1_.refs_2_, bf16[12288,256]{1,0:T(8,128)(2,1)} %get-tuple-element.237.refs_3_), custom_call_target="tpu_custom_call" | custom-call | tf_op jit(solution)/shard_map/cond/branch_1_fun/pallas_call | solution.py:216
  (68 shorter events, 10.8 us)
Async XLA Ops:
  1.4 2.7 copy-start
  1.4 2.7 copy-start.2
  2.5 81.3 %collective-permute-start.1 = (bf16[64,8320]{1,0:T(8,128)(2,1)}, bf16[64,8320]{1,0:T(8,128)(2,1)}, u32[]{:S(2)}, u32[]{:S(2)}) collective-permute-start(bf16[64,8320]{1,0:T(8,128)(2,1)} %get-tuple-element.285), channel_id=1, source_target_pairs={{64,0},{65,1},{66,2},{67,3},{68,4},{69,5},{70,6},{71,7},{72,8},{73... | collective-permute-start | bytes 3194888 | tf_op jit(solution)/shard_map/ppermute | solution.py:335
  12.6 65.6 %all-to-all-start.10 = ((bf16[32,144,256]{2,1,0:T(8,128)(2,1)}), bf16[32,144,256]{2,1,0:T(8,128)(2,1)S(1)}, u32[]{:S(2)}, u32[]{:S(2)}) async-start(bf16[32,144,256]{2,1,0:T(8,128)(2,1)} %pad_maximum_fusion.3), calls=%async_computation.10 | async-start | bytes 4718592 | tf_op jit(solution)/shard_map/cond/branch_0_fun/all_to_all | solution.py:226
  24.0 3.0 copy-start.1
  80.2 2.1 copy-start.9
  80.2 2.1 collective-permute-start
  82.3 0.6 copy-start.8
  83.1 0.7 collective-permute-start.2
  83.8 0.7 collective-permute-start.3
  84.5 0.8 copy-start.6
  84.5 0.7 collective-permute-start.4
  85.3 0.8 copy-start.5
  85.3 0.7 collective-permute-start.5
  86.0 1.0 copy-start.4
  86.3 0.7 collective-permute-start.6
  87.0 0.8 copy-start.3
  87.0 0.7 collective-permute-start.7
  87.7 189.1 %collective-permute-start.8 = (bf16[64,256]{1,0:T(8,128)(2,1)S(1)}, bf16[64,256]{1,0:T(8,128)(2,1)S(1)}, u32[]{:S(2)}, u32[]{:S(2)}) collective-permute-start(bf16[64,256]{1,0:T(8,128)(2,1)S(1)} %get-tuple-element.292), channel_id=1, source_target_pairs={{192,224},{160,192},{193,225},{161,193},{194,226},{162,194},{195,2... | collective-permute-start | bytes 98312 | tf_op jit(solution)/shard_map/ppermute | solution.py:340
  306.5 17.0 %collective-permute-start.9 = (bf16[64,256]{1,0:T(8,128)(2,1)S(1)}, bf16[64,256]{1,0:T(8,128)(2,1)S(1)}, u32[]{:S(2)}, u32[]{:S(2)}) collective-permute-start(bf16[64,256]{1,0:T(8,128)(2,1)S(1)} %get-tuple-element.293), channel_id=1, source_target_pairs={{192,224},{193,225},{194,226},{195,227},{196,228},{197,229},{198,2... | collective-permute-start | bytes 98312 | tf_op jit(solution)/shard_map/ppermute | solution.py:340
  323.5 29.7 %copy-start.10 = (bf16[64,256]{1,0:T(8,128)(2,1)S(1)}, bf16[64,256]{1,0:T(8,128)(2,1)}, u32[]{:S(2)}) copy-start(bf16[64,256]{1,0:T(8,128)(2,1)} %copy-done.9) | copy-start | bytes 98308

commit v8 on v7

--- a/solution.py
+++ b/solution.py
@@ -77,8 +77,8 @@
 
 
 def first_kernel(
-    rank_most, hidden_ref, base_hbm, maps_hbm, gain_ref, table_ref, owner_ref, order_hbm,
-    base_out, sent_out, base_ref, maps_ref, base_sems, maps_sems,
+    rank_most, hidden_ref, base_hbm, maps_hbm, gain_ref, table_ref, owner_ref,
+    base_out, low_out, base_ref, maps_ref, base_sems, maps_sems,
 ):
     rows = hidden_ref.shape[0]
     width, cols = base_ref.shape
@@ -108,8 +108,13 @@
     ids, rank = ids_and_rank(table_ref)
     wanted = ids == (first + groups).astype(jnp.float32)
     factor = scaling(rank_most, rank, (rows, held))
-    low = spread(jnp.where(wanted, shrunk * inverse * factor, 0.0), rank_most)
-    sent_out[...] = fold(rank_most, jnp.concatenate([low] * (cols // held), axis=1), cols)
+    low_out[...] = spread(jnp.where(wanted, shrunk * inverse * factor, 0.0), rank_most)
+
+
+def fold_kernel(rank_most, low_ref, order_hbm, out_ref):
+    cols = out_ref.shape[1]
+    low = jnp.concatenate([low_ref[...]] * (cols // low_ref.shape[1]), axis=1)
+    out_ref[...] = fold(rank_most, low, cols)
 
 
 def finish(rank_most, h_ref, base, low, ids, expand_ref, out_ref, start=0):
@@ -127,13 +132,16 @@
 
 
 def first_after_kernel(
-    rank_most, h_ref, got_ref, table_ref, base_ref, expand_ref, out_ref
+    rank_most, h_ref, got_ref, table_ref, base_ref, expand_hbm, out_ref, expand_ref, sems
 ):
+    copies = fetches(expand_hbm, expand_ref, sems)
     partial = jnp.zeros(got_ref.shape[1:], jnp.float32)
     for j in range(got_ref.shape[0]):
         partial = partial + got_ref[j].astype(jnp.float32)
     low = unfold(rank_most, partial)
     ids, _ = ids_and_rank(table_ref)
+    for copy in copies:
+        copy.wait()
     finish(rank_most, h_ref, base_ref[...], low, ids, expand_ref, out_ref)
 
 
@@ -241,18 +249,19 @@
         block = jnp.concatenate([tokens[micro], info], axis=1)
         return gather(block).reshape(rows, model_width + LANES)
 
-    def first_layer(hidden, table, order):
-        base, sent = call(
+    first_shapes = [((rows, cols), full), ((rows, held), full)]
+
+    def first_part(hidden, table):
+        return call(
             first_kernel,
-            [((rows, cols), full), ((packed, cols), half)],
+            first_shapes,
             hidden,
             base_weight[0],
             maps,
             gain,
             table,
             number(owner),
-            order,
-            specs=[vmem, hbm, hbm, vmem, vmem, smem, hbm],
+            specs=[vmem, hbm, hbm, vmem, vmem, smem],
             scratch=[
                 pltpu.VMEM((model_width, cols), half),
                 pltpu.VMEM((held, model_width), half),
@@ -260,6 +269,9 @@
                 fetched,
             ],
         )
+
+    def first_rest(hidden, table, base, low, order):
+        (sent,) = call(fold_kernel, [((packed, cols), half)], low, order, specs=[vmem, hbm])
         own = lax.dynamic_slice_in_dim(hidden, owner * cols, cols, 1)
         return call(
             first_after_kernel,
@@ -269,11 +281,13 @@
             table,
             base,
             expand,
+            specs=[vmem, vmem, vmem, vmem, hbm],
+            scratch=[pltpu.VMEM((all_held, cols), half), fetched],
         )[0]
 
     def open_first(hidden):
         table, next_table = tables(hidden[:, model_width:])
-        h = first_layer(hidden, table, hidden)
+        h = first_rest(hidden, table, *first_part(hidden, table), hidden)
         shrink, wide = call(
             unused_kernel, [((all_held, cols), half), ((wide_rows, cols), half)]
         )
@@ -282,10 +296,11 @@
     def open_other(hidden):
         by_dest = shrink_weight[0].reshape(ad_count, devices, cols, rank_most)
         by_dest = by_dest.transpose(1, 0, 3, 2).reshape(devices, held, cols)
-        extra = jnp.pad(info, ((0, 16 - own_rows), (0, cols - LANES)))
+        base = (base_weight[0].astype(full) * gain_row[:, None]).astype(half)
+        base, head = lax.optimization_barrier((base, info))
+        extra = jnp.pad(head, ((0, 16 - own_rows), (0, cols - LANES)))
         extra = jnp.broadcast_to(extra, (devices, 16, cols))
         got = exchange(jnp.concatenate([by_dest, extra], axis=1))
-        base = (base_weight[0].astype(full) * gain_row[:, None]).astype(half)
         wide = jnp.concatenate([base, expand], axis=0)
         table, next_table = tables(got[:, held : held + own_rows, :LANES].reshape(rows, LANES))
         shrink = got[:, :held].reshape(all_held, cols)
@@ -341,16 +356,28 @@
         leads, trails = segment == stage, segment == stage - 1
         now = lax.optimization_barrier(jnp.where(leads, table, next_table))
         if stage == 1:
-            got = lax.cond(
-                leads,
-                lambda: spread_out(h, now, shrink),
-                lambda: jnp.zeros(block_shape, half),
+            branch = jnp.where(trails, 2, jnp.where(leads, 1, 0))
+
+            def zeros(*shapes):
+                return [jnp.zeros(*shape) for shape in shapes]
+
+            block = (block_shape, half)
+            got, first_base, low = lax.switch(
+                branch,
+                (
+                    lambda: zeros(block, *first_shapes),
+                    lambda: [spread_out(h, now, shrink), *zeros(*first_shapes)],
+                    lambda: [*zeros(block), *first_part(later, now)],
+                ),
             )
             over = lax.ppermute(got[0, :16, :LANES], "segment", [(1, 0)])
-            branch = jnp.where(trails, 2, jnp.where(leads, 1, 0))
             h = lax.switch(
                 branch,
-                (nothing, lambda: project(h, got, now, wide), lambda: first_layer(later, now, over)),
+                (
+                    nothing,
+                    lambda: project(h, got, now, wide),
+                    lambda: first_rest(later, now, first_base, low, over),
+                ),
             )
         else:
             h = lax.cond(

time: 355 us -> 362 us (1.020)
  local copies, waits for them, and re-layouts: 9.28 us -> 14 us
  blocking collectives: 50.2 us -> 54.2 us
    all_to_all x1, waiting for transfers between devices: 32.4 us -> 39.3 us  [exchange(): return lax.all_to_all(blocks, 'adapter', 0, 0, tiled=True)]
    ppermute x8, waiting for transfers between devices: 203 us -> 198 us  [on_device(): h = lax.ppermute(h, 'segment', pairs)]
    concatenate x1, other arithmetic: 18.8 us -> 14.4 us  [open_other(): wide = jnp.concatenate([base, expand], axis=0)]
    all_to_all x2, blocking collectives: 50.2 us -> 54.2 us  [exchange(): return lax.all_to_all(blocks, 'adapter', 0, 0, tiled=True)]
where the time goes in v8:
time: 362 us; the launch traced here: 361 us
  waiting for transfers between devices  238 us (66%)
  blocking collectives  54.2 us (15%)
  other arithmetic  25.2 us (7%)
  starting transfers between devices  19.5 us (5%)
  local copies, waits for them, and re-layouts  14 us (4%)
  Pallas kernels  9.74 us (3%)
    ppermute x8, waiting for transfers between devices, on_device(): h = lax.ppermute(h, 'segment', pairs)  198 us
    all_to_all x2, blocking collectives, exchange(): return lax.all_to_all(blocks, 'adapter', 0, 0, tiled=True)  54.2 us
    all_to_all x1, waiting for transfers between devices, exchange(): return lax.all_to_all(blocks, 'adapter', 0, 0, tiled=True)  39.3 us
    concatenate x1, other arithmetic, open_other(): wide = jnp.concatenate([base, expand], axis=0)  14.4 us
    all_to_all x1, starting transfers between devices, exchange(): return lax.all_to_all(blocks, 'adapter', 0, 0, tiled=True)  11.5 us
    pallas_call x5, Pallas kernels, call(): pl.pallas_call(lambda *refs: kernel(rank_most, *refs), out_shape=[jax.Sha...  9.74 us
  transfers between devices with their start and end apart: 11, of which 3 were waited for; matrix products, arithmetic and copies ran while one was open for 9% of the time, Pallas kernels for 0%

profile of v8, /device:TPU:7, one launch (start us, length us, event | category | flops | bytes accessed | tf_op | source)
XLA Modules:
  0.0 361.0 jit_solution(3927405681878392061)
XLA Ops:
  1.4 1.1 conditional.12
  1.4 1.1 conditional
  1.4 1.1 broadcast.33
  3.3 83.3 %conditional.13 = (bf16[64,256]{1,0:T(8,128)(2,1)}, f32[64,128]{1,0:T(8,128)}, f32[64,128]{1,0:T(8,128)}, bf16[4096,256]{1,0:T(8,128)(2,1)S(1)}, bf16[12288,256]{1,0:T(8,128)(2,1)}) conditional(s32[]{:T(128)} %convert_element_type.58, (bf16[1,2,8192,64]{2,3,1,0:T(8,128)(2,1)S(1)}, bf16[1,8192,256]{2,1,0:T(8,128)(2,1)}, f32[1,8192]{1,0:T(1,128)}, ...), branch_computations={%region_4.5_spmd, %region_5.6_spmd} | conditional | flops 26738692 | bytes 58315416 | solution.py:351
  3.4 4.3 %fusion = bf16[8192,256]{1,0:T(8,128)(2,1)} fusion(bf16[1,8192,256]{2,1,0:T(8,128)(2,1)} %get-tuple-element.178, f32[8192]{0:T(1024)} %bitcast.51), kind=kLoop, calls=%fused_computation.5 | loop fusion | flops 6291456 | bytes 8421376 | tf_op jit(solution)/shard_map/cond/branch_0_fun/convert_element_type | solution.py:299
  7.7 3.2 copy.11
  11.0 3.5 copy.8
  14.6 1.6 pad_maximum_fusion.3
  16.1 11.5 %all-to-all-start.10 = ((bf16[32,144,256]{2,1,0:T(8,128)(2,1)}), bf16[32,144,256]{2,1,0:T(8,128)(2,1)}, u32[]{:S(2)}, u32[]{:S(2)}) async-start(bf16[32,144,256]{2,1,0:T(8,128)(2,1)} %pad_maximum_fusion.3), calls=%async_computation.10 | async-start | bytes 4718592 | tf_op jit(solution)/shard_map/cond/branch_0_fun/all_to_all | solution.py:234
  28.3 14.4 %pad_maximum_fusion.2 = bf16[12288,256]{1,0:T(8,128)(2,1)} fusion(bf16[4096,256]{1,0:T(8,128)(2,1)S(1)} %copy-done.2, bf16[8192,256]{1,0:T(8,128)(2,1)} %fusion), kind=kLoop, calls=%fused_computation.6 | loop fusion | flops 12582912 | bytes 12582912 | tf_op jit(solution)/shard_map/cond/branch_0_fun/concatenate | solution.py:304
  42.7 39.3 %all-to-all-done.10 = bf16[32,144,256]{2,1,0:T(8,128)(2,1)} async-done(((bf16[32,144,256]{2,1,0:T(8,128)(2,1)}), bf16[32,144,256]{2,1,0:T(8,128)(2,1)}, u32[]{:S(2)}, u32[]{:S(2)}) %all-to-all-start.10) | async-done | bytes 2359328 | tf_op jit(solution)/shard_map/cond/branch_0_fun/all_to_all | solution.py:234
  82.0 0.9 slice.29
  83.7 1.7 slice.30
  87.3 1.5 broadcast_select_fusion
  95.3 1.3 collective-permute-start.8
  96.6 186.9 %collective-permute-done.8 = bf16[64,256]{1,0:T(8,128)(2,1)S(1)} collective-permute-done((bf16[64,256]{1,0:T(8,128)(2,1)S(1)}, bf16[64,256]{1,0:T(8,128)(2,1)S(1)}, u32[]{:S(2)}, u32[]{:S(2)}) %collective-permute-start.8) | collective-permute-done | bytes 32800 | tf_op jit(solution)/shard_map/ppermute | solution.py:355
  283.6 33.7 %conditional.21 = (bf16[64,256]{1,0:T(8,128)(2,1)S(1)}) conditional(s32[]{:T(128)} %convert_element_type.52, () %tuple.90, (bf16[64,256]{1,0:T(8,128)(2,1)S(1)}, f32[64,128]{1,0:T(8,128)S(1)}, bf16[4096,256]{1,0:T(8,128)(2,1)S(1)}, bf16[12288,256]{1,0:T(8,128)(2,1)}) %tuple.159), branch_computations={%region_22.23_spmd, %region_23.24_spmd} | conditional | bytes 3973128 | solution.py:383
  284.5 29.1 %all_to_all.60.refs_1_ = bf16[32,80,256]{2,1,0:T(8,128)(2,1)S(1)} all-to-all(bf16[32,80,256]{2,1,0:T(8,128)(2,1)S(1)} %broadcast_in_dim.43), channel_id=1, replica_groups=mesh['segment'=8,'adapter'=32] {'adapter'}, dimensions={0} | all-to-all | bytes 2621440 | tf_op jit(solution)/shard_map/cond/branch_1_fun/all_to_all | solution.py:234
  313.6 3.6 %branch_1_fun.39 = bf16[64,256]{1,0:T(8,128)(2,1)S(1)} custom-call(bf16[64,256]{1,0:T(8,128)(2,1)S(1)} %get-tuple-element.244.refs_0_, bf16[32,80,256]{2,1,0:T(8,128)(2,1)S(1)} %all_to_all.60.refs_1_, f32[64,128]{1,0:T(8,128)S(1)} %get-tuple-element.245.refs_1_.refs_2_, bf16[12288,256]{1,0:T(8,128)(2,1)} %get-tuple-element.247.refs_3_), custom_call_target="tpu_custom_call" | custom-call | tf_op jit(solution)/shard_map/cond/branch_1_fun/pallas_call | solution.py:224
  317.3 1.3 collective-permute-start.9
  318.6 11.3 %collective-permute-done.9 = bf16[64,256]{1,0:T(8,128)(2,1)S(1)} collective-permute-done((bf16[64,256]{1,0:T(8,128)(2,1)S(1)}, bf16[64,256]{1,0:T(8,128)(2,1)S(1)}, u32[]{:S(2)}, u32[]{:S(2)}) %collective-permute-start.9) | collective-permute-done | bytes 32800 | tf_op jit(solution)/shard_map/ppermute | solution.py:355
  329.9 29.6 %conditional.22 = (bf16[64,256]{1,0:T(8,128)(2,1)S(1)}) conditional(s32[]{:T(128)} %convert_element_type.51, () %tuple.89, (bf16[64,256]{1,0:T(8,128)(2,1)S(1)}, f32[64,128]{1,0:T(8,128)S(1)}, bf16[4096,256]{1,0:T(8,128)(2,1)S(1)}, bf16[12288,256]{1,0:T(8,128)(2,1)}) %tuple.158), branch_computations={%region_24.25_spmd, %region_25.26_spmd} | conditional | bytes 3973128 | solution.py:383
  330.8 25.1 %all_to_all.61.refs_1_ = bf16[32,80,256]{2,1,0:T(8,128)(2,1)S(1)} all-to-all(bf16[32,80,256]{2,1,0:T(8,128)(2,1)S(1)} %broadcast_in_dim.44), channel_id=1, replica_groups=mesh['segment'=8,'adapter'=32] {'adapter'}, dimensions={0} | all-to-all | bytes 2621440 | tf_op jit(solution)/shard_map/cond/branch_1_fun/all_to_all | solution.py:234
  355.9 3.6 %branch_1_fun.41 = bf16[64,256]{1,0:T(8,128)(2,1)S(1)} custom-call(bf16[64,256]{1,0:T(8,128)(2,1)S(1)} %get-tuple-element.248.refs_0_, bf16[32,80,256]{2,1,0:T(8,128)(2,1)S(1)} %all_to_all.61.refs_1_, f32[64,128]{1,0:T(8,128)S(1)} %get-tuple-element.249.refs_1_.refs_2_, bf16[12288,256]{1,0:T(8,128)(2,1)} %get-tuple-element.251.refs_3_), custom_call_target="tpu_custom_call" | custom-call | tf_op jit(solution)/shard_map/cond/branch_1_fun/pallas_call | solution.py:224
  (72 shorter events, 16.0 us)
Async XLA Ops:
  1.4 2.0 copy-start
  2.5 86.3 %collective-permute-start.1 = (bf16[64,8320]{1,0:T(8,128)(2,1)}, bf16[64,8320]{1,0:T(8,128)(2,1)S(1)}, u32[]{:S(2)}, u32[]{:S(2)}) collective-permute-start(bf16[64,8320]{1,0:T(8,128)(2,1)} %get-tuple-element.314), channel_id=1, source_target_pairs={{64,0},{65,1},{66,2},{67,3},{68,4},{69,5},{70,6},{71,7},{72,8},{73... | collective-permute-start | bytes 3194888 | tf_op jit(solution)/shard_map/ppermute | solution.py:350
  16.1 12.2 %copy-start.2 = (bf16[4096,256]{1,0:T(8,128)(2,1)S(1)}, bf16[4096,256]{1,0:T(8,128)(2,1)}, u32[]{:S(2)}) copy-start(bf16[4096,256]{1,0:T(8,128)(2,1)} %get-tuple-element.189) | copy-start | bytes 6291460 | tf_op jit(solution)/shard_map/cond
  16.1 65.9 %all-to-all-start.10 = ((bf16[32,144,256]{2,1,0:T(8,128)(2,1)}), bf16[32,144,256]{2,1,0:T(8,128)(2,1)}, u32[]{:S(2)}, u32[]{:S(2)}) async-start(bf16[32,144,256]{2,1,0:T(8,128)(2,1)} %pad_maximum_fusion.3), calls=%async_computation.10 | async-start | bytes 4718592 | tf_op jit(solution)/shard_map/cond/branch_0_fun/all_to_all | solution.py:234
  86.6 2.2 collective-permute-start
  88.8 0.6 copy-start.11
  88.8 1.0 copy-start.3
  90.5 0.7 collective-permute-start.2
  91.2 0.8 copy-start.10
  91.3 0.7 collective-permute-start.3
  92.0 0.8 copy-start.9
  92.0 0.7 collective-permute-start.4
  92.7 0.8 copy-start.8
  92.7 0.7 collective-permute-start.5
  93.5 0.8 copy-start.7
  93.5 0.8 collective-permute-start.6
  94.3 1.0 copy-start.6
  94.6 0.7 collective-permute-start.7
  95.3 188.3 %copy-start.5 = (f32[64,128]{1,0:T(8,128)S(1)}, f32[64,128]{1,0:T(8,128)}, u32[]{:S(2)}) copy-start(f32[64,128]{1,0:T(8,128)} %get-tuple-element.285) | copy-start | bytes 98308
  95.3 188.2 %collective-permute-start.8 = (bf16[64,256]{1,0:T(8,128)(2,1)S(1)}, bf16[64,256]{1,0:T(8,128)(2,1)S(1)}, u32[]{:S(2)}, u32[]{:S(2)}) collective-permute-start(bf16[64,256]{1,0:T(8,128)(2,1)S(1)} %get-tuple-element.320), channel_id=1, source_target_pairs={{192,224},{160,192},{193,225},{161,193},{194,226},{162,194},{195,2... | collective-permute-start | bytes 98312 | tf_op jit(solution)/shard_map/ppermute | solution.py:355
  283.6 46.3 %copy-start.4 = (f32[64,128]{1,0:T(8,128)S(1)}, f32[64,128]{1,0:T(8,128)}, u32[]{:S(2)}) copy-start(f32[64,128]{1,0:T(8,128)} %get-tuple-element.284) | copy-start | bytes 98308
  317.3 12.6 %collective-permute-start.9 = (bf16[64,256]{1,0:T(8,128)(2,1)S(1)}, bf16[64,256]{1,0:T(8,128)(2,1)S(1)}, u32[]{:S(2)}, u32[]{:S(2)}) collective-permute-start(bf16[64,256]{1,0:T(8,128)(2,1)S(1)} %get-tuple-element.321), channel_id=1, source_target_pairs={{192,224},{193,225},{194,226},{195,227},{196,228},{197,229},{198,2... | collective-permute-start | bytes 98312 | tf_op jit(solution)/shard_map/ppermute | solution.py:355

commit v9 on v7

--- a/solution.py
+++ b/solution.py
@@ -6,7 +6,7 @@
 from jax.sharding import PartitionSpec as P
 
 GROUP = 4
-CHUNKS = 8
+CHUNKS = 4
 LANES = 128
 
 
@@ -282,10 +282,11 @@
     def open_other(hidden):
         by_dest = shrink_weight[0].reshape(ad_count, devices, cols, rank_most)
         by_dest = by_dest.transpose(1, 0, 3, 2).reshape(devices, held, cols)
-        extra = jnp.pad(info, ((0, 16 - own_rows), (0, cols - LANES)))
+        base = (base_weight[0].astype(full) * gain_row[:, None]).astype(half)
+        base, head = lax.optimization_barrier((base, info))
+        extra = jnp.pad(head, ((0, 16 - own_rows), (0, cols - LANES)))
         extra = jnp.broadcast_to(extra, (devices, 16, cols))
         got = exchange(jnp.concatenate([by_dest, extra], axis=1))
-        base = (base_weight[0].astype(full) * gain_row[:, None]).astype(half)
         wide = jnp.concatenate([base, expand], axis=0)
         table, next_table = tables(got[:, held : held + own_rows, :LANES].reshape(rows, LANES))
         shrink = got[:, :held].reshape(all_held, cols)

time: 355 us -> 357 us (level)
    all_to_all x1, waiting for transfers between devices: 32.4 us -> 39.9 us  [exchange(): return lax.all_to_all(blocks, 'adapter', 0, 0, tiled=True)]
    ppermute x8, waiting for transfers between devices: 203 us -> 199 us  [on_device(): h = lax.ppermute(h, 'segment', pairs)]
    concatenate x1, other arithmetic: 18.8 us -> 14.5 us  [open_other(): wide = jnp.concatenate([base, expand], axis=0)]
where the time goes in v9:
time: 357 us; the launch traced here: 356 us
  waiting for transfers between devices  239 us (67%)
  blocking collectives  49.7 us (14%)
  other arithmetic  24.4 us (7%)
  starting transfers between devices  20.3 us (6%)
  local copies, waits for them, and re-layouts  11.6 us (3%)
  Pallas kernels  9.69 us (3%)
    ppermute x8, waiting for transfers between devices, on_device(): h = lax.ppermute(h, 'segment', pairs)  199 us
    all_to_all x2, blocking collectives, exchange(): return lax.all_to_all(blocks, 'adapter', 0, 0, tiled=True)  49.7 us
    all_to_all x1, waiting for transfers between devices, exchange(): return lax.all_to_all(blocks, 'adapter', 0, 0, tiled=True)  39.9 us
    concatenate x1, other arithmetic, open_other(): wide = jnp.concatenate([base, expand], axis=0)  14.5 us
    all_to_all x1, starting transfers between devices, exchange(): return lax.all_to_all(blocks, 'adapter', 0, 0, tiled=True)  11.5 us
    pallas_call x5, Pallas kernels, call(): pl.pallas_call(lambda *refs: kernel(rank_most, *refs), out_shape=[jax.Sha...  9.69 us
  transfers between devices with their start and end apart: 11, of which 3 were waited for; matrix products, arithmetic and copies ran while one was open for 9% of the time, Pallas kernels for 0%

profile of v9, /device:TPU:7, one launch (start us, length us, event | category | flops | bytes accessed | tf_op | source)
XLA Modules:
  0.0 355.5 jit_solution(10090492249588047142)
XLA Ops:
  1.4 1.1 conditional.12
  1.4 1.1 conditional
  1.4 1.1 broadcast.23
  2.5 1.6 collective-permute-start.1
  4.1 82.8 %conditional.13 = (bf16[64,256]{1,0:T(8,128)(2,1)S(1)}, f32[64,128]{1,0:T(8,128)}, f32[64,128]{1,0:T(8,128)S(1)}, bf16[4096,256]{1,0:T(8,128)(2,1)S(1)}, bf16[12288,256]{1,0:T(8,128)(2,1)}) conditional(s32[]{:T(128)} %convert_element_type.61, (bf16[1,2,8192,64]{2,3,1,0:T(8,128)(2,1)S(1)}, bf16[1,8192,256]{2,1,0:T(8,128)(2,1)}, ...), branch_computations={%region_4.5_spmd, %region_5.6_spmd} | conditional | flops 26738692 | bytes 58315416 | solution.py:337
  4.2 4.3 %fusion = bf16[8192,256]{1,0:T(8,128)(2,1)} fusion(bf16[1,8192,256]{2,1,0:T(8,128)(2,1)} %get-tuple-element.166, f32[8192]{0:T(1024)S(1)} %bitcast.51), kind=kLoop, calls=%fused_computation.5 | loop fusion | flops 6291456 | bytes 8421376 | tf_op jit(solution)/shard_map/cond/branch_0_fun/convert_element_type | solution.py:285
  8.5 3.2 copy.11
  11.7 3.5 copy.8
  15.3 1.6 pad_maximum_fusion.3
  16.9 11.5 %all-to-all-start.10 = ((bf16[32,144,256]{2,1,0:T(8,128)(2,1)}), bf16[32,144,256]{2,1,0:T(8,128)(2,1)}, u32[]{:S(2)}, u32[]{:S(2)}) async-start(bf16[32,144,256]{2,1,0:T(8,128)(2,1)} %pad_maximum_fusion.3), calls=%async_computation.10 | async-start | bytes 4718592 | tf_op jit(solution)/shard_map/cond/branch_0_fun/all_to_all | solution.py:226
  28.4 14.5 %pad_maximum_fusion.2 = bf16[12288,256]{1,0:T(8,128)(2,1)} fusion(bf16[4096,256]{1,0:T(8,128)(2,1)S(1)} %copy-done.1, bf16[8192,256]{1,0:T(8,128)(2,1)} %fusion), kind=kLoop, calls=%fused_computation.6 | loop fusion | flops 12582912 | bytes 12582912 | tf_op jit(solution)/shard_map/cond/branch_0_fun/concatenate | solution.py:290
  42.8 39.9 %all-to-all-done.10 = bf16[32,144,256]{2,1,0:T(8,128)(2,1)} async-done(((bf16[32,144,256]{2,1,0:T(8,128)(2,1)}), bf16[32,144,256]{2,1,0:T(8,128)(2,1)}, u32[]{:S(2)}, u32[]{:S(2)}) %all-to-all-start.10) | async-done | bytes 2359328 | tf_op jit(solution)/shard_map/cond/branch_0_fun/all_to_all | solution.py:226
  84.4 1.7 slice.30
  87.7 1.4 broadcast_select_fusion
  94.5 1.3 collective-permute-start.8
  95.8 182.6 %collective-permute-done.8 = bf16[64,256]{1,0:T(8,128)(2,1)S(1)} collective-permute-done((bf16[64,256]{1,0:T(8,128)(2,1)S(1)}, bf16[64,256]{1,0:T(8,128)(2,1)S(1)}, u32[]{:S(2)}, u32[]{:S(2)}) %collective-permute-start.8) | collective-permute-done | bytes 32800 | tf_op jit(solution)/shard_map/ppermute | solution.py:341
  278.4 29.6 %conditional.21 = (bf16[64,256]{1,0:T(8,128)(2,1)S(1)}) conditional(s32[]{:T(128)} %convert_element_type.55, () %tuple.84, (bf16[64,256]{1,0:T(8,128)(2,1)S(1)}, f32[64,128]{1,0:T(8,128)S(1)}, bf16[4096,256]{1,0:T(8,128)(2,1)S(1)}, bf16[12288,256]{1,0:T(8,128)(2,1)}) %tuple.104), branch_computations={%region_21.22_spmd, %region_22.23_spmd} | conditional | bytes 3973128 | solution.py:357
  279.3 25.1 %all_to_all.60.refs_1_ = bf16[32,80,256]{2,1,0:T(8,128)(2,1)S(1)} all-to-all(bf16[32,80,256]{2,1,0:T(8,128)(2,1)S(1)} %broadcast_in_dim.43), channel_id=1, replica_groups=mesh['segment'=8,'adapter'=32] {'adapter'}, dimensions={0} | all-to-all | bytes 2621440 | tf_op jit(solution)/shard_map/cond/branch_1_fun/all_to_all | solution.py:226
  304.4 3.6 %branch_1_fun.37 = bf16[64,256]{1,0:T(8,128)(2,1)S(1)} custom-call(bf16[64,256]{1,0:T(8,128)(2,1)S(1)} %get-tuple-element.232.refs_0_, bf16[32,80,256]{2,1,0:T(8,128)(2,1)S(1)} %all_to_all.60.refs_1_, f32[64,128]{1,0:T(8,128)S(1)} %get-tuple-element.233.refs_1_.refs_2_, bf16[12288,256]{1,0:T(8,128)(2,1)} %get-tuple-element.235.refs_3_), custom_call_target="tpu_custom_call" | custom-call | tf_op jit(solution)/shard_map/cond/branch_1_fun/pallas_call | solution.py:216
  308.0 1.3 collective-permute-start.9
  309.3 16.3 %collective-permute-done.9 = bf16[64,256]{1,0:T(8,128)(2,1)S(1)} collective-permute-done((bf16[64,256]{1,0:T(8,128)(2,1)S(1)}, bf16[64,256]{1,0:T(8,128)(2,1)S(1)}, u32[]{:S(2)}, u32[]{:S(2)}) %collective-permute-start.9) | collective-permute-done | bytes 32800 | tf_op jit(solution)/shard_map/ppermute | solution.py:341
  325.6 29.2 %conditional.22 = (bf16[64,256]{1,0:T(8,128)(2,1)S(1)}) conditional(s32[]{:T(128)} %convert_element_type.54, () %tuple.83, (bf16[64,256]{1,0:T(8,128)(2,1)S(1)}, f32[64,128]{1,0:T(8,128)S(1)}, bf16[4096,256]{1,0:T(8,128)(2,1)S(1)}, bf16[12288,256]{1,0:T(8,128)(2,1)}) %tuple.105), branch_computations={%region_23.24_spmd, %region_24.25_spmd} | conditional | bytes 3973128 | solution.py:357
  326.5 24.7 %all_to_all.61.refs_1_ = bf16[32,80,256]{2,1,0:T(8,128)(2,1)S(1)} all-to-all(bf16[32,80,256]{2,1,0:T(8,128)(2,1)S(1)} %broadcast_in_dim.44), channel_id=1, replica_groups=mesh['segment'=8,'adapter'=32] {'adapter'}, dimensions={0} | all-to-all | bytes 2621440 | tf_op jit(solution)/shard_map/cond/branch_1_fun/all_to_all | solution.py:226
  351.2 3.6 %branch_1_fun.39 = bf16[64,256]{1,0:T(8,128)(2,1)S(1)} custom-call(bf16[64,256]{1,0:T(8,128)(2,1)S(1)} %get-tuple-element.236.refs_0_, bf16[32,80,256]{2,1,0:T(8,128)(2,1)S(1)} %all_to_all.61.refs_1_, f32[64,128]{1,0:T(8,128)S(1)} %get-tuple-element.237.refs_1_.refs_2_, bf16[12288,256]{1,0:T(8,128)(2,1)} %get-tuple-element.239.refs_3_), custom_call_target="tpu_custom_call" | custom-call | tf_op jit(solution)/shard_map/cond/branch_1_fun/pallas_call | solution.py:216
  (68 shorter events, 12.2 us)
Async XLA Ops:
  1.4 2.8 copy-start
  1.4 2.8 copy-start.2
  2.5 88.0 %collective-permute-start.1 = (bf16[64,8320]{1,0:T(8,128)(2,1)}, bf16[64,8320]{1,0:T(8,128)(2,1)}, u32[]{:S(2)}, u32[]{:S(2)}) collective-permute-start(bf16[64,8320]{1,0:T(8,128)(2,1)} %get-tuple-element.287), channel_id=1, source_target_pairs={{64,0},{65,1},{66,2},{67,3},{68,4},{69,5},{70,6},{71,7},{72,8},{73... | collective-permute-start | bytes 3194888 | tf_op jit(solution)/shard_map/ppermute | solution.py:336
  16.9 11.5 %copy-start.1 = (bf16[4096,256]{1,0:T(8,128)(2,1)S(1)}, bf16[4096,256]{1,0:T(8,128)(2,1)}, u32[]{:S(2)}) copy-start(bf16[4096,256]{1,0:T(8,128)(2,1)} %get-tuple-element.182) | copy-start | bytes 6291460 | tf_op jit(solution)/shard_map/cond
  16.9 65.9 %all-to-all-start.10 = ((bf16[32,144,256]{2,1,0:T(8,128)(2,1)}), bf16[32,144,256]{2,1,0:T(8,128)(2,1)}, u32[]{:S(2)}, u32[]{:S(2)}) async-start(bf16[32,144,256]{2,1,0:T(8,128)(2,1)} %pad_maximum_fusion.3), calls=%async_computation.10 | async-start | bytes 4718592 | tf_op jit(solution)/shard_map/cond/branch_0_fun/all_to_all | solution.py:226
  87.0 2.1 copy-start.9
  87.0 2.1 collective-permute-start
  89.1 0.6 copy-start.8
  89.8 0.7 collective-permute-start.2
  90.6 0.7 collective-permute-start.3
  91.2 0.8 copy-start.6
  91.3 0.7 collective-permute-start.4
  92.0 0.8 copy-start.5
  92.0 0.7 collective-permute-start.5
  92.8 0.8 copy-start.4
  92.8 0.7 collective-permute-start.6
  93.5 0.9 copy-start.3
  93.7 0.7 collective-permute-start.7
  94.5 183.9 %collective-permute-start.8 = (bf16[64,256]{1,0:T(8,128)(2,1)S(1)}, bf16[64,256]{1,0:T(8,128)(2,1)S(1)}, u32[]{:S(2)}, u32[]{:S(2)}) collective-permute-start(bf16[64,256]{1,0:T(8,128)(2,1)S(1)} %get-tuple-element.294), channel_id=1, source_target_pairs={{192,224},{160,192},{193,225},{161,193},{194,226},{162,194},{195,2... | collective-permute-start | bytes 98312 | tf_op jit(solution)/shard_map/ppermute | solution.py:341
  308.0 17.6 %collective-permute-start.9 = (bf16[64,256]{1,0:T(8,128)(2,1)S(1)}, bf16[64,256]{1,0:T(8,128)(2,1)S(1)}, u32[]{:S(2)}, u32[]{:S(2)}) collective-permute-start(bf16[64,256]{1,0:T(8,128)(2,1)S(1)} %get-tuple-element.295), channel_id=1, source_target_pairs={{192,224},{193,225},{194,226},{195,227},{196,228},{197,229},{198,2... | collective-permute-start | bytes 98312 | tf_op jit(solution)/shard_map/ppermute | solution.py:341
  325.6 29.2 %copy-start.10 = (bf16[64,256]{1,0:T(8,128)(2,1)S(1)}, bf16[64,256]{1,0:T(8,128)(2,1)}, u32[]{:S(2)}) copy-start(bf16[64,256]{1,0:T(8,128)(2,1)} %copy-done.9) | copy-start | bytes 98308

commit v10 on v9

--- a/solution.py
+++ b/solution.py
@@ -201,6 +201,7 @@
     held = ad_count * rank_most
     all_held = total_adapters * rank_most
     wide_rows = model_width + all_held
+    width = model_width // 2
     gain_row = gain[0]
     expand = expand_weight[0].reshape(all_held, cols)
     maps = shrink_weight[0].transpose(0, 2, 1).reshape(held, model_width)
@@ -237,9 +238,10 @@
     def number(value):
         return jnp.asarray(value, jnp.int32).reshape(1)
 
-    def gather_rows(micro):
-        block = jnp.concatenate([tokens[micro], info], axis=1)
-        return gather(block).reshape(rows, model_width + LANES)
+    def gather_rows(micro, start, width):
+        block = lax.dynamic_slice_in_dim(tokens[micro], start, width, 1)
+        block = jnp.concatenate([block, info], axis=1)
+        return gather(block).reshape(rows, width + LANES)
 
     def first_layer(hidden, table, order):
         base, sent = call(
@@ -271,15 +273,16 @@
             expand,
         )[0]
 
-    def open_first(hidden):
-        table, next_table = tables(hidden[:, model_width:])
+    def open_first(head, rest):
+        table, next_table = tables(head[:, width:])
+        hidden = jnp.concatenate([head[:, :width], rest[:, :width]], axis=1)
         h = first_layer(hidden, table, hidden)
         shrink, wide = call(
             unused_kernel, [((all_held, cols), half), ((wide_rows, cols), half)]
         )
         return h, table, next_table, shrink, wide
 
-    def open_other(hidden):
+    def open_other(head, rest):
         by_dest = shrink_weight[0].reshape(ad_count, devices, cols, rank_most)
         by_dest = by_dest.transpose(1, 0, 3, 2).reshape(devices, held, cols)
         base = (base_weight[0].astype(full) * gain_row[:, None]).astype(half)
@@ -324,17 +327,23 @@
     def nothing():
         return jnp.zeros((rows, cols), half)
 
-    hidden = lax.cond(
-        segment == 0,
-        lambda: gather_rows(0),
-        lambda: lax.cond(
-            segment == 2,
-            lambda: gather_rows(1),
-            lambda: jnp.zeros((rows, model_width + LANES), half),
-        ),
-    )
-    later = lax.ppermute(hidden, "segment", [(2, 0)])
-    h, table, next_table, shrink, wide = lax.cond(segment == 0, open_first, open_other, hidden)
+    def no_rows(width):
+        return jnp.zeros((rows, width + LANES), half)
+
+    sides, beyond = (2, segments - 2), segments // 2
+    side = lax.cond(
+        (segment == sides[0]) | (segment == sides[1]),
+        lambda: gather_rows(0, jnp.where(segment == sides[0], 0, width), width),
+        lambda: no_rows(width),
+    )
+    head, rest = [lax.ppermute(side, "segment", [(s, 0)]) for s in sides]
+    lent = lax.cond(
+        segment == beyond, lambda: gather_rows(1, 0, model_width), lambda: no_rows(model_width)
+    )
+    later = lax.ppermute(lent, "segment", [(beyond, 0)])
+    h, table, next_table, shrink, wide = lax.cond(
+        segment == 0, open_first, open_other, head, rest
+    )
     outs = [h, h]
     for stage in range(1, segments + 1):
         pairs = [(s, s + 1) for s in (stage - 1, stage - 2) if 0 <= s < segments - 1]

time: 357 us -> 374 us (1.048)
  waiting for transfers between devices: 239 us -> 252 us
    ppermute x8, waiting for transfers between devices: 199 us -> 235 us  [on_device(): h = lax.ppermute(h, 'segment', pairs)]
    all_to_all x1, waiting for transfers between devices: 39.9 us -> 16.9 us  [exchange(): return lax.all_to_all(blocks, 'adapter', 0, 0, tiled=True)]
  transfers between devices with their start and end apart: 11 -> 13, of which waited for: 3 -> 3; matrix products, arithmetic and copies ran while one was open for 9% -> 9% of each run, Pallas kernels for 0% -> 0%
where the time goes in v10:
time: 374 us; the launch traced here: 373 us
  waiting for transfers between devices  252 us (67%)
  blocking collectives  50.2 us (13%)
  other arithmetic  25.2 us (7%)
  starting transfers between devices  22.6 us (6%)
  local copies, waits for them, and re-layouts  12.8 us (3%)
  Pallas kernels  9.67 us (3%)
    ppermute x8, waiting for transfers between devices, on_device(): h = lax.ppermute(h, 'segment', pairs)  235 us
    all_to_all x2, blocking collectives, exchange(): return lax.all_to_all(blocks, 'adapter', 0, 0, tiled=True)  50.2 us
    all_to_all x1, waiting for transfers between devices, exchange(): return lax.all_to_all(blocks, 'adapter', 0, 0, tiled=True)  16.9 us
    concatenate x1, other arithmetic, open_other(): wide = jnp.concatenate([base, expand], axis=0)  14.5 us
    all_to_all x1, starting transfers between devices, exchange(): return lax.all_to_all(blocks, 'adapter', 0, 0, tiled=True)  11.5 us
    pallas_call x5, Pallas kernels, call(): pl.pallas_call(lambda *refs: kernel(rank_most, *refs), out_shape=[jax.Sha...  9.67 us
  transfers between devices with their start and end apart: 13, of which 3 were waited for; matrix products, arithmetic and copies ran while one was open for 9% of the time, Pallas kernels for 0%

profile of v10, /device:TPU:7, one launch (start us, length us, event | category | flops | bytes accessed | tf_op | source)
XLA Modules:
  0.0 373.1 jit_solution(11772425166474705447)
XLA Ops:
  1.4 1.1 conditional.15
  1.4 1.0 broadcast.30
  2.4 1.8 collective-permute-start.3
  5.0 1.5 collective-permute-start.1
  6.5 60.2 %conditional.13 = (bf16[64,256]{1,0:T(8,128)(2,1)}, f32[64,128]{1,0:T(8,128)S(1)}, f32[64,128]{1,0:T(8,128)}, bf16[4096,256]{1,0:T(8,128)(2,1)S(1)}, bf16[12288,256]{1,0:T(8,128)(2,1)}) conditional(s32[]{:T(128)} %convert_element_type.63, (bf16[1,2,8192,64]{2,3,1,0:T(8,128)(2,1)S(1)}, bf16[1,8192,256]{2,1,0:T(8,128)(2,1)}, f32[1,8192]{1,0:T(1,128)S(1)}, ...), branch_computations={%region_2.3_spmd, %region_3.4_spmd} | conditional | flops 26738692 | bytes 58315416 | solution.py:344
  6.5 4.3 %fusion = bf16[8192,256]{1,0:T(8,128)(2,1)} fusion(bf16[1,8192,256]{2,1,0:T(8,128)(2,1)} %get-tuple-element.160, f32[8192]{0:T(1024)S(1)} %bitcast.51), kind=kLoop, calls=%fused_computation.3 | loop fusion | flops 6291456 | bytes 8421376 | tf_op jit(solution)/shard_map/cond/branch_0_fun/convert_element_type | solution.py:288
  10.8 3.2 copy.10
  14.0 3.5 copy.8
  17.6 1.6 pad_maximum_fusion.2
  19.2 11.5 %all-to-all-start.9 = ((bf16[32,144,256]{2,1,0:T(8,128)(2,1)}), bf16[32,144,256]{2,1,0:T(8,128)(2,1)}, u32[]{:S(2)}, u32[]{:S(2)}) async-start(bf16[32,144,256]{2,1,0:T(8,128)(2,1)} %pad_maximum_fusion.2), calls=%async_computation.9 | async-start | bytes 4718592 | tf_op jit(solution)/shard_map/cond/branch_0_fun/all_to_all | solution.py:227
  30.7 14.5 %pad_maximum_fusion.1 = bf16[12288,256]{1,0:T(8,128)(2,1)} fusion(bf16[4096,256]{1,0:T(8,128)(2,1)S(1)} %copy-done.3, bf16[8192,256]{1,0:T(8,128)(2,1)} %fusion), kind=kLoop, calls=%fused_computation.4 | loop fusion | flops 12582912 | bytes 12582912 | tf_op jit(solution)/shard_map/cond/branch_0_fun/concatenate | solution.py:293
  45.1 16.9 %all-to-all-done.9 = bf16[32,144,256]{2,1,0:T(8,128)(2,1)} async-done(((bf16[32,144,256]{2,1,0:T(8,128)(2,1)}), bf16[32,144,256]{2,1,0:T(8,128)(2,1)}, u32[]{:S(2)}, u32[]{:S(2)}) %all-to-all-start.9) | async-done | bytes 2359328 | tf_op jit(solution)/shard_map/cond/branch_0_fun/all_to_all | solution.py:227
  63.7 1.7 slice.36
  67.3 1.4 broadcast_select_fusion
  74.6 1.3 collective-permute-start.10
  75.9 219.4 %collective-permute-done.10 = bf16[64,256]{1,0:T(8,128)(2,1)S(1)} collective-permute-done((bf16[64,256]{1,0:T(8,128)(2,1)S(1)}, bf16[64,256]{1,0:T(8,128)(2,1)S(1)}, u32[]{:S(2)}, u32[]{:S(2)}) %collective-permute-start.10) | collective-permute-done | bytes 32800 | tf_op jit(solution)/shard_map/ppermute | solution.py:350
  295.4 29.6 %conditional.22 = (bf16[64,256]{1,0:T(8,128)(2,1)S(1)}) conditional(s32[]{:T(128)} %convert_element_type.57, () %tuple.84, (bf16[64,256]{1,0:T(8,128)(2,1)S(1)}, f32[64,128]{1,0:T(8,128)S(1)}, bf16[4096,256]{1,0:T(8,128)(2,1)S(1)}, bf16[12288,256]{1,0:T(8,128)(2,1)}) %tuple.106), branch_computations={%region_21.22_spmd, %region_22.23_spmd} | conditional | bytes 3973128 | solution.py:366
  296.3 25.1 %all_to_all.60.refs_1_ = bf16[32,80,256]{2,1,0:T(8,128)(2,1)S(1)} all-to-all(bf16[32,80,256]{2,1,0:T(8,128)(2,1)S(1)} %broadcast_in_dim.43), channel_id=1, replica_groups=mesh['segment'=8,'adapter'=32] {'adapter'}, dimensions={0} | all-to-all | bytes 2621440 | tf_op jit(solution)/shard_map/cond/branch_1_fun/all_to_all | solution.py:227
  321.3 3.6 branch_1_fun.37
  325.0 1.3 collective-permute-start.11
  326.3 15.7 %collective-permute-done.11 = bf16[64,256]{1,0:T(8,128)(2,1)S(1)} collective-permute-done((bf16[64,256]{1,0:T(8,128)(2,1)S(1)}, bf16[64,256]{1,0:T(8,128)(2,1)S(1)}, u32[]{:S(2)}, u32[]{:S(2)}) %collective-permute-start.11) | collective-permute-done | bytes 32800 | tf_op jit(solution)/shard_map/ppermute | solution.py:350
  342.0 29.7 %conditional.23 = (bf16[64,256]{1,0:T(8,128)(2,1)S(1)}) conditional(s32[]{:T(128)} %convert_element_type.56, () %tuple.83, (bf16[64,256]{1,0:T(8,128)(2,1)S(1)}, f32[64,128]{1,0:T(8,128)S(1)}, bf16[4096,256]{1,0:T(8,128)(2,1)S(1)}, bf16[12288,256]{1,0:T(8,128)(2,1)}) %tuple.107), branch_computations={%region_23.24_spmd, %region_24.25_spmd} | conditional | bytes 3973128 | solution.py:366
  342.9 25.1 %all_to_all.61.refs_1_ = bf16[32,80,256]{2,1,0:T(8,128)(2,1)S(1)} all-to-all(bf16[32,80,256]{2,1,0:T(8,128)(2,1)S(1)} %broadcast_in_dim.44), channel_id=1, replica_groups=mesh['segment'=8,'adapter'=32] {'adapter'}, dimensions={0} | all-to-all | bytes 2621440 | tf_op jit(solution)/shard_map/cond/branch_1_fun/all_to_all | solution.py:227
  368.0 3.6 branch_1_fun.39
  (67 shorter events, 15.5 us)
Async XLA Ops:
  2.4 4.0 %copy-start.1 = (bf16[1,2,8192,64]{2,3,1,0:T(8,128)(2,1)S(1)}, bf16[1,2,8192,64]{2,3,1,0:T(8,128)(2,1)}, u32[]{:S(2)}) copy-start(bf16[1,2,8192,64]{2,3,1,0:T(8,128)(2,1)} %param.37) | copy-start | bytes 6291460
  2.4 4.0 %copy-start.5 = (f32[1,8192]{1,0:T(1,128)S(1)}, f32[1,8192]{1,0:T(1,128)}, u32[]{:S(2)}) copy-start(f32[1,8192]{1,0:T(1,128)} %param.35) | copy-start | bytes 98308
  2.4 67.7 %collective-permute-start.3 = (bf16[64,8320]{1,0:T(8,128)(2,1)}, bf16[64,8320]{1,0:T(8,128)(2,1)}, u32[]{:S(2)}, u32[]{:S(2)}) collective-permute-start(bf16[64,8320]{1,0:T(8,128)(2,1)} %get-tuple-element.284), channel_id=1, source_target_pairs={{128,0},{129,1},{130,2},{131,3},{132,4},{133,5},{134,6},{135,7},{1... | collective-permute-start | bytes 3194888 | tf_op jit(solution)/shard_map/ppermute | solution.py:343
  4.3 2.2 collective-permute-start
  5.0 1.5 collective-permute-start.1
  19.2 11.5 %copy-start.3 = (bf16[4096,256]{1,0:T(8,128)(2,1)S(1)}, bf16[4096,256]{1,0:T(8,128)(2,1)}, u32[]{:S(2)}) copy-start(bf16[4096,256]{1,0:T(8,128)(2,1)} %get-tuple-element.176) | copy-start | bytes 6291460 | tf_op jit(solution)/shard_map/cond
  19.2 42.8 %all-to-all-start.9 = ((bf16[32,144,256]{2,1,0:T(8,128)(2,1)}), bf16[32,144,256]{2,1,0:T(8,128)(2,1)}, u32[]{:S(2)}, u32[]{:S(2)}) async-start(bf16[32,144,256]{2,1,0:T(8,128)(2,1)} %pad_maximum_fusion.2), calls=%async_computation.9 | async-start | bytes 4718592 | tf_op jit(solution)/shard_map/cond/branch_0_fun/all_to_all | solution.py:227
  66.6 2.1 collective-permute-start.2
  68.7 0.6 copy-start.14
  69.4 0.7 collective-permute-start.4
  70.7 0.7 collective-permute-start.5
  71.4 0.8 copy-start.10
  71.5 0.7 collective-permute-start.6
  72.2 0.8 copy-start.9
  72.2 0.7 collective-permute-start.7
  72.9 0.8 copy-start.8
  72.9 0.7 collective-permute-start.8
  73.9 0.7 collective-permute-start.9
  74.6 220.8 %collective-permute-start.10 = (bf16[64,256]{1,0:T(8,128)(2,1)S(1)}, bf16[64,256]{1,0:T(8,128)(2,1)S(1)}, u32[]{:S(2)}, u32[]{:S(2)}) collective-permute-start(bf16[64,256]{1,0:T(8,128)(2,1)S(1)} %get-tuple-element.290), channel_id=1, source_target_pairs={{192,224},{160,192},{193,225},{161,193},{194,226},{162,194},{195,2... | collective-permute-start | bytes 98312 | tf_op jit(solution)/shard_map/ppermute | solution.py:350
  325.0 17.0 %collective-permute-start.11 = (bf16[64,256]{1,0:T(8,128)(2,1)S(1)}, bf16[64,256]{1,0:T(8,128)(2,1)S(1)}, u32[]{:S(2)}, u32[]{:S(2)}) collective-permute-start(bf16[64,256]{1,0:T(8,128)(2,1)S(1)} %get-tuple-element.291), channel_id=1, source_target_pairs={{192,224},{193,225},{194,226},{195,227},{196,228},{197,229},{198,2... | collective-permute-start | bytes 98312 | tf_op jit(solution)/shard_map/ppermute | solution.py:350

commit v11 on v7

--- a/solution.py
+++ b/solution.py
@@ -271,13 +271,25 @@
             expand,
         )[0]
 
+    def unused():
+        return call(unused_kernel, [((all_held, cols), half), ((wide_rows, cols), half)])
+
+    def nothing():
+        return jnp.zeros((rows, cols), half)
+
+    def second_gather(h):
+        return gather(h).transpose(1, 0, 2).reshape(rows, model_width)
+
     def open_first(hidden):
         table, next_table = tables(hidden[:, model_width:])
         h = first_layer(hidden, table, hidden)
-        shrink, wide = call(
-            unused_kernel, [((all_held, cols), half), ((wide_rows, cols), half)]
-        )
+        shrink, wide = unused()
         return h, table, next_table, shrink, wide
+
+    def open_second(hidden):
+        table, next_table = tables(gather(info).reshape(rows, LANES))
+        shrink, wide = unused()
+        return nothing(), table, next_table, shrink, wide
 
     def open_other(hidden):
         by_dest = shrink_weight[0].reshape(ad_count, devices, cols, rank_most)
@@ -320,9 +332,6 @@
             ],
         )[0]
 
-    def nothing():
-        return jnp.zeros((rows, cols), half)
-
     hidden = lax.cond(
         segment == 0,
         lambda: gather_rows(0),
@@ -333,7 +342,9 @@
         ),
     )
     later = lax.ppermute(hidden, "segment", [(2, 0)])
-    h, table, next_table, shrink, wide = lax.cond(segment == 0, open_first, open_other, hidden)
+    h, table, next_table, shrink, wide = lax.switch(
+        jnp.minimum(segment, 2), (open_first, open_second, open_other), hidden
+    )
     outs = [h, h]
     for stage in range(1, segments + 1):
         pairs = [(s, s + 1) for s in (stage - 1, stage - 2) if 0 <= s < segments - 1]
@@ -343,14 +354,25 @@
         if stage == 1:
             got = lax.cond(
                 leads,
-                lambda: spread_out(h, now, shrink),
-                lambda: jnp.zeros(block_shape, half),
+                lambda: second_gather(h),
+                lambda: jnp.zeros((rows, model_width), half),
             )
-            over = lax.ppermute(got[0, :16, :LANES], "segment", [(1, 0)])
+            over = lax.ppermute(got[:16, :LANES], "segment", [(1, 0)])
             branch = jnp.where(trails, 2, jnp.where(leads, 1, 0))
             h = lax.switch(
                 branch,
-                (nothing, lambda: project(h, got, now, wide), lambda: first_layer(later, now, over)),
+                (nothing, lambda: first_layer(got, now, got), lambda: first_layer(later, now, over)),
+            )
+        elif stage == 2:
+            branch = jnp.where(trails, 2, jnp.where(leads, 1, 0))
+
+            def again():
+                gathered = second_gather(h)
+                return first_layer(gathered, now, gathered)
+
+            h = lax.switch(
+                branch,
+                (nothing, lambda: project(h, spread_out(h, now, shrink), now, wide), again),
             )
         else:
             h = lax.cond(

time: 355 us -> 387 us (1.090); the launches traced: 354 us -> 380 us
  waiting for transfers between devices: 236 us -> 250 us
  blocking collectives: 50.2 us -> 54.4 us
    ppermute x8, waiting for transfers between devices: 203 us -> 217 us  [on_device(): h = lax.ppermute(h, 'segment', pairs)]
    all_to_all x2, blocking collectives: 50.2 us -> 54.4 us  [exchange(): return lax.all_to_all(blocks, 'adapter', 0, 0, tiled=True)]
where the time goes in v11:
time: 387 us; the launch traced here: 380 us
  waiting for transfers between devices  250 us (65%)
  blocking collectives  54.4 us (14%)
  other arithmetic  27.4 us (7%)
  starting transfers between devices  20.4 us (5%)
  local copies, waits for them, and re-layouts  13.1 us (3%)
  Pallas kernels  9.74 us (3%)
  loops' own time  4.48 us (1%)
    ppermute x8, waiting for transfers between devices, on_device(): h = lax.ppermute(h, 'segment', pairs)  217 us
    all_to_all x2, blocking collectives, exchange(): return lax.all_to_all(blocks, 'adapter', 0, 0, tiled=True)  54.4 us
    all_to_all x1, waiting for transfers between devices, exchange(): return lax.all_to_all(blocks, 'adapter', 0, 0, tiled=True)  32.6 us
    concatenate x1, other arithmetic, open_other(): wide = jnp.concatenate([base, expand], axis=0)  18.8 us
    all_to_all x1, starting transfers between devices, exchange(): return lax.all_to_all(blocks, 'adapter', 0, 0, tiled=True)  11.5 us
    pallas_call x5, Pallas kernels, call(): pl.pallas_call(lambda *refs: kernel(rank_most, *refs), out_shape=[jax.Sha...  9.74 us
  transfers between devices with their start and end apart: 11, of which 3 were waited for; matrix products, arithmetic and copies ran while one was open for 9% of the time, Pallas kernels for 0%

profile of v11, /device:TPU:7, one launch (start us, length us, event | category | flops | bytes accessed | tf_op | source)
XLA Modules:
  0.0 380.3 jit_solution(6476780466472342997)
XLA Ops:
  1.4 1.1 conditional.12
  1.4 1.1 conditional
  1.4 1.1 broadcast.25
  2.5 1.7 collective-permute-start.1
  4.2 80.2 %conditional.13 = (bf16[64,256]{1,0:T(8,128)(2,1)S(1)}, f32[64,128]{1,0:T(8,128)}, f32[64,128]{1,0:T(8,128)}, bf16[4096,256]{1,0:T(8,128)(2,1)S(1)}, bf16[12288,256]{1,0:T(8,128)(2,1)}) conditional(s32[]{:T(128)} %clamp.11, (s32[]{:T(128)}, bf16[64,8320]{1,0:T(8,128)(2,1)}, bf16[1,8192,256]{2,1,0:T(8,128)(2,1)}, ...), branch_computations={%region_4.5_spmd, %region_5.6_spmd, %region_6.7_spmd} | conditional | flops 26738692 | bytes 58315416 | solution.py:345
  4.2 4.8 %copy.27 = bf16[1,2,8192,64]{3,2,1,0:T(8,128)(2,1)} copy(bf16[1,2,8192,64]{2,3,1,0:T(8,128)(2,1)} %get-tuple-element.310) | data formatting | bytes 4194304 | tf_op jit(solution)/shard_map
  8.9 3.5 copy.21
  12.6 1.6 pad_maximum_fusion.3
  14.2 11.5 %all-to-all-start.12 = ((bf16[32,144,256]{2,1,0:T(8,128)(2,1)}), bf16[32,144,256]{2,1,0:T(8,128)(2,1)}, u32[]{:S(2)}, u32[]{:S(2)}) async-start(bf16[32,144,256]{2,1,0:T(8,128)(2,1)} %pad_maximum_fusion.3), calls=%async_computation.12 | async-start | bytes 4718592 | tf_op jit(solution)/shard_map/cond/branch_2_fun/all_to_all | solution.py:226
  25.7 3.0 fusion
  28.7 18.8 %pad_maximum_fusion.2 = bf16[12288,256]{1,0:T(8,128)(2,1)} fusion(bf16[4096,256]{1,0:T(8,128)(2,1)S(1)} %copy-done.1, bf16[8192,256]{1,0:T(8,128)(2,1)S(1)} %fusion), kind=kLoop, calls=%fused_computation.7 | loop fusion | flops 12582912 | bytes 12582912 | tf_op jit(solution)/shard_map/cond/branch_2_fun/concatenate | solution.py:301
  47.5 32.6 %all-to-all-done.12 = bf16[32,144,256]{2,1,0:T(8,128)(2,1)} async-done(((bf16[32,144,256]{2,1,0:T(8,128)(2,1)}), bf16[32,144,256]{2,1,0:T(8,128)(2,1)}, u32[]{:S(2)}, u32[]{:S(2)}) %all-to-all-start.12) | async-done | bytes 2359328 | tf_op jit(solution)/shard_map/cond/branch_2_fun/all_to_all | solution.py:226
  81.8 1.7 slice.30
  88.6 4.1 %conditional.17 = (bf16[64,256]{1,0:T(8,128)(2,1)S(1)}) conditional(s32[]{:T(128)} %convert_element_type.55, () %tuple.94, (bf16[64,256]{1,0:T(8,128)(2,1)S(1)}, f32[64,128]{1,0:T(8,128)}, bf16[4096,256]{1,0:T(8,128)(2,1)S(1)}, bf16[12288,256]{1,0:T(8,128)(2,1)}) %tuple.106), branch_computations={%region_15.16_spmd, %region_16.17_spmd} | conditional | bytes 4104228 | solution.py:378
  94.9 1.3 collective-permute-start.8
  96.2 206.1 %collective-permute-done.8 = bf16[64,256]{1,0:T(8,128)(2,1)S(1)} collective-permute-done((bf16[64,256]{1,0:T(8,128)(2,1)S(1)}, bf16[64,256]{1,0:T(8,128)(2,1)S(1)}, u32[]{:S(2)}, u32[]{:S(2)}) %collective-permute-start.8) | collective-permute-done | bytes 32800 | tf_op jit(solution)/shard_map/ppermute | solution.py:351
  302.4 33.9 %conditional.21 = (bf16[64,256]{1,0:T(8,128)(2,1)S(1)}) conditional(s32[]{:T(128)} %convert_element_type.51, () %tuple.90, (bf16[64,256]{1,0:T(8,128)(2,1)S(1)}, f32[64,128]{1,0:T(8,128)S(1)}, bf16[4096,256]{1,0:T(8,128)(2,1)S(1)}, bf16[12288,256]{1,0:T(8,128)(2,1)}) %tuple.174), branch_computations={%region_23.24_spmd, %region_24.25_spmd} | conditional | bytes 3973128 | solution.py:378
  303.3 29.4 %all_to_all.77.refs_1_ = bf16[32,80,256]{2,1,0:T(8,128)(2,1)S(1)} all-to-all(bf16[32,80,256]{2,1,0:T(8,128)(2,1)S(1)} %broadcast_in_dim.55), channel_id=1, replica_groups=mesh['segment'=8,'adapter'=32] {'adapter'}, dimensions={0} | all-to-all | bytes 2621440 | tf_op jit(solution)/shard_map/cond/branch_1_fun/all_to_all | solution.py:226
  332.7 3.6 branch_1_fun.33
  336.3 1.3 collective-permute-start.9
  337.6 11.1 %collective-permute-done.9 = bf16[64,256]{1,0:T(8,128)(2,1)S(1)} collective-permute-done((bf16[64,256]{1,0:T(8,128)(2,1)S(1)}, bf16[64,256]{1,0:T(8,128)(2,1)S(1)}, u32[]{:S(2)}, u32[]{:S(2)}) %collective-permute-start.9) | collective-permute-done | bytes 32800 | tf_op jit(solution)/shard_map/ppermute | solution.py:351
  348.7 29.6 %conditional.22 = (bf16[64,256]{1,0:T(8,128)(2,1)S(1)}) conditional(s32[]{:T(128)} %convert_element_type.50, () %tuple.89, (bf16[64,256]{1,0:T(8,128)(2,1)S(1)}, f32[64,128]{1,0:T(8,128)S(1)}, bf16[4096,256]{1,0:T(8,128)(2,1)S(1)}, bf16[12288,256]{1,0:T(8,128)(2,1)}) %tuple.173), branch_computations={%region_25.26_spmd, %region_26.27_spmd} | conditional | bytes 3973128 | solution.py:378
  349.6 25.1 %all_to_all.78.refs_1_ = bf16[32,80,256]{2,1,0:T(8,128)(2,1)S(1)} all-to-all(bf16[32,80,256]{2,1,0:T(8,128)(2,1)S(1)} %broadcast_in_dim.56), channel_id=1, replica_groups=mesh['segment'=8,'adapter'=32] {'adapter'}, dimensions={0} | all-to-all | bytes 2621440 | tf_op jit(solution)/shard_map/cond/branch_1_fun/all_to_all | solution.py:226
  374.7 3.6 branch_1_fun.35
  (74 shorter events, 14.0 us)
Async XLA Ops:
  1.4 2.8 copy-start.2
  2.5 84.1 %collective-permute-start.1 = (bf16[64,8320]{1,0:T(8,128)(2,1)}, bf16[64,8320]{1,0:T(8,128)(2,1)}, u32[]{:S(2)}, u32[]{:S(2)}) collective-permute-start(bf16[64,8320]{1,0:T(8,128)(2,1)} %get-tuple-element.347), channel_id=1, source_target_pairs={{64,0},{65,1},{66,2},{67,3},{68,4},{69,5},{70,6},{71,7},{72,8},{73... | collective-permute-start | bytes 3194888 | tf_op jit(solution)/shard_map/ppermute | solution.py:344
  14.2 65.9 %all-to-all-start.12 = ((bf16[32,144,256]{2,1,0:T(8,128)(2,1)}), bf16[32,144,256]{2,1,0:T(8,128)(2,1)}, u32[]{:S(2)}, u32[]{:S(2)}) async-start(bf16[32,144,256]{2,1,0:T(8,128)(2,1)} %pad_maximum_fusion.3), calls=%async_computation.12 | async-start | bytes 4718592 | tf_op jit(solution)/shard_map/cond/branch_2_fun/all_to_all | solution.py:226
  25.7 3.0 copy-start.1
  84.3 0.7 copy-start.15
  84.3 0.7 collective-permute-start
  85.0 0.8 copy-start.14
  85.0 0.8 copy-start.19
  85.2 1.4 collective-permute-start.2
  87.2 0.7 collective-permute-start.3
  87.9 0.7 copy-start.17
  87.9 0.7 collective-permute-start.4
  88.6 4.8 %copy-start.11 = (f32[64,128]{1,0:T(8,128)S(1)}, f32[64,128]{1,0:T(8,128)}, u32[]{:S(2)}) copy-start(f32[64,128]{1,0:T(8,128)} %get-tuple-element.325) | copy-start | bytes 98308
  92.7 0.7 collective-permute-start.5
  93.4 0.8 copy-start.10
  93.5 0.7 collective-permute-start.6
  94.2 0.8 copy-start.9
  94.2 0.7 collective-permute-start.7
  94.9 207.5 %copy-start.8 = (f32[64,128]{1,0:T(8,128)S(1)}, f32[64,128]{1,0:T(8,128)}, u32[]{:S(2)}) copy-start(f32[64,128]{1,0:T(8,128)} %get-tuple-element.322) | copy-start | bytes 98308
  94.9 207.4 %collective-permute-start.8 = (bf16[64,256]{1,0:T(8,128)(2,1)S(1)}, bf16[64,256]{1,0:T(8,128)(2,1)S(1)}, u32[]{:S(2)}, u32[]{:S(2)}) collective-permute-start(bf16[64,256]{1,0:T(8,128)(2,1)S(1)} %get-tuple-element.354), channel_id=1, source_target_pairs={{192,224},{160,192},{193,225},{161,193},{194,226},{162,194},{195,2... | collective-permute-start | bytes 98312 | tf_op jit(solution)/shard_map/ppermute | solution.py:351
  302.4 46.3 %copy-start.7 = (f32[64,128]{1,0:T(8,128)S(1)}, f32[64,128]{1,0:T(8,128)}, u32[]{:S(2)}) copy-start(f32[64,128]{1,0:T(8,128)} %get-tuple-element.321) | copy-start | bytes 98308
  336.3 12.4 %collective-permute-start.9 = (bf16[64,256]{1,0:T(8,128)(2,1)S(1)}, bf16[64,256]{1,0:T(8,128)(2,1)S(1)}, u32[]{:S(2)}, u32[]{:S(2)}) collective-permute-start(bf16[64,256]{1,0:T(8,128)(2,1)S(1)} %get-tuple-element.355), channel_id=1, source_target_pairs={{192,224},{193,225},{194,226},{195,227},{196,228},{197,229},{198,2... | collective-permute-start | bytes 98312 | tf_op jit(solution)/shard_map/ppermute | solution.py:351
  348.7 29.7 %copy-start.16 = (bf16[64,256]{1,0:T(8,128)(2,1)S(1)}, bf16[64,256]{1,0:T(8,128)(2,1)}, u32[]{:S(2)}) copy-start(bf16[64,256]{1,0:T(8,128)(2,1)} %copy-done.15) | copy-start | bytes 98308
  348.7 29.7 %copy-start.18 = (bf16[64,256]{1,0:T(8,128)(2,1)S(1)}, bf16[64,256]{1,0:T(8,128)(2,1)}, u32[]{:S(2)}) copy-start(bf16[64,256]{1,0:T(8,128)(2,1)} %copy-done.17) | copy-start | bytes 98308

commit v12 on v7

--- a/solution.py
+++ b/solution.py
@@ -7,6 +7,7 @@
 
 GROUP = 4
 CHUNKS = 8
+DEPTH = 3
 LANES = 128
 
 
@@ -50,9 +51,15 @@
     for c in range(pieces):
         part = (slice(None),) * axis + (pl.ds(c * size, size),)
         copies.append(pltpu.make_async_copy(source.at[part], target.at[part], sems.at[c]))
-    for copy in copies:
+    for copy in copies[:DEPTH]:
         copy.start()
-    return copies
+
+    def wait(c):
+        copies[c].wait()
+        if c + DEPTH < pieces:
+            copies[c + DEPTH].start()
+
+    return wait
 
 
 def inverse_rms(squares, width):
@@ -83,16 +90,16 @@
     rows = hidden_ref.shape[0]
     width, cols = base_ref.shape
     held = maps_ref.shape[0]
-    base_copies = fetches(base_hbm, base_ref, base_sems)
-    maps_copies = fetches(maps_hbm, maps_ref, maps_sems, axis=1)
+    base_wait = fetches(base_hbm, base_ref, base_sems)
+    maps_wait = fetches(maps_hbm, maps_ref, maps_sems, axis=1)
     base = jnp.zeros((rows, cols), jnp.float32)
     shrunk = jnp.zeros((rows, held), jnp.float32)
     squares = jnp.zeros((rows, cols), jnp.float32)
     steps = width // cols
     for j in range(steps):
         if j % (steps // CHUNKS) == 0:
-            base_copies[j // (steps // CHUNKS)].wait()
-            maps_copies[j // (steps // CHUNKS)].wait()
+            base_wait(j // (steps // CHUNKS))
+            maps_wait(j // (steps // CHUNKS))
         part = slice(j * cols, (j + 1) * cols)
         wide = hidden_ref[:, part].astype(jnp.float32)
         squares = squares + wide * wide
@@ -159,14 +166,14 @@
     rank_most, h_ref, got_ref, table_ref, wide_hbm, out_ref, wide_ref, sems
 ):
     rows, cols = h_ref.shape
-    copies = fetches(wide_hbm, wide_ref, sems)
+    wait = fetches(wide_hbm, wide_ref, sems)
     sources = got_ref.shape[0]
     base = jnp.zeros((rows, cols), jnp.float32)
     squares = jnp.zeros((rows, cols), jnp.float32)
     partial = jnp.zeros((rows // GROUP, cols), jnp.float32)
     for j in range(sources):
         if j % (sources // CHUNKS) == 0:
-            copies[j // (sources // CHUNKS)].wait()
+            wait(j // (sources // CHUNKS))
         block = got_ref[j, :rows, :]
         base = base + jnp.dot(
             block, wide_ref[j * cols : (j + 1) * cols, :], preferred_element_type=jnp.float32
@@ -177,8 +184,8 @@
     inverse = inverse_rms(squares, sources * cols)
     ids, rank = ids_and_rank(table_ref)
     low = unfold(rank_most, partial) * inverse * scaling(rank_most, rank, (rows, cols))
-    for copy in copies[CHUNKS:]:
-        copy.wait()
+    for c in range(CHUNKS, sems.shape[0]):
+        wait(c)
     finish(rank_most, h_ref, base * inverse, low, ids, wide_ref, out_ref, sources * cols)
 
 

time: 355 us -> 372 us (1.048)
  waiting for transfers between devices: 236 us -> 249 us
  Pallas kernels: 9.73 us -> 13.9 us
    ppermute x8, waiting for transfers between devices: 203 us -> 217 us  [on_device(): h = lax.ppermute(h, 'segment', pairs)]
    pallas_call x5, Pallas kernels: 9.73 us -> 13.9 us  [call(): pl.pallas_call(lambda *refs: kernel(rank_most, *refs), out_shape=[jax.Sha...]
where the time goes in v12:
time: 372 us; the launch traced here: 371 us
  waiting for transfers between devices  249 us (67%)
  blocking collectives  50.2 us (13%)
  other arithmetic  27.5 us (7%)
  starting transfers between devices  20.2 us (5%)
  Pallas kernels  13.9 us (4%)
  local copies, waits for them, and re-layouts  9.28 us (2%)
    ppermute x8, waiting for transfers between devices, on_device(): h = lax.ppermute(h, 'segment', pairs)  217 us
    all_to_all x2, blocking collectives, exchange(): return lax.all_to_all(blocks, 'adapter', 0, 0, tiled=True)  50.2 us
    all_to_all x1, waiting for transfers between devices, exchange(): return lax.all_to_all(blocks, 'adapter', 0, 0, tiled=True)  32.4 us
    concatenate x1, other arithmetic, open_other(): wide = jnp.concatenate([base, expand], axis=0)  18.8 us
    pallas_call x5, Pallas kernels, call(): pl.pallas_call(lambda *refs: kernel(rank_most, *refs), out_shape=[jax.Sha...  13.9 us
    all_to_all x1, starting transfers between devices, exchange(): return lax.all_to_all(blocks, 'adapter', 0, 0, tiled=True)  11.4 us
  transfers between devices with their start and end apart: 11, of which 3 were waited for; matrix products, arithmetic and copies ran while one was open for 9% of the time, Pallas kernels for 0%

profile of v12, /device:TPU:7, one launch (start us, length us, event | category | flops | bytes accessed | tf_op | source)
XLA Modules:
  0.0 371.3 jit_solution(17107894885895552772)
XLA Ops:
  1.4 1.1 conditional.12
  1.4 1.1 conditional
  1.4 1.1 broadcast.23
  2.5 1.6 collective-permute-start.1
  4.1 76.1 %conditional.13 = (bf16[64,256]{1,0:T(8,128)(2,1)S(1)}, f32[64,128]{1,0:T(8,128)}, f32[64,128]{1,0:T(8,128)S(1)}, bf16[4096,256]{1,0:T(8,128)(2,1)S(1)}, bf16[12288,256]{1,0:T(8,128)(2,1)}) conditional(s32[]{:T(128)} %convert_element_type.61, (bf16[1,2,8192,64]{2,3,1,0:T(8,128)(2,1)S(1)}, bf16[2,128]{0,1:T(8,128)(2,1)S(1)}, s32[]{:T(128)}, ...), branch_computations={%region_4.5_spmd, %region_5.6_spmd} | conditional | flops 26738692 | bytes 58315416 | solution.py:343
  4.1 3.2 copy.11
  7.3 3.5 copy.8
  11.0 1.6 pad_maximum_fusion.3
  12.6 11.4 %all-to-all-start.10 = ((bf16[32,144,256]{2,1,0:T(8,128)(2,1)}), bf16[32,144,256]{2,1,0:T(8,128)(2,1)S(1)}, u32[]{:S(2)}, u32[]{:S(2)}) async-start(bf16[32,144,256]{2,1,0:T(8,128)(2,1)} %pad_maximum_fusion.3), calls=%async_computation.10 | async-start | bytes 4718592 | tf_op jit(solution)/shard_map/cond/branch_0_fun/all_to_all | solution.py:233
  24.1 3.0 fusion
  27.1 18.8 %pad_maximum_fusion.2 = bf16[12288,256]{1,0:T(8,128)(2,1)} fusion(bf16[4096,256]{1,0:T(8,128)(2,1)S(1)} %copy-done.1, bf16[8192,256]{1,0:T(8,128)(2,1)S(1)} %fusion), kind=kLoop, calls=%fused_computation.6 | loop fusion | flops 12582912 | bytes 12582912 | tf_op jit(solution)/shard_map/cond/branch_0_fun/concatenate | solution.py:296
  45.9 32.4 %all-to-all-done.10 = bf16[32,144,256]{2,1,0:T(8,128)(2,1)S(1)} async-done(((bf16[32,144,256]{2,1,0:T(8,128)(2,1)}), bf16[32,144,256]{2,1,0:T(8,128)(2,1)S(1)}, u32[]{:S(2)}, u32[]{:S(2)}) %all-to-all-start.10) | async-done | bytes 2359328 | tf_op jit(solution)/shard_map/cond/branch_0_fun/all_to_all | solution.py:233
  80.9 1.4 broadcast_select_fusion
  87.7 1.3 collective-permute-start.8
  89.1 201.3 %collective-permute-done.8 = bf16[64,256]{1,0:T(8,128)(2,1)S(1)} collective-permute-done((bf16[64,256]{1,0:T(8,128)(2,1)S(1)}, bf16[64,256]{1,0:T(8,128)(2,1)S(1)}, u32[]{:S(2)}, u32[]{:S(2)}) %collective-permute-start.8) | collective-permute-done | bytes 32800 | tf_op jit(solution)/shard_map/ppermute | solution.py:347
  290.4 31.7 %conditional.21 = (bf16[64,256]{1,0:T(8,128)(2,1)S(1)}) conditional(s32[]{:T(128)} %convert_element_type.55, () %tuple.83, (bf16[64,256]{1,0:T(8,128)(2,1)S(1)}, f32[64,128]{1,0:T(8,128)S(1)}, bf16[4096,256]{1,0:T(8,128)(2,1)S(1)}, bf16[12288,256]{1,0:T(8,128)(2,1)}) %tuple.103), branch_computations={%region_21.22_spmd, %region_22.23_spmd} | conditional | bytes 3973128 | solution.py:363
  291.3 25.1 %all_to_all.60.refs_1_ = bf16[32,80,256]{2,1,0:T(8,128)(2,1)S(1)} all-to-all(bf16[32,80,256]{2,1,0:T(8,128)(2,1)S(1)} %broadcast_in_dim.43), channel_id=1, replica_groups=mesh['segment'=8,'adapter'=32] {'adapter'}, dimensions={0} | all-to-all | bytes 2621440 | tf_op jit(solution)/shard_map/cond/branch_1_fun/all_to_all | solution.py:233
  316.4 5.7 %branch_1_fun.37 = bf16[64,256]{1,0:T(8,128)(2,1)S(1)} custom-call(bf16[64,256]{1,0:T(8,128)(2,1)S(1)} %get-tuple-element.230.refs_0_, bf16[32,80,256]{2,1,0:T(8,128)(2,1)S(1)} %all_to_all.60.refs_1_, f32[64,128]{1,0:T(8,128)S(1)} %get-tuple-element.231.refs_1_.refs_2_, bf16[12288,256]{1,0:T(8,128)(2,1)} %get-tuple-element.233.refs_3_), custom_call_target="tpu_custom_call" | custom-call | tf_op jit(solution)/shard_map/cond/branch_1_fun/pallas_call | solution.py:223
  322.1 1.3 collective-permute-start.9
  323.4 15.4 %collective-permute-done.9 = bf16[64,256]{1,0:T(8,128)(2,1)S(1)} collective-permute-done((bf16[64,256]{1,0:T(8,128)(2,1)S(1)}, bf16[64,256]{1,0:T(8,128)(2,1)S(1)}, u32[]{:S(2)}, u32[]{:S(2)}) %collective-permute-start.9) | collective-permute-done | bytes 32800 | tf_op jit(solution)/shard_map/ppermute | solution.py:347
  338.8 31.7 %conditional.22 = (bf16[64,256]{1,0:T(8,128)(2,1)S(1)}) conditional(s32[]{:T(128)} %convert_element_type.54, () %tuple.82, (bf16[64,256]{1,0:T(8,128)(2,1)S(1)}, f32[64,128]{1,0:T(8,128)S(1)}, bf16[4096,256]{1,0:T(8,128)(2,1)S(1)}, bf16[12288,256]{1,0:T(8,128)(2,1)}) %tuple.104), branch_computations={%region_23.24_spmd, %region_24.25_spmd} | conditional | bytes 3973128 | solution.py:363
  338.8 0.8 branch_1_fun.38
  339.7 25.1 %all_to_all.61.refs_1_ = bf16[32,80,256]{2,1,0:T(8,128)(2,1)S(1)} all-to-all(bf16[32,80,256]{2,1,0:T(8,128)(2,1)S(1)} %broadcast_in_dim.44), channel_id=1, replica_groups=mesh['segment'=8,'adapter'=32] {'adapter'}, dimensions={0} | all-to-all | bytes 2621440 | tf_op jit(solution)/shard_map/cond/branch_1_fun/all_to_all | solution.py:233
  364.8 5.7 %branch_1_fun.39 = bf16[64,256]{1,0:T(8,128)(2,1)S(1)} custom-call(bf16[64,256]{1,0:T(8,128)(2,1)S(1)} %get-tuple-element.234.refs_0_, bf16[32,80,256]{2,1,0:T(8,128)(2,1)S(1)} %all_to_all.61.refs_1_, f32[64,128]{1,0:T(8,128)S(1)} %get-tuple-element.235.refs_1_.refs_2_, bf16[12288,256]{1,0:T(8,128)(2,1)} %get-tuple-element.237.refs_3_), custom_call_target="tpu_custom_call" | custom-call | tf_op jit(solution)/shard_map/cond/branch_1_fun/pallas_call | solution.py:223
  (68 shorter events, 10.8 us)
Async XLA Ops:
  1.4 2.7 copy-start
  1.4 2.7 copy-start.2
  2.5 81.3 %collective-permute-start.1 = (bf16[64,8320]{1,0:T(8,128)(2,1)}, bf16[64,8320]{1,0:T(8,128)(2,1)}, u32[]{:S(2)}, u32[]{:S(2)}) collective-permute-start(bf16[64,8320]{1,0:T(8,128)(2,1)} %get-tuple-element.285), channel_id=1, source_target_pairs={{64,0},{65,1},{66,2},{67,3},{68,4},{69,5},{70,6},{71,7},{72,8},{73... | collective-permute-start | bytes 3194888 | tf_op jit(solution)/shard_map/ppermute | solution.py:342
  12.6 65.6 %all-to-all-start.10 = ((bf16[32,144,256]{2,1,0:T(8,128)(2,1)}), bf16[32,144,256]{2,1,0:T(8,128)(2,1)S(1)}, u32[]{:S(2)}, u32[]{:S(2)}) async-start(bf16[32,144,256]{2,1,0:T(8,128)(2,1)} %pad_maximum_fusion.3), calls=%async_computation.10 | async-start | bytes 4718592 | tf_op jit(solution)/shard_map/cond/branch_0_fun/all_to_all | solution.py:233
  24.0 3.0 copy-start.1
  80.2 2.1 copy-start.9
  80.2 2.1 collective-permute-start
  82.3 0.6 copy-start.8
  83.1 0.7 collective-permute-start.2
  83.8 0.7 collective-permute-start.3
  84.5 0.8 copy-start.6
  84.5 0.7 collective-permute-start.4
  85.3 0.8 copy-start.5
  85.3 0.7 collective-permute-start.5
  86.0 1.0 copy-start.4
  86.3 0.7 collective-permute-start.6
  87.0 0.8 copy-start.3
  87.0 0.7 collective-permute-start.7
  87.7 202.6 %collective-permute-start.8 = (bf16[64,256]{1,0:T(8,128)(2,1)S(1)}, bf16[64,256]{1,0:T(8,128)(2,1)S(1)}, u32[]{:S(2)}, u32[]{:S(2)}) collective-permute-start(bf16[64,256]{1,0:T(8,128)(2,1)S(1)} %get-tuple-element.292), channel_id=1, source_target_pairs={{192,224},{160,192},{193,225},{161,193},{194,226},{162,194},{195,2... | collective-permute-start | bytes 98312 | tf_op jit(solution)/shard_map/ppermute | solution.py:347
  322.1 16.7 %collective-permute-start.9 = (bf16[64,256]{1,0:T(8,128)(2,1)S(1)}, bf16[64,256]{1,0:T(8,128)(2,1)S(1)}, u32[]{:S(2)}, u32[]{:S(2)}) collective-permute-start(bf16[64,256]{1,0:T(8,128)(2,1)S(1)} %get-tuple-element.293), channel_id=1, source_target_pairs={{192,224},{193,225},{194,226},{195,227},{196,228},{197,229},{198,2... | collective-permute-start | bytes 98312 | tf_op jit(solution)/shard_map/ppermute | solution.py:347
  338.8 31.8 %copy-start.10 = (bf16[64,256]{1,0:T(8,128)(2,1)S(1)}, bf16[64,256]{1,0:T(8,128)(2,1)}, u32[]{:S(2)}) copy-start(bf16[64,256]{1,0:T(8,128)(2,1)} %copy-done.9) | copy-start | bytes 98308

commit v13 on v7

--- a/solution.py
+++ b/solution.py
@@ -6,7 +6,7 @@
 from jax.sharding import PartitionSpec as P
 
 GROUP = 4
-CHUNKS = 8
+CHUNKS = 16
 LANES = 128
 
 

time: 355 us -> 368 us (1.037)
  waiting for transfers between devices: 236 us -> 241 us
    ppermute x8, waiting for transfers between devices: 203 us -> 209 us  [on_device(): h = lax.ppermute(h, 'segment', pairs)]
where the time goes in v13:
time: 368 us; the launch traced here: 363 us
  waiting for transfers between devices  241 us (65%)
  blocking collectives  50.2 us (14%)
  other arithmetic  27.5 us (7%)
  starting transfers between devices  20.2 us (5%)
  Pallas kernels  9.91 us (3%)
  local copies, waits for them, and re-layouts  9.28 us (3%)
  loops' own time  4.03 us (1%)
    ppermute x8, waiting for transfers between devices, on_device(): h = lax.ppermute(h, 'segment', pairs)  209 us
    all_to_all x2, blocking collectives, exchange(): return lax.all_to_all(blocks, 'adapter', 0, 0, tiled=True)  50.2 us
    all_to_all x1, waiting for transfers between devices, exchange(): return lax.all_to_all(blocks, 'adapter', 0, 0, tiled=True)  32.6 us
    concatenate x1, other arithmetic, open_other(): wide = jnp.concatenate([base, expand], axis=0)  18.8 us
    all_to_all x1, starting transfers between devices, exchange(): return lax.all_to_all(blocks, 'adapter', 0, 0, tiled=True)  11.4 us
    pallas_call x5, Pallas kernels, call(): pl.pallas_call(lambda *refs: kernel(rank_most, *refs), out_shape=[jax.Sha...  9.91 us
  transfers between devices with their start and end apart: 11, of which 3 were waited for; matrix products, arithmetic and copies ran while one was open for 9% of the time, Pallas kernels for 0%

profile of v13, /device:TPU:7, one launch (start us, length us, event | category | flops | bytes accessed | tf_op | source)
XLA Modules:
  0.0 363.4 jit_solution(17807480844460136419)
XLA Ops:
  1.4 1.1 conditional.12
  1.4 1.1 conditional
  1.4 1.1 broadcast.23
  2.5 1.6 collective-permute-start.1
  4.1 76.3 %conditional.13 = (bf16[64,256]{1,0:T(8,128)(2,1)S(1)}, f32[64,128]{1,0:T(8,128)}, f32[64,128]{1,0:T(8,128)S(1)}, bf16[4096,256]{1,0:T(8,128)(2,1)S(1)}, bf16[12288,256]{1,0:T(8,128)(2,1)}) conditional(s32[]{:T(128)} %convert_element_type.61, (bf16[1,2,8192,64]{2,3,1,0:T(8,128)(2,1)S(1)}, bf16[2,128]{0,1:T(8,128)(2,1)S(1)}, s32[]{:T(128)}, ...), branch_computations={%region_4.5_spmd, %region_5.6_spmd} | conditional | flops 26738692 | bytes 58315416 | solution.py:336
  4.1 3.2 copy.11
  7.3 3.5 copy.8
  11.0 1.6 pad_maximum_fusion.3
  12.6 11.4 %all-to-all-start.10 = ((bf16[32,144,256]{2,1,0:T(8,128)(2,1)}), bf16[32,144,256]{2,1,0:T(8,128)(2,1)S(1)}, u32[]{:S(2)}, u32[]{:S(2)}) async-start(bf16[32,144,256]{2,1,0:T(8,128)(2,1)} %pad_maximum_fusion.3), calls=%async_computation.10 | async-start | bytes 4718592 | tf_op jit(solution)/shard_map/cond/branch_0_fun/all_to_all | solution.py:226
  24.0 3.0 fusion
  27.1 18.8 %pad_maximum_fusion.2 = bf16[12288,256]{1,0:T(8,128)(2,1)} fusion(bf16[4096,256]{1,0:T(8,128)(2,1)S(1)} %copy-done.1, bf16[8192,256]{1,0:T(8,128)(2,1)S(1)} %fusion), kind=kLoop, calls=%fused_computation.6 | loop fusion | flops 12582912 | bytes 12582912 | tf_op jit(solution)/shard_map/cond/branch_0_fun/concatenate | solution.py:289
  45.9 32.6 %all-to-all-done.10 = bf16[32,144,256]{2,1,0:T(8,128)(2,1)S(1)} async-done(((bf16[32,144,256]{2,1,0:T(8,128)(2,1)}), bf16[32,144,256]{2,1,0:T(8,128)(2,1)S(1)}, u32[]{:S(2)}, u32[]{:S(2)}) %all-to-all-start.10) | async-done | bytes 2359328 | tf_op jit(solution)/shard_map/cond/branch_0_fun/all_to_all | solution.py:226
  81.1 1.4 broadcast_select_fusion
  85.4 3.6 conditional.17
  91.3 1.3 collective-permute-start.8
  92.6 193.3 %collective-permute-done.8 = bf16[64,256]{1,0:T(8,128)(2,1)S(1)} collective-permute-done((bf16[64,256]{1,0:T(8,128)(2,1)S(1)}, bf16[64,256]{1,0:T(8,128)(2,1)S(1)}, u32[]{:S(2)}, u32[]{:S(2)}) %collective-permute-start.8) | collective-permute-done | bytes 32800 | tf_op jit(solution)/shard_map/ppermute | solution.py:340
  285.8 29.7 %conditional.21 = (bf16[64,256]{1,0:T(8,128)(2,1)S(1)}) conditional(s32[]{:T(128)} %convert_element_type.55, () %tuple.83, (bf16[64,256]{1,0:T(8,128)(2,1)S(1)}, f32[64,128]{1,0:T(8,128)S(1)}, bf16[4096,256]{1,0:T(8,128)(2,1)S(1)}, bf16[12288,256]{1,0:T(8,128)(2,1)}) %tuple.103), branch_computations={%region_21.22_spmd, %region_22.23_spmd} | conditional | bytes 3973128 | solution.py:356
  286.7 25.1 %all_to_all.60.refs_1_ = bf16[32,80,256]{2,1,0:T(8,128)(2,1)S(1)} all-to-all(bf16[32,80,256]{2,1,0:T(8,128)(2,1)S(1)} %broadcast_in_dim.43), channel_id=1, replica_groups=mesh['segment'=8,'adapter'=32] {'adapter'}, dimensions={0} | all-to-all | bytes 2621440 | tf_op jit(solution)/shard_map/cond/branch_1_fun/all_to_all | solution.py:226
  311.8 3.7 %branch_1_fun.37 = bf16[64,256]{1,0:T(8,128)(2,1)S(1)} custom-call(bf16[64,256]{1,0:T(8,128)(2,1)S(1)} %get-tuple-element.230.refs_0_, bf16[32,80,256]{2,1,0:T(8,128)(2,1)S(1)} %all_to_all.60.refs_1_, f32[64,128]{1,0:T(8,128)S(1)} %get-tuple-element.231.refs_1_.refs_2_, bf16[12288,256]{1,0:T(8,128)(2,1)} %get-tuple-element.233.refs_3_), custom_call_target="tpu_custom_call" | custom-call | tf_op jit(solution)/shard_map/cond/branch_1_fun/pallas_call | solution.py:216
  315.6 1.3 collective-permute-start.9
  316.9 15.6 %collective-permute-done.9 = bf16[64,256]{1,0:T(8,128)(2,1)S(1)} collective-permute-done((bf16[64,256]{1,0:T(8,128)(2,1)S(1)}, bf16[64,256]{1,0:T(8,128)(2,1)S(1)}, u32[]{:S(2)}, u32[]{:S(2)}) %collective-permute-start.9) | collective-permute-done | bytes 32800 | tf_op jit(solution)/shard_map/ppermute | solution.py:340
  332.5 29.8 %conditional.22 = (bf16[64,256]{1,0:T(8,128)(2,1)S(1)}) conditional(s32[]{:T(128)} %convert_element_type.54, () %tuple.82, (bf16[64,256]{1,0:T(8,128)(2,1)S(1)}, f32[64,128]{1,0:T(8,128)S(1)}, bf16[4096,256]{1,0:T(8,128)(2,1)S(1)}, bf16[12288,256]{1,0:T(8,128)(2,1)}) %tuple.104), branch_computations={%region_23.24_spmd, %region_24.25_spmd} | conditional | bytes 3973128 | solution.py:356
  333.4 25.1 %all_to_all.61.refs_1_ = bf16[32,80,256]{2,1,0:T(8,128)(2,1)S(1)} all-to-all(bf16[32,80,256]{2,1,0:T(8,128)(2,1)S(1)} %broadcast_in_dim.44), channel_id=1, replica_groups=mesh['segment'=8,'adapter'=32] {'adapter'}, dimensions={0} | all-to-all | bytes 2621440 | tf_op jit(solution)/shard_map/cond/branch_1_fun/all_to_all | solution.py:226
  358.6 3.7 %branch_1_fun.39 = bf16[64,256]{1,0:T(8,128)(2,1)S(1)} custom-call(bf16[64,256]{1,0:T(8,128)(2,1)S(1)} %get-tuple-element.234.refs_0_, bf16[32,80,256]{2,1,0:T(8,128)(2,1)S(1)} %all_to_all.61.refs_1_, f32[64,128]{1,0:T(8,128)S(1)} %get-tuple-element.235.refs_1_.refs_2_, bf16[12288,256]{1,0:T(8,128)(2,1)} %get-tuple-element.237.refs_3_), custom_call_target="tpu_custom_call" | custom-call | tf_op jit(solution)/shard_map/cond/branch_1_fun/pallas_call | solution.py:216
  (68 shorter events, 11.4 us)
Async XLA Ops:
  1.4 2.7 copy-start
  1.4 2.7 copy-start.2
  2.5 81.5 %collective-permute-start.1 = (bf16[64,8320]{1,0:T(8,128)(2,1)}, bf16[64,8320]{1,0:T(8,128)(2,1)}, u32[]{:S(2)}, u32[]{:S(2)}) collective-permute-start(bf16[64,8320]{1,0:T(8,128)(2,1)} %get-tuple-element.285), channel_id=1, source_target_pairs={{64,0},{65,1},{66,2},{67,3},{68,4},{69,5},{70,6},{71,7},{72,8},{73... | collective-permute-start | bytes 3194888 | tf_op jit(solution)/shard_map/ppermute | solution.py:335
  12.6 65.8 %all-to-all-start.10 = ((bf16[32,144,256]{2,1,0:T(8,128)(2,1)}), bf16[32,144,256]{2,1,0:T(8,128)(2,1)S(1)}, u32[]{:S(2)}, u32[]{:S(2)}) async-start(bf16[32,144,256]{2,1,0:T(8,128)(2,1)} %pad_maximum_fusion.3), calls=%async_computation.10 | async-start | bytes 4718592 | tf_op jit(solution)/shard_map/cond/branch_0_fun/all_to_all | solution.py:226
  24.0 3.0 copy-start.1
  80.4 2.1 copy-start.9
  80.4 2.1 collective-permute-start
  82.5 0.6 copy-start.8
  83.2 0.7 collective-permute-start.2
  84.0 0.7 collective-permute-start.3
  84.7 0.8 copy-start.6
  84.7 0.7 collective-permute-start.4
  85.4 4.3 %copy-start.5 = (f32[64,128]{1,0:T(8,128)S(1)}, f32[64,128]{1,0:T(8,128)}, u32[]{:S(2)}) copy-start(f32[64,128]{1,0:T(8,128)} %get-tuple-element.268) | copy-start | bytes 98308
  89.1 0.7 collective-permute-start.5
  89.7 0.8 copy-start.4
  89.8 0.7 collective-permute-start.6
  90.5 0.8 copy-start.3
  90.5 0.7 collective-permute-start.7
  91.3 194.6 %collective-permute-start.8 = (bf16[64,256]{1,0:T(8,128)(2,1)S(1)}, bf16[64,256]{1,0:T(8,128)(2,1)S(1)}, u32[]{:S(2)}, u32[]{:S(2)}) collective-permute-start(bf16[64,256]{1,0:T(8,128)(2,1)S(1)} %get-tuple-element.292), channel_id=1, source_target_pairs={{192,224},{160,192},{193,225},{161,193},{194,226},{162,194},{195,2... | collective-permute-start | bytes 98312 | tf_op jit(solution)/shard_map/ppermute | solution.py:340
  315.6 16.9 %collective-permute-start.9 = (bf16[64,256]{1,0:T(8,128)(2,1)S(1)}, bf16[64,256]{1,0:T(8,128)(2,1)S(1)}, u32[]{:S(2)}, u32[]{:S(2)}) collective-permute-start(bf16[64,256]{1,0:T(8,128)(2,1)S(1)} %get-tuple-element.293), channel_id=1, source_target_pairs={{192,224},{193,225},{194,226},{195,227},{196,228},{197,229},{198,2... | collective-permute-start | bytes 98312 | tf_op jit(solution)/shard_map/ppermute | solution.py:340
  332.5 29.8 %copy-start.10 = (bf16[64,256]{1,0:T(8,128)(2,1)S(1)}, bf16[64,256]{1,0:T(8,128)(2,1)}, u32[]{:S(2)}) copy-start(bf16[64,256]{1,0:T(8,128)(2,1)} %copy-done.9) | copy-start | bytes 98308
